TPU v7x, 32 devices: a whole 2x2x4 slice. The times are simulated.
32 devices in a mesh: groups: 2 (over x), blk: 16 (over z, y, core).
Axes of the slice: x: 2, y: 2, z: 4, core: 2. Of those that a mesh axis runs over, the one named last changes fastest.
Arguments:
- query_inputs: bfloat16 [8192, 4096], P(('groups', 'blk')), parts along dimension 0, may hold values from -6 to 6
- query_grads: bfloat16 [8192, 4096], P(('groups', 'blk')), parts along dimension 0, may hold values from -6 to 6
- proj_in: bfloat16 [4096, 64], replicated, may hold values from -0.09375 to 0.09375
- proj_out: bfloat16 [4096, 64], replicated, may hold values from -0.09375 to 0.09375
- train_rows: bfloat16 [8192, 4096], P(('groups', 'blk')), parts along dimension 0, may hold values from -0.09375 to 0.09375
- token_owner: int32 [8192, 1], P(('groups', 'blk')), parts along dimension 0, may hold values from 0 to 15; in each aligned block of 256 rows (0 to 255, 256 to 511, ...) at most 64 rows name the same one
- token_slot: int32 [8192], P(('groups', 'blk')), parts along dimension 0, may hold values from 0 to 31
Outputs:
- influence: bfloat16 [12, 32, 8192], P(None, None, ('groups', 'blk')), parts along dimension 2
There are 2 independent parts, one for each index of `groups`. A program takes and returns all parts, laid end to end along the dimension named above; an argument that names none is the same for every part. Nothing has to cross between parts.
Inputs may be any that keep to these rules, and one draw needn't show every extreme that they name: `token_owner`: within the tokens of one device no owner is named by more than 64 tokens, a bound that some block reaches.
All inputs are finite; a program needn't handle non-finite values. Where the computation divides by a largest or mean magnitude, that divisor is 1e-20 or more.
Results may differ from a plain program's by a relative error of at most 0.0069.
Values may be sent and summed in bfloat16 or wider, within the bound.
No kernel may reach another device: no remote copies, remote signals or barrier semaphores. Data moves between devices by JAX's collectives and lax.ppermute only.
A program may use at most 64 MiB of HBM per device.

v0:
```python
import jax
import jax.numpy as jnp
from jax import lax
from jax.sharding import PartitionSpec as P

DOC_DEV = 32
STOPS = 12
NEWTON_STEPS = 6
LEAD = 5


HIGHEST_PRECISION = lax.Precision.HIGHEST


def passed_along(value, axis, steps):
    count = lax.axis_size(axis)
    pairs = [(source, (source + steps) % count) for source in range(count)]
    return lax.ppermute(value, axis, pairs)


def inverse_factor(gram_sum, counts):
    width_low = gram_sum.shape[1]
    identity_mat = jnp.eye(width_low, dtype=jnp.float32)
    damped = gram_sum / (counts[:, None, None] + 1.0) + identity_mat[None]
    row_bound = jnp.max(jnp.sum(jnp.abs(damped), axis=2), axis=1)
    approx = identity_mat[None] / row_bound[:, None, None]
    for iteration in range(NEWTON_STEPS):
        product = jnp.einsum("dab,dbc->dac", damped, approx, precision=HIGHEST_PRECISION)
        approx = jnp.einsum(
            "dab,dbc->dac", approx, 2.0 * identity_mat[None] - product, precision=HIGHEST_PRECISION
        )
    return approx


def local(query_inputs, query_grads, proj_in, proj_out, train_rows, token_owner, token_slot):
    tok_count = query_inputs.shape[0]
    width_low = proj_in.shape[1]
    owners = lax.axis_size("blk")
    capacity = 4 * tok_count // owners
    grads_low = jnp.dot(query_grads, proj_out, preferred_element_type=jnp.float32).astype(
        jnp.bfloat16
    )
    inputs_low = jnp.dot(query_inputs, proj_in, preferred_element_type=jnp.float32).astype(
        jnp.bfloat16
    )
    low_rows = jnp.concatenate([grads_low, inputs_low], axis=1)
    owner_ids = token_owner[:, 0]
    owner_hot = (owner_ids[:, None] == jnp.arange(owners, dtype=jnp.int32)[None, :]).astype(
        jnp.float32
    )
    tok_index = jnp.arange(tok_count, dtype=jnp.int32)
    earlier = (tok_index[:, None] > tok_index[None, :]).astype(jnp.float32)
    before = jnp.dot(earlier, owner_hot, precision=HIGHEST_PRECISION)
    rank_in = jnp.sum(before * owner_hot, axis=1).astype(jnp.int32)
    position = owner_ids * capacity + rank_in
    slot_index = jnp.arange(owners * capacity, dtype=jnp.int32)
    placed = slot_index[:, None] == position[None, :]
    send_rows = jnp.dot(
        placed.astype(jnp.bfloat16), low_rows, preferred_element_type=jnp.float32
    ).astype(jnp.bfloat16)
    send_slot = jnp.sum(jnp.where(placed, token_slot[None, :] + 1, 0), axis=1)
    recv_rows, recv_slot = (
        lax.all_to_all(
            send_rows.reshape(owners, capacity, 2 * width_low),
            "blk",
            split_axis=0,
            concat_axis=0,
            tiled=True,
        ),
        lax.all_to_all(
            send_slot.reshape(owners, capacity), "blk", split_axis=0, concat_axis=0, tiled=True
        ),
    )
    recv_rows = recv_rows.reshape(owners * capacity, 2 * width_low)
    recv_slot = recv_slot.reshape(owners * capacity)
    doc_index = jnp.arange(1, DOC_DEV + 1, dtype=jnp.int32)
    doc_hot = recv_slot[:, None] == doc_index[None, :]
    counts = jnp.sum(doc_hot.astype(jnp.float32), axis=0)
    hot_bf = doc_hot.astype(jnp.bfloat16)
    grads_recv = recv_rows[:, :width_low]
    inputs_recv = recv_rows[:, width_low:]
    spread_grads = (hot_bf[:, :, None] * grads_recv[:, None, :]).reshape(
        owners * capacity, DOC_DEV * width_low
    )
    spread_inputs = (hot_bf[:, :, None] * inputs_recv[:, None, :]).reshape(
        owners * capacity, DOC_DEV * width_low
    )
    contract = (((0,), (0,)), ((), ()))
    grad_gram = lax.dot_general(
        spread_grads, recv_rows, contract, preferred_element_type=jnp.float32
    ).reshape(DOC_DEV, width_low, 2 * width_low)
    outer_b = grad_gram[:, :, :width_low]
    doc_grad = grad_gram[:, :, width_low:]
    outer_a = lax.dot_general(
        spread_inputs, inputs_recv, contract, preferred_element_type=jnp.float32
    ).reshape(DOC_DEV, width_low, width_low)
    inv_a = inverse_factor(outer_a, counts)
    inv_b = inverse_factor(outer_b, counts)
    tilted = jnp.einsum("dab,dbc->dac", inv_b, doc_grad, precision=HIGHEST_PRECISION)
    tilted = jnp.einsum("dab,dbc->dac", tilted, inv_a, precision=HIGHEST_PRECISION)
    queries = tilted.reshape(DOC_DEV, width_low * width_low).astype(jnp.bfloat16)
    score_dims = (((1,), (1,)), ((), ()))

    def scoring(block):
        return lax.dot_general(
            block, train_rows, score_dims, preferred_element_type=jnp.float32
        ).astype(jnp.bfloat16)

    def step_ahead(current_block, unused):
        arrived = passed_along(current_block, "blk", 1)
        return (arrived, scoring(arrived))

    def step_back(current_block):
        arrived = passed_along(current_block, "blk", -1)
        return (arrived, scoring(arrived))

    def both_ways(carried, unused):
        ahead_block, back_block = carried
        ahead_block, ahead_tile = step_ahead(ahead_block, unused)
        back_block, back_tile = step_back(back_block)
        return ((ahead_block, back_block), (ahead_tile, back_tile))

    last_pair, paired_tiles = lax.scan(both_ways, (queries, queries), None, length=LEAD)
    ahead_tiles, back_tiles = paired_tiles
    tail_block, tail_tiles = lax.scan(step_ahead, last_pair[0], None, length=STOPS - 1 - 2 * LEAD)
    stacked = jnp.concatenate(
        [jnp.flip(back_tiles, 0), scoring(queries)[None], ahead_tiles, tail_tiles], axis=0
    )
    return stacked


def solution(mesh):
    placed = (
        P(("groups", "blk"), None),
        P(("groups", "blk"), None),
        P(),
        P(),
        P(("groups", "blk"), None),
        P(("groups", "blk"), None),
        P(("groups", "blk")),
    )
    return jax.shard_map(
        local,
        mesh=mesh,
        in_specs=placed,
        out_specs=P(None, None, ("groups", "blk")),
        check_vma=False,
    )
```

profile of v0, /device:TPU:0, one launch (start us, length us, event | category | flops | bytes accessed | tf_op | source)
XLA Modules:
  0.0 149.2 jit_solution(2262987183202212464)
XLA Ops:
  2.7 7.4 %all-to-all-start = ((s32[16,1,64]{2,1,0:T(1,128)}), s32[16,1,64]{2,1,0:T(1,128)S(1)}, u32[]{:S(2)}, u32[]{:S(2)}) async-start(s32[16,1,64]{2,1,0:T(1,128)} %all_to_all.9), calls=%async_computation | async-start | bytes 16384 | tf_op jit(solution)/shard_map/all_to_all | solution.py:70
  13.8 2.6 %all-to-all-done = s32[16,1,64]{2,1,0:T(1,128)S(1)} async-done(((s32[16,1,64]{2,1,0:T(1,128)}), s32[16,1,64]{2,1,0:T(1,128)S(1)}, u32[]{:S(2)}, u32[]{:S(2)}) %all-to-all-start) | async-done | bytes 4128 | tf_op jit(solution)/shard_map/all_to_all | solution.py:70
  16.4 3.7 %all-to-all-start.1 = ((bf16[16,64,128]{2,1,0:T(8,128)(2,1)}), bf16[16,64,128]{2,1,0:T(8,128)(2,1)S(1)}, u32[]{:S(2)}, u32[]{:S(2)}) async-start(bf16[16,64,128]{2,1,0:T(8,128)(2,1)} %bitcast.3), calls=%async_computation.1 | async-start | bytes 524288 | tf_op jit(solution)/shard_map/all_to_all | solution.py:63
  22.8 7.1 %all-to-all-done.1 = bf16[16,64,128]{2,1,0:T(8,128)(2,1)S(1)} async-done(((bf16[16,64,128]{2,1,0:T(8,128)(2,1)}), bf16[16,64,128]{2,1,0:T(8,128)(2,1)S(1)}, u32[]{:S(2)}, u32[]{:S(2)}) %all-to-all-start.1) | async-done | bytes 262176 | tf_op jit(solution)/shard_map/all_to_all | solution.py:63
  52.6 2.2 %fusion.23 = f32[32,64,64]{2,1,0:T(8,128)} fusion(f32[32,64,64]{2,1,0:T(8,128)S(1)} %fusion.62, f32[32,64,128]{2,1,0:T(8,128)S(1)} %fusion.6), kind=kOutput, calls=%fused_computation.40 | convolution fusion | flops 100663296 | bytes 2097152 | tf_op jit(solution)/shard_map/dab,dbc->dac/dot_general | solution.py:99
  56.6 3.0 %abs_reduce_fusion = (f32[32,64]{1,0:T(8,128)}, f32[32,64,64]{2,1,0:T(8,128)S(1)}) fusion(f32[64,64]{1,0:T(8,128)S(1)} %fusion.47, f32[32]{0:T(128)} %broadcast_add_fusion.1, bf16[1024,128]{1,0:T(8,128)(2,1)S(1)} %bitcast.110, bf16[1024,64]{0,1:T(8,128)(2,1)} %copy.13, bf16[1024,32]{0,1:T(8,128)(2,1)} %compare_convert_fusion.1), kind=kOutput, calls=%fused_computation.44 | convolution fusion | flops 271054848 | bytes 1007744 | tf_op jit(solution)/shard_map/dot_general | solution.py:94
  77.3 61.8 %while.4 = (s32[]{:T(128)}, bf16[32,4096]{1,0:T(8,128)(2,1)S(1)}, bf16[32,4096]{1,0:T(8,128)(2,1)S(1)}, bf16[5,32,256]{2,1,0:T(8,128)(2,1)}, bf16[5,32,256]{2,1,...) while((s32[]{:T(128)}, bf16[32,4096]{1,0:T(8,128)(2,1)S(1)}, bf16[32,4096]{1,0:T(8,128)(2,1)S(1)}, ...), condition=%wide.region_8.9_spmd, body=%wide.region_7.8_spmd.sunk | while | flops 134234112 | bytes 16285897 | solution.py:123
  77.4 4.4 %collective-permute-start.1 = (bf16[32,4096]{1,0:T(8,128)(2,1)S(1)}, bf16[32,4096]{1,0:T(8,128)(2,1)S(1)}, u32[]{:S(2)}, u32[]{:S(2)}) collective-permute-start(bf16[32,4096]{1,0:T(8,128)(2,1)S(1)} %get-tuple-element.118), channel_id=1, source_target_pairs={{0,15},{1,0},{2,1},{3,2},{4,3},{5,4},{6,5},{7,6},{8,7},{9,8},{10,9... | collective-permute-start | bytes 786440 | tf_op jit(solution)/shard_map/while/body/eval_jaxpr/ppermute | solution.py:18
  81.8 4.2 %collective-permute-done = bf16[32,4096]{1,0:T(8,128)(2,1)S(1)} collective-permute-done((bf16[32,4096]{1,0:T(8,128)(2,1)S(1)}, bf16[32,4096]{1,0:T(8,128)(2,1)S(1)}, u32[]{:S(2)}, u32[]{:S(2)}) %collective-permute-start) | collective-permute-done | bytes 262176 | tf_op jit(solution)/shard_map/while/body/eval_jaxpr/ppermute | solution.py:18
  86.0 2.9 %fusion.132 = bf16[5,32,256]{2,1,0:T(8,128)(2,1)} fusion(bf16[5,32,256]{2,1,0:T(8,128)(2,1)} %get-tuple-element.119, s32[]{:T(128)S(6)} %copy.26, bf16[32,4096]{1,0:T(8,128)(2,1)S(1)} %collective-permute-done, bf16[256,4096]{1,0:T(8,128)(2,1)} %get-tuple-element.128), kind=kOutput, calls=%fused_computation.3.clone.1 | convolution fusion | flops 67117056 | bytes 2375684 | tf_op jit(solution)/shard_map/while/body/eval_jaxpr/dot_general | solution.py:105
  89.7 4.4 %collective-permute-start.1 = (bf16[32,4096]{1,0:T(8,128)(2,1)S(1)}, bf16[32,4096]{1,0:T(8,128)(2,1)S(1)}, u32[]{:S(2)}, u32[]{:S(2)}) collective-permute-start(bf16[32,4096]{1,0:T(8,128)(2,1)S(1)} %get-tuple-element.118), channel_id=1, source_target_pairs={{0,15},{1,0},{2,1},{3,2},{4,3},{5,4},{6,5},{7,6},{8,7},{9,8},{10,9... | collective-permute-start | bytes 786440 | tf_op jit(solution)/shard_map/while/body/eval_jaxpr/ppermute | solution.py:18
  94.1 4.2 %collective-permute-done = bf16[32,4096]{1,0:T(8,128)(2,1)S(1)} collective-permute-done((bf16[32,4096]{1,0:T(8,128)(2,1)S(1)}, bf16[32,4096]{1,0:T(8,128)(2,1)S(1)}, u32[]{:S(2)}, u32[]{:S(2)}) %collective-permute-start) | collective-permute-done | bytes 262176 | tf_op jit(solution)/shard_map/while/body/eval_jaxpr/ppermute | solution.py:18
  98.3 2.9 %fusion.132 = bf16[5,32,256]{2,1,0:T(8,128)(2,1)} fusion(bf16[5,32,256]{2,1,0:T(8,128)(2,1)} %get-tuple-element.119, s32[]{:T(128)S(6)} %copy.26, bf16[32,4096]{1,0:T(8,128)(2,1)S(1)} %collective-permute-done, bf16[256,4096]{1,0:T(8,128)(2,1)} %get-tuple-element.128), kind=kOutput, calls=%fused_computation.3.clone.1 | convolution fusion | flops 67117056 | bytes 2375684 | tf_op jit(solution)/shard_map/while/body/eval_jaxpr/dot_general | solution.py:105
  102.0 4.4 %collective-permute-start.1 = (bf16[32,4096]{1,0:T(8,128)(2,1)S(1)}, bf16[32,4096]{1,0:T(8,128)(2,1)S(1)}, u32[]{:S(2)}, u32[]{:S(2)}) collective-permute-start(bf16[32,4096]{1,0:T(8,128)(2,1)S(1)} %get-tuple-element.118), channel_id=1, source_target_pairs={{0,15},{1,0},{2,1},{3,2},{4,3},{5,4},{6,5},{7,6},{8,7},{9,8},{10,9... | collective-permute-start | bytes 786440 | tf_op jit(solution)/shard_map/while/body/eval_jaxpr/ppermute | solution.py:18
  106.5 4.2 %collective-permute-done = bf16[32,4096]{1,0:T(8,128)(2,1)S(1)} collective-permute-done((bf16[32,4096]{1,0:T(8,128)(2,1)S(1)}, bf16[32,4096]{1,0:T(8,128)(2,1)S(1)}, u32[]{:S(2)}, u32[]{:S(2)}) %collective-permute-start) | collective-permute-done | bytes 262176 | tf_op jit(solution)/shard_map/while/body/eval_jaxpr/ppermute | solution.py:18
  110.7 2.9 %fusion.132 = bf16[5,32,256]{2,1,0:T(8,128)(2,1)} fusion(bf16[5,32,256]{2,1,0:T(8,128)(2,1)} %get-tuple-element.119, s32[]{:T(128)S(6)} %copy.26, bf16[32,4096]{1,0:T(8,128)(2,1)S(1)} %collective-permute-done, bf16[256,4096]{1,0:T(8,128)(2,1)} %get-tuple-element.128), kind=kOutput, calls=%fused_computation.3.clone.1 | convolution fusion | flops 67117056 | bytes 2375684 | tf_op jit(solution)/shard_map/while/body/eval_jaxpr/dot_general | solution.py:105
  114.4 4.4 %collective-permute-start.1 = (bf16[32,4096]{1,0:T(8,128)(2,1)S(1)}, bf16[32,4096]{1,0:T(8,128)(2,1)S(1)}, u32[]{:S(2)}, u32[]{:S(2)}) collective-permute-start(bf16[32,4096]{1,0:T(8,128)(2,1)S(1)} %get-tuple-element.118), channel_id=1, source_target_pairs={{0,15},{1,0},{2,1},{3,2},{4,3},{5,4},{6,5},{7,6},{8,7},{9,8},{10,9... | collective-permute-start | bytes 786440 | tf_op jit(solution)/shard_map/while/body/eval_jaxpr/ppermute | solution.py:18
  118.8 4.2 %collective-permute-done = bf16[32,4096]{1,0:T(8,128)(2,1)S(1)} collective-permute-done((bf16[32,4096]{1,0:T(8,128)(2,1)S(1)}, bf16[32,4096]{1,0:T(8,128)(2,1)S(1)}, u32[]{:S(2)}, u32[]{:S(2)}) %collective-permute-start) | collective-permute-done | bytes 262176 | tf_op jit(solution)/shard_map/while/body/eval_jaxpr/ppermute | solution.py:18
  123.0 2.9 %fusion.132 = bf16[5,32,256]{2,1,0:T(8,128)(2,1)} fusion(bf16[5,32,256]{2,1,0:T(8,128)(2,1)} %get-tuple-element.119, s32[]{:T(128)S(6)} %copy.26, bf16[32,4096]{1,0:T(8,128)(2,1)S(1)} %collective-permute-done, bf16[256,4096]{1,0:T(8,128)(2,1)} %get-tuple-element.128), kind=kOutput, calls=%fused_computation.3.clone.1 | convolution fusion | flops 67117056 | bytes 2375684 | tf_op jit(solution)/shard_map/while/body/eval_jaxpr/dot_general | solution.py:105
  126.8 4.4 %collective-permute-start.1 = (bf16[32,4096]{1,0:T(8,128)(2,1)S(1)}, bf16[32,4096]{1,0:T(8,128)(2,1)S(1)}, u32[]{:S(2)}, u32[]{:S(2)}) collective-permute-start(bf16[32,4096]{1,0:T(8,128)(2,1)S(1)} %get-tuple-element.118), channel_id=1, source_target_pairs={{0,15},{1,0},{2,1},{3,2},{4,3},{5,4},{6,5},{7,6},{8,7},{9,8},{10,9... | collective-permute-start | bytes 786440 | tf_op jit(solution)/shard_map/while/body/eval_jaxpr/ppermute | solution.py:18
  131.2 4.2 %collective-permute-done = bf16[32,4096]{1,0:T(8,128)(2,1)S(1)} collective-permute-done((bf16[32,4096]{1,0:T(8,128)(2,1)S(1)}, bf16[32,4096]{1,0:T(8,128)(2,1)S(1)}, u32[]{:S(2)}, u32[]{:S(2)}) %collective-permute-start) | collective-permute-done | bytes 262176 | tf_op jit(solution)/shard_map/while/body/eval_jaxpr/ppermute | solution.py:18
  135.4 2.9 %fusion.132 = bf16[5,32,256]{2,1,0:T(8,128)(2,1)} fusion(bf16[5,32,256]{2,1,0:T(8,128)(2,1)} %get-tuple-element.119, s32[]{:T(128)S(6)} %copy.26, bf16[32,4096]{1,0:T(8,128)(2,1)S(1)} %collective-permute-done, bf16[256,4096]{1,0:T(8,128)(2,1)} %get-tuple-element.128), kind=kOutput, calls=%fused_computation.3.clone.1 | convolution fusion | flops 67117056 | bytes 2375684 | tf_op jit(solution)/shard_map/while/body/eval_jaxpr/dot_general | solution.py:105
  139.2 2.5 %fusion.20 = bf16[1,32,256]{2,1,0:T(8,128)(2,1)S(1)} fusion(bf16[32,4096]{1,0:T(8,128)(2,1)S(1)} %convert_element_type.71, bf16[256,4096]{1,0:T(8,128)(2,1)} %get-tuple-element.130), kind=kOutput, calls=%fused_computation.37 | convolution fusion | flops 67117056 | bytes 2375680 | tf_op jit(solution)/shard_map/dot_general | solution.py:105
  141.7 5.9 %collective-permute-done.2 = bf16[32,4096]{1,0:T(8,128)(2,1)S(1)} collective-permute-done((bf16[32,4096]{1,0:T(8,128)(2,1)S(1)}, bf16[32,4096]{1,0:T(8,128)(2,1)S(1)}, u32[]{:S(2)}, u32[]{:S(2)}) %collective-permute-start.2) | collective-permute-done | bytes 262176 | tf_op jit(solution)/shard_map/while/body/eval_jaxpr/ppermute | solution.py:18
  (110 shorter events, 56.7 us)
Async XLA Ops:
  0.0 10.1 %copy-start = (bf16[256,4096]{1,0:T(8,128)(2,1)S(1)}, bf16[256,4096]{1,0:T(8,128)(2,1)}, u32[]{:S(2)}) copy-start(bf16[256,4096]{1,0:T(8,128)(2,1)} %param.9) | copy-start | bytes 6291460
  0.0 12.0 %copy-start.9 = (bf16[4096,64]{0,1:T(8,128)(2,1)S(1)}, bf16[4096,64]{0,1:T(8,128)(2,1)}, u32[]{:S(2)}) copy-start(bf16[4096,64]{0,1:T(8,128)(2,1)} %param.12) | copy-start | bytes 1572868
  2.7 13.7 %all-to-all-start = ((s32[16,1,64]{2,1,0:T(1,128)}), s32[16,1,64]{2,1,0:T(1,128)S(1)}, u32[]{:S(2)}, u32[]{:S(2)}) async-start(s32[16,1,64]{2,1,0:T(1,128)} %all_to_all.9), calls=%async_computation | async-start | bytes 16384 | tf_op jit(solution)/shard_map/all_to_all | solution.py:70
  16.4 13.5 %all-to-all-start.1 = ((bf16[16,64,128]{2,1,0:T(8,128)(2,1)}), bf16[16,64,128]{2,1,0:T(8,128)(2,1)S(1)}, u32[]{:S(2)}, u32[]{:S(2)}) async-start(bf16[16,64,128]{2,1,0:T(8,128)(2,1)} %bitcast.3), calls=%async_computation.1 | async-start | bytes 524288 | tf_op jit(solution)/shard_map/all_to_all | solution.py:63
  31.6 2.2 %copy-start.5 = (f32[32]{0:T(128)S(1)}, f32[32]{0:T(128)}, u32[]{:S(2)}) copy-start(f32[32]{0:T(128)} %broadcast_add_fusion.1) | copy-start | bytes 388
  36.2 2.1 %copy-start.7 = (f32[32]{0:T(128)S(1)}, f32[32]{0:T(128)}, u32[]{:S(2)}) copy-start(f32[32]{0:T(128)} %reduce_max.18) | copy-start | bytes 388
  77.3 8.7 %collective-permute-start = (bf16[32,4096]{1,0:T(8,128)(2,1)S(1)}, bf16[32,4096]{1,0:T(8,128)(2,1)S(1)}, u32[]{:S(2)}, u32[]{:S(2)}) collective-permute-start(bf16[32,4096]{1,0:T(8,128)(2,1)S(1)} %get-tuple-element.117), channel_id=1, source_target_pairs={{0,1},{1,2},{2,3},{3,4},{4,5},{5,6},{6,7},{7,8},{8,9},{9,10},{10,1... | collective-permute-start | bytes 786440 | tf_op jit(solution)/shard_map/while/body/eval_jaxpr/ppermute | solution.py:18
  77.4 8.6 %collective-permute-start.1 = (bf16[32,4096]{1,0:T(8,128)(2,1)S(1)}, bf16[32,4096]{1,0:T(8,128)(2,1)S(1)}, u32[]{:S(2)}, u32[]{:S(2)}) collective-permute-start(bf16[32,4096]{1,0:T(8,128)(2,1)S(1)} %get-tuple-element.118), channel_id=1, source_target_pairs={{0,15},{1,0},{2,1},{3,2},{4,3},{5,4},{6,5},{7,6},{8,7},{9,8},{10,9... | collective-permute-start | bytes 786440 | tf_op jit(solution)/shard_map/while/body/eval_jaxpr/ppermute | solution.py:18
  81.8 7.2 %copy-start.1 = (bf16[256,4096]{1,0:T(8,128)(2,1)S(1)}, bf16[256,4096]{1,0:T(8,128)(2,1)}, u32[]{:S(2)}) copy-start(bf16[256,4096]{1,0:T(8,128)(2,1)} %get-tuple-element.128) | copy-start | bytes 6291460 | tf_op jit(solution)/shard_map/while
  89.7 8.6 %collective-permute-start = (bf16[32,4096]{1,0:T(8,128)(2,1)S(1)}, bf16[32,4096]{1,0:T(8,128)(2,1)S(1)}, u32[]{:S(2)}, u32[]{:S(2)}) collective-permute-start(bf16[32,4096]{1,0:T(8,128)(2,1)S(1)} %get-tuple-element.117), channel_id=1, source_target_pairs={{0,1},{1,2},{2,3},{3,4},{4,5},{5,6},{6,7},{7,8},{8,9},{9,10},{10,1... | collective-permute-start | bytes 786440 | tf_op jit(solution)/shard_map/while/body/eval_jaxpr/ppermute | solution.py:18
  89.7 8.6 %collective-permute-start.1 = (bf16[32,4096]{1,0:T(8,128)(2,1)S(1)}, bf16[32,4096]{1,0:T(8,128)(2,1)S(1)}, u32[]{:S(2)}, u32[]{:S(2)}) collective-permute-start(bf16[32,4096]{1,0:T(8,128)(2,1)S(1)} %get-tuple-element.118), channel_id=1, source_target_pairs={{0,15},{1,0},{2,1},{3,2},{4,3},{5,4},{6,5},{7,6},{8,7},{9,8},{10,9... | collective-permute-start | bytes 786440 | tf_op jit(solution)/shard_map/while/body/eval_jaxpr/ppermute | solution.py:18
  94.1 7.2 %copy-start.1 = (bf16[256,4096]{1,0:T(8,128)(2,1)S(1)}, bf16[256,4096]{1,0:T(8,128)(2,1)}, u32[]{:S(2)}) copy-start(bf16[256,4096]{1,0:T(8,128)(2,1)} %get-tuple-element.128) | copy-start | bytes 6291460 | tf_op jit(solution)/shard_map/while
  102.0 8.6 %collective-permute-start = (bf16[32,4096]{1,0:T(8,128)(2,1)S(1)}, bf16[32,4096]{1,0:T(8,128)(2,1)S(1)}, u32[]{:S(2)}, u32[]{:S(2)}) collective-permute-start(bf16[32,4096]{1,0:T(8,128)(2,1)S(1)} %get-tuple-element.117), channel_id=1, source_target_pairs={{0,1},{1,2},{2,3},{3,4},{4,5},{5,6},{6,7},{7,8},{8,9},{9,10},{10,1... | collective-permute-start | bytes 786440 | tf_op jit(solution)/shard_map/while/body/eval_jaxpr/ppermute | solution.py:18
  102.0 8.6 %collective-permute-start.1 = (bf16[32,4096]{1,0:T(8,128)(2,1)S(1)}, bf16[32,4096]{1,0:T(8,128)(2,1)S(1)}, u32[]{:S(2)}, u32[]{:S(2)}) collective-permute-start(bf16[32,4096]{1,0:T(8,128)(2,1)S(1)} %get-tuple-element.118), channel_id=1, source_target_pairs={{0,15},{1,0},{2,1},{3,2},{4,3},{5,4},{6,5},{7,6},{8,7},{9,8},{10,9... | collective-permute-start | bytes 786440 | tf_op jit(solution)/shard_map/while/body/eval_jaxpr/ppermute | solution.py:18
  106.5 7.2 %copy-start.1 = (bf16[256,4096]{1,0:T(8,128)(2,1)S(1)}, bf16[256,4096]{1,0:T(8,128)(2,1)}, u32[]{:S(2)}) copy-start(bf16[256,4096]{1,0:T(8,128)(2,1)} %get-tuple-element.128) | copy-start | bytes 6291460 | tf_op jit(solution)/shard_map/while
  114.4 8.6 %collective-permute-start = (bf16[32,4096]{1,0:T(8,128)(2,1)S(1)}, bf16[32,4096]{1,0:T(8,128)(2,1)S(1)}, u32[]{:S(2)}, u32[]{:S(2)}) collective-permute-start(bf16[32,4096]{1,0:T(8,128)(2,1)S(1)} %get-tuple-element.117), channel_id=1, source_target_pairs={{0,1},{1,2},{2,3},{3,4},{4,5},{5,6},{6,7},{7,8},{8,9},{9,10},{10,1... | collective-permute-start | bytes 786440 | tf_op jit(solution)/shard_map/while/body/eval_jaxpr/ppermute | solution.py:18
  114.4 8.6 %collective-permute-start.1 = (bf16[32,4096]{1,0:T(8,128)(2,1)S(1)}, bf16[32,4096]{1,0:T(8,128)(2,1)S(1)}, u32[]{:S(2)}, u32[]{:S(2)}) collective-permute-start(bf16[32,4096]{1,0:T(8,128)(2,1)S(1)} %get-tuple-element.118), channel_id=1, source_target_pairs={{0,15},{1,0},{2,1},{3,2},{4,3},{5,4},{6,5},{7,6},{8,7},{9,8},{10,9... | collective-permute-start | bytes 786440 | tf_op jit(solution)/shard_map/while/body/eval_jaxpr/ppermute | solution.py:18
  118.8 7.2 %copy-start.1 = (bf16[256,4096]{1,0:T(8,128)(2,1)S(1)}, bf16[256,4096]{1,0:T(8,128)(2,1)}, u32[]{:S(2)}) copy-start(bf16[256,4096]{1,0:T(8,128)(2,1)} %get-tuple-element.128) | copy-start | bytes 6291460 | tf_op jit(solution)/shard_map/while
  126.7 8.6 %collective-permute-start = (bf16[32,4096]{1,0:T(8,128)(2,1)S(1)}, bf16[32,4096]{1,0:T(8,128)(2,1)S(1)}, u32[]{:S(2)}, u32[]{:S(2)}) collective-permute-start(bf16[32,4096]{1,0:T(8,128)(2,1)S(1)} %get-tuple-element.117), channel_id=1, source_target_pairs={{0,1},{1,2},{2,3},{3,4},{4,5},{5,6},{6,7},{7,8},{8,9},{9,10},{10,1... | collective-permute-start | bytes 786440 | tf_op jit(solution)/shard_map/while/body/eval_jaxpr/ppermute | solution.py:18
  126.8 8.6 %collective-permute-start.1 = (bf16[32,4096]{1,0:T(8,128)(2,1)S(1)}, bf16[32,4096]{1,0:T(8,128)(2,1)S(1)}, u32[]{:S(2)}, u32[]{:S(2)}) collective-permute-start(bf16[32,4096]{1,0:T(8,128)(2,1)S(1)} %get-tuple-element.118), channel_id=1, source_target_pairs={{0,15},{1,0},{2,1},{3,2},{4,3},{5,4},{6,5},{7,6},{8,7},{9,8},{10,9... | collective-permute-start | bytes 786440 | tf_op jit(solution)/shard_map/while/body/eval_jaxpr/ppermute | solution.py:18
  131.2 7.2 %copy-start.1 = (bf16[256,4096]{1,0:T(8,128)(2,1)S(1)}, bf16[256,4096]{1,0:T(8,128)(2,1)}, u32[]{:S(2)}) copy-start(bf16[256,4096]{1,0:T(8,128)(2,1)} %get-tuple-element.128) | copy-start | bytes 6291460 | tf_op jit(solution)/shard_map/while
  139.1 8.5 %collective-permute-start.2 = (bf16[32,4096]{1,0:T(8,128)(2,1)S(1)}, bf16[32,4096]{1,0:T(8,128)(2,1)S(1)}, u32[]{:S(2)}, u32[]{:S(2)}) collective-permute-start(bf16[32,4096]{1,0:T(8,128)(2,1)S(1)} %get-tuple-element.53), channel_id=1, source_target_pairs={{0,1},{1,2},{2,3},{3,4},{4,5},{5,6},{6,7},{7,8},{8,9},{9,10},{10,1... | collective-permute-start | bytes 786440 | tf_op jit(solution)/shard_map/while/body/eval_jaxpr/ppermute | solution.py:18
  139.2 8.4 %copy-start.2 = (bf16[256,4096]{1,0:T(8,128)(2,1)S(1)}, bf16[256,4096]{1,0:T(8,128)(2,1)}, u32[]{:S(2)}) copy-start(bf16[256,4096]{1,0:T(8,128)(2,1)} %get-tuple-element.130) | copy-start | bytes 6291460
  139.2 9.1 %copy-start.4 = (bf16[5,32,256]{2,1,0:T(8,128)(2,1)S(1)}, bf16[5,32,256]{2,1,0:T(8,128)(2,1)}, u32[]{:S(2)}) copy-start(bf16[5,32,256]{2,1,0:T(8,128)(2,1)} %get-tuple-element.52) | copy-start | bytes 245764
  (3 other events, 4.4 us)
where the time goes:
time: 152 us; the launch traced here: 149 us
  matrix products  66.1 us (43%)
  waiting for transfers between devices  36.4 us (24%)
  starting transfers between devices  33.6 us (22%)
  other arithmetic  7.02 us (5%)
  local copies, waits for them, and re-layouts  5.39 us (4%)
    ppermute x11, waiting for transfers between devices, passed_along(): return lax.ppermute(value, axis, pairs)  26.7 us
    ppermute x11, starting transfers between devices, passed_along(): return lax.ppermute(value, axis, pairs)  22.5 us
    dot_general x12, matrix products, scoring(): lax.dot_general(block, train_rows, score_dims, preferred_element_type=jnp...  21.5 us
    dot_general x12, matrix products, inverse_factor(): jnp.einsum('dab,dbc->dac', damped, approx, precision=HIGHEST_PRECISION)  16.1 us
    dot_general x12, matrix products, inverse_factor(): jnp.einsum('dab,dbc->dac', approx, 2.0 * identity_mat[None] - product, pr...  15.1 us
    all_to_all x1, starting transfers between devices, local(): lax.all_to_all(send_slot.reshape(owners, capacity), 'blk', split_axis=0,...  7.39 us
    all_to_all x1, waiting for transfers between devices, local(): lax.all_to_all(send_rows.reshape(owners, capacity, 2 * width_low), 'blk',...  7.14 us
    all_to_all x1, starting transfers between devices, local(): lax.all_to_all(send_rows.reshape(owners, capacity, 2 * width_low), 'blk',...  3.7 us
  transfers between devices with their start and end apart: 13, of which 8 were waited for; matrix products, arithmetic and copies ran while one was open for 6% of the time, Pallas kernels for 0%

commit v1 on v0

--- a/solution.py
+++ b/solution.py
@@ -1,17 +1,311 @@
+import functools
 import jax
 import jax.numpy as jnp
+import numpy as np
 from jax import lax
+from jax.experimental import pallas as pl
+from jax.experimental.pallas import tpu as pltpu
 from jax.sharding import PartitionSpec as P
 
 DOC_DEV = 32
 STOPS = 12
 NEWTON_STEPS = 6
 LEAD = 5
-
-
+TAIL = 16
+F32 = jnp.float32
+BF16 = jnp.bfloat16
 HIGHEST_PRECISION = lax.Precision.HIGHEST
 
 
+def pack_kernel(inputs_ref, grads_ref, pin_ref, pout_ref, owner_ref, slot_ref, send_ref, ilow_ref, glow_ref):
+    step = pl.program_id(0)
+
+    @pl.when(step == 0)
+    def _():
+        ilow_ref[...] = jnp.zeros_like(ilow_ref)
+        glow_ref[...] = jnp.zeros_like(glow_ref)
+
+    ilow_ref[...] += jnp.dot(inputs_ref[...], pin_ref[...], preferred_element_type=F32)
+    glow_ref[...] += jnp.dot(grads_ref[...], pout_ref[...], preferred_element_type=F32)
+
+    @pl.when(step == pl.num_programs(0) - 1)
+    def _():
+        owners, per, wide = send_ref.shape
+        cap = per - TAIL
+        toks = slot_ref.shape[1]
+        low = jnp.concatenate([glow_ref[...], ilow_ref[...]], axis=1).astype(BF16)
+        owner_col = owner_ref[...]
+        hot = (owner_col == lax.broadcasted_iota(jnp.int32, (toks, owners), 1)).astype(F32)
+        tri = lax.broadcasted_iota(jnp.int32, (toks, toks), 0) > lax.broadcasted_iota(jnp.int32, (toks, toks), 1)
+        before = jnp.dot(tri.astype(F32).astype(BF16), hot.astype(BF16), preferred_element_type=F32)
+        rank = jnp.sum(before * hot, axis=1, keepdims=True)
+        both = jnp.concatenate(
+            [jnp.broadcast_to(rank, (toks, wide)), jnp.broadcast_to(owner_col.astype(F32), (toks, wide))], axis=1
+        ).T
+        rank_row = both[:1]
+        owner_row = both[wide : wide + 1]
+        position = (owner_row * cap + rank_row).astype(jnp.int32)
+        placed = lax.broadcasted_iota(jnp.int32, (owners * cap, toks), 0) == position
+        rows = jnp.dot(placed.astype(F32).astype(BF16), low, preferred_element_type=F32).astype(BF16)
+        hot_row = owner_row == lax.broadcasted_iota(jnp.int32, (owners, toks), 0).astype(F32)
+        named = jnp.where(hot_row, slot_ref[...].astype(F32) + 1.0, 0.0).astype(BF16)
+        lane = lax.broadcasted_iota(jnp.int32, (toks, wide), 1) % cap
+        at_lane = (rank.astype(jnp.int32) == lane).astype(F32).astype(BF16)
+        slots = jnp.dot(named, at_lane, preferred_element_type=F32).astype(BF16)
+        for o in range(owners):
+            send_ref[o, :cap, :] = rows[o * cap : (o + 1) * cap]
+            send_ref[o, cap:, :] = jnp.broadcast_to(slots.astype(F32)[o : o + 1], (TAIL, wide)).astype(BF16)
+
+
+def packed_rows(query_inputs, query_grads, proj_in, proj_out, token_owner, token_slot, owners, cap):
+    toks, width = query_inputs.shape
+    low = proj_in.shape[1]
+    steps = 4
+    part = width // steps
+    return pl.pallas_call(
+        pack_kernel,
+        grid=(steps,),
+        out_shape=jax.ShapeDtypeStruct((owners, cap + TAIL, 2 * low), BF16),
+        in_specs=[
+            pl.BlockSpec((toks, part), lambda i: (0, i)),
+            pl.BlockSpec((toks, part), lambda i: (0, i)),
+            pl.BlockSpec((part, low), lambda i: (i, 0)),
+            pl.BlockSpec((part, low), lambda i: (i, 0)),
+            pl.BlockSpec((toks, 1), lambda i: (0, 0)),
+            pl.BlockSpec((1, toks), lambda i: (0, 0)),
+        ],
+        out_specs=pl.BlockSpec((owners, cap + TAIL, 2 * low), lambda i: (0, 0, 0)),
+        scratch_shapes=[pltpu.VMEM((toks, low), F32), pltpu.VMEM((toks, low), F32)],
+        compiler_params=pltpu.CompilerParams(vmem_limit_bytes=40 * 2**20),
+    )(query_inputs, query_grads, proj_in, proj_out, token_owner, token_slot.reshape(1, toks))
+
+
+def split(value, parts):
+    out = []
+    for _ in range(parts):
+        top = value.astype(BF16)
+        out.append(top)
+        value = value - top.astype(F32)
+    return out
+
+
+def times(left, right):
+    rows = left.shape[0]
+    parts = split(left, len(right))
+    total = None
+    for order, piece in enumerate(right):
+        used = parts[: len(right) - order]
+        got = jnp.dot(jnp.concatenate(used, axis=0), piece, preferred_element_type=F32)
+        for j in range(len(used)):
+            term = got[j * rows : (j + 1) * rows]
+            total = term if total is None else total + term
+    return total
+
+
+def on_diagonal(wide, parts):
+    rows = wide.shape[0]
+    pair = wide.shape[1] // 2
+    first = lax.broadcasted_iota(jnp.int32, (rows, pair), 1) < rows
+    zero = jnp.zeros((rows, pair), BF16)
+    out = []
+    for part in split(wide, parts):
+        ahead, after = part[:, :pair], part[:, pair:]
+        none = jnp.zeros_like(ahead)
+        out.append(
+            jnp.concatenate(
+                [
+                    jnp.concatenate([jnp.where(first, ahead, none), zero], axis=1),
+                    jnp.concatenate([jnp.where(first, none, ahead), zero], axis=1),
+                    jnp.concatenate([zero, jnp.where(first, after, none)], axis=1),
+                    jnp.concatenate([zero, jnp.where(first, none, after)], axis=1),
+                ],
+                axis=0,
+            )
+        )
+    return out
+
+
+def query_kernel(first_doc, recv_ref, out_ref, gram_ref, rows_ref, count_ref):
+    docs, low, _ = out_ref.shape
+    sources, per, wide = recv_ref.shape
+    cap = per - TAIL
+    rows = jnp.concatenate([recv_ref[s, :cap, :] for s in range(sources)], axis=0)
+    rows_ref[...] = rows.T
+    half = lax.broadcasted_iota(jnp.int32, (1, wide), 1) < low
+    named = [recv_ref[s, cap:, :].astype(F32)[:1] for s in range(sources)]
+    slot = jnp.concatenate([jnp.where(half, named[s], named[s + 1]) for s in range(0, sources, 2)], axis=1)
+    across = rows_ref[...]
+    for d in range(docs):
+        mine = (slot == (first_doc + d + 1)).astype(F32)
+        gram_ref[d] = jnp.dot(across * mine.astype(BF16), rows, preferred_element_type=F32)
+        count_ref[d : d + 1, :] = jnp.broadcast_to(jnp.sum(mine, axis=1, keepdims=True), (1, wide))
+
+    row_at = lax.broadcasted_iota(jnp.int32, (low, wide), 0)
+    lane_at = lax.broadcasted_iota(jnp.int32, (low, wide), 1)
+    first = lane_at < low
+    eye = ((row_at == lane_at) | (row_at + low == lane_at)).astype(F32)
+    eyes = jnp.concatenate([eye, eye], axis=1)
+    powers, scales, mixed = [], [], []
+    for g in range(0, docs, 2):
+        errors, inverses, grads = [], [], []
+        for d in (g, g + 1):
+            both = gram_ref[d]
+            outer = jnp.where(first, both[:low], both[low:])
+            damped = outer / (count_ref[d : d + 1, :] + 1.0) + eye
+            sums = jnp.sum(jnp.abs(damped), axis=0, keepdims=True)
+            bound_b = jnp.max(jnp.where(half, sums, 0.0), axis=1, keepdims=True)
+            bound_a = jnp.max(jnp.where(half, 0.0, sums), axis=1, keepdims=True)
+            inverse = 1.0 / jnp.where(half, bound_b, bound_a)
+            errors.append(eye - damped * inverse)
+            inverses.append(inverse)
+            grads.append(jnp.where(first, 0.0, both[:low]))
+        powers.append(jnp.concatenate(errors, axis=1))
+        scales.append(jnp.concatenate(inverses, axis=1))
+        mixed.append(grads)
+    totals = [eyes + power for power in powers]
+    powers = [times(power, on_diagonal(power, 2)) for power in powers]
+    for _ in range(NEWTON_STEPS - 2):
+        stepped = [
+            times(jnp.concatenate([power, total], axis=0), on_diagonal(power, 2))
+            for power, total in zip(powers, totals)
+        ]
+        powers = [both[:low] for both in stepped]
+        totals = [total + both[low:] for total, both in zip(totals, stepped)]
+    totals = [total + times(total, on_diagonal(power, 2)) for power, total in zip(powers, totals)]
+    totals = [total * scale for total, scale in zip(totals, scales)]
+    tilted = []
+    for total, grads in zip(totals, mixed):
+        right = []
+        gap = jnp.zeros((low, 2 * wide), BF16)
+        zero = jnp.zeros((low, wide), BF16)
+        for ahead, after in zip(split(grads[0], 3), split(grads[1], 3)):
+            right.append(
+                jnp.concatenate(
+                    [jnp.concatenate([ahead, zero], axis=1), gap, jnp.concatenate([zero, after], axis=1), gap], axis=0
+                )
+            )
+        tilted.append(times(total, right))
+    found = [times(tilt, on_diagonal(total, 3)) for tilt, total in zip(tilted, totals)]
+    for g, query in enumerate(found):
+        out_ref[2 * g] = query[:, low:wide].astype(BF16)
+        out_ref[2 * g + 1] = query[:, wide + low :].astype(BF16)
+
+
+def queries_of(recv, first_doc, docs, low):
+    sources, per, wide = recv.shape
+    found = pl.pallas_call(
+        functools.partial(query_kernel, first_doc),
+        out_shape=jax.ShapeDtypeStruct((docs, low, low), BF16),
+        in_specs=[pl.BlockSpec(memory_space=pltpu.VMEM)],
+        out_specs=pl.BlockSpec(memory_space=pltpu.VMEM),
+        scratch_shapes=[
+            pltpu.VMEM((docs, wide, wide), F32),
+            pltpu.VMEM((wide, sources * (per - TAIL)), BF16),
+            pltpu.VMEM((docs, wide), F32),
+        ],
+        cost_estimate=pl.CostEstimate(flops=4 * 10**9, bytes_accessed=2**20, transcendentals=0),
+        compiler_params=pltpu.CompilerParams(vmem_limit_bytes=40 * 2**20),
+    )(recv)
+    return found.reshape(docs, low * low)
+
+
+def order_kernel(from_ref, *refs):
+    chunks = (len(refs) - 1) // 2
+    out_ref = refs[-1]
+    docs = refs[0].shape[1]
+    blocks = refs[0].shape[0]
+    for k in range(out_ref.shape[0]):
+        place = from_ref[k]
+
+        @pl.when(place < blocks)
+        def _():
+            for c in range(chunks):
+                out_ref[k, c * docs : (c + 1) * docs, :] = refs[2 * c][place]
+
+        @pl.when(place >= blocks)
+        def _():
+            for c in range(chunks):
+                out_ref[k, c * docs : (c + 1) * docs, :] = refs[2 * c + 1][place - blocks]
+
+
+def ring_tables(owners):
+    chips = owners // 2
+    line = chips // 2
+    chip_at = [2 * p if p < line else 2 * (chips - 1 - p) + 1 for p in range(chips)]
+    spot = {m: p for p, m in enumerate(chip_at)}
+    pairs = []
+    for p in range(chips):
+        pairs.append((2 * chip_at[p], 2 * chip_at[(p + 1) % chips]))
+        pairs.append((2 * chip_at[p] + 1, 2 * chip_at[(p - 1) % chips] + 1))
+    held = {}
+    for device in range(owners):
+        m, core = divmod(device, 2)
+        sign = -1 if core == 0 else 1
+        listed = [device]
+        for hop in range(1, chips // 2):
+            there = chip_at[(spot[m] + sign * hop) % chips]
+            listed += [2 * there, 2 * there + 1]
+        listed.append(2 * chip_at[(spot[m] + sign * (chips // 2)) % chips] + core)
+        held[device] = listed
+    where = np.zeros((owners, STOPS), np.int32)
+    for device in range(owners):
+        for k in range(STOPS):
+            owner = (device + LEAD - k) % owners
+            if owner in held[device]:
+                where[device, k] = held[device].index(owner)
+            else:
+                where[device, k] = chips + held[device ^ 1].index(owner)
+    swap = [(device, device ^ 1) for device in range(owners)]
+    return pairs, swap, where
+
+
+def gathered(query_inputs, query_grads, proj_in, proj_out, train_rows, token_owner, token_slot):
+    toks = query_inputs.shape[0]
+    low = proj_in.shape[1]
+    owners = lax.axis_size("blk")
+    chips = owners // 2
+    train = train_rows.shape[0]
+    cap = 4 * toks // owners
+    ring, swap, where = ring_tables(owners)
+    place = lax.axis_index("blk")
+    odd = lax.rem(place, 2) == 1
+    from_where = jnp.asarray(where)[place]
+
+    other_rows = lax.ppermute(train_rows, "blk", swap)
+    both_rows = jnp.concatenate([train_rows, other_rows], axis=0)
+
+    send = packed_rows(query_inputs, query_grads, proj_in, proj_out, token_owner, token_slot, owners, cap)
+    recv = lax.all_to_all(send, "blk", split_axis=0, concat_axis=0, tiled=True)
+
+    def scoring(block):
+        return lax.dot_general(
+            block, both_rows, (((1,), (1,)), ((), ())), preferred_element_type=F32
+        ).astype(BF16)
+
+    chunks = 2
+    docs = DOC_DEV // chunks
+    results = []
+    for c in range(chunks):
+        mine = queries_of(recv, c * docs, docs, low)
+        theirs = lax.ppermute(mine, "blk", swap)
+        even_block = jnp.where(odd, theirs, mine)
+        odd_block = jnp.where(odd, mine, theirs)
+        travelling = jnp.concatenate([even_block, odd_block], axis=0)
+        tiles = [scoring(mine)]
+        for hop in range(1, chips // 2):
+            travelling = lax.ppermute(travelling, "blk", ring)
+            tiles.append(scoring(travelling))
+        last = jnp.where(odd, travelling[docs:], travelling[:docs])
+        tiles.append(scoring(lax.ppermute(last, "blk", ring)))
+        tiles = jnp.concatenate(tiles, axis=0).reshape(chips, docs, 2 * train)
+        own_tiles = tiles[:, :, :train]
+        results += [own_tiles, lax.ppermute(tiles[:, :, train:], "blk", swap)]
+    return pl.pallas_call(
+        order_kernel,
+        out_shape=jax.ShapeDtypeStruct((STOPS, DOC_DEV, train), BF16),
+        in_specs=[pl.BlockSpec(memory_space=pltpu.SMEM)] + [pl.BlockSpec(memory_space=pltpu.VMEM)] * (2 * chunks),
+        out_specs=pl.BlockSpec(memory_space=pltpu.VMEM),
+    )(from_where, *results)
 def passed_along(value, axis, steps):
     count = lax.axis_size(axis)
     pairs = [(source, (source + steps) % count) for source in range(count)]
@@ -32,7 +326,7 @@
     return approx
 
 
-def local(query_inputs, query_grads, proj_in, proj_out, train_rows, token_owner, token_slot):
+def passed(query_inputs, query_grads, proj_in, proj_out, train_rows, token_owner, token_slot):
     tok_count = query_inputs.shape[0]
     width_low = proj_in.shape[1]
     owners = lax.axis_size("blk")
@@ -130,6 +424,14 @@
 
 
 def solution(mesh):
+    owners = mesh.shape["blk"]
+
+    def local(query_inputs, query_grads, proj_in, *rest):
+        low = proj_in.shape[1]
+        cap = 4 * query_inputs.shape[0] // owners
+        close = owners % 4 == 0 and STOPS <= owners <= 2 * STOPS and cap == low and cap % TAIL == 0
+        return (gathered if close else passed)(query_inputs, query_grads, proj_in, *rest)
+
     placed = (
         P(("groups", "blk"), None),
         P(("groups", "blk"), None),

time: 152 us -> 84.8 us (0.56); the launches traced: 149 us -> 84.3 us
  matrix products: 66.1 us -> 13.9 us
  starting transfers between devices: 33.6 us -> 13.4 us
  Pallas kernels: 0 us -> 14.5 us
  waiting for transfers between devices: 36.4 us -> 28.1 us
  local copies, waits for them, and re-layouts: 5.39 us -> 13.4 us
  other arithmetic: 7.02 us -> 0.82 us
    dot_general x44 -> x10, matrix products: 66.1 us -> 13.9 us  [scoring(): lax.dot_general(block, both_rows, (((1,), (1,)), ((), ())), preferred_ele...]
    ppermute x11 -> x13, starting transfers between devices: 22.5 us -> 6.06 us  [the longest x6 3.77 us: gathered(): travelling = lax.ppermute(travelling, 'blk', ring)]
    pallas_call x0 -> x4, Pallas kernels: none -> 14.5 us  [the longest x2 9.17 us: queries_of(): pl.pallas_call(functools.partial(query_kernel, first_doc), out_shape=jax....]
    ppermute x11 -> x13, waiting for transfers between devices: 26.7 us -> 17 us  [the longest x6 16.6 us: gathered(): travelling = lax.ppermute(travelling, 'blk', ring)]
    unnamed x20 -> x16, local copies, waits for them, and re-layouts: 0.09 us -> 8.58 us
    all_to_all x2 -> x1, starting transfers between devices: 11.1 us -> 7.38 us  [gathered(): recv = lax.all_to_all(send, 'blk', split_axis=0, concat_axis=0, tiled=True)]
    reduce_max x2 -> x0, other arithmetic: 2.25 us -> none  [inverse_factor(): row_bound = jnp.max(jnp.sum(jnp.abs(damped), axis=2), axis=1)]
    slice x3 -> x2, local copies, waits for them, and re-layouts: 3.37 us -> 1.31 us  [gathered(): results += [own_tiles, lax.ppermute(tiles[:, :, train:], 'blk', swap)]]
  transfers between devices with their start and end apart: 13 -> 14, of which waited for: 8 -> 8; matrix products, arithmetic and copies ran while one was open for 6% -> 23% of each run, Pallas kernels for 0% -> 5%
where the time goes in v1:
time: 84.8 us; the launch traced here: 84.3 us
  waiting for transfers between devices  28.1 us (33%)
  Pallas kernels  14.5 us (17%)
  matrix products  13.9 us (16%)
  local copies, waits for them, and re-layouts  13.4 us (16%)
  starting transfers between devices  13.4 us (16%)
    ppermute x6, waiting for transfers between devices, gathered(): travelling = lax.ppermute(travelling, 'blk', ring)  16.6 us
    dot_general x10, matrix products, scoring(): lax.dot_general(block, both_rows, (((1,), (1,)), ((), ())), preferred_ele...  13.9 us
    all_to_all x1, waiting for transfers between devices, gathered(): recv = lax.all_to_all(send, 'blk', split_axis=0, concat_axis=0, tiled=True)  11.1 us
    pallas_call x2, Pallas kernels, queries_of(): pl.pallas_call(functools.partial(query_kernel, first_doc), out_shape=jax....  9.17 us
    unnamed x16, local copies, waits for them, and re-layouts  8.58 us
    all_to_all x1, starting transfers between devices, gathered(): recv = lax.all_to_all(send, 'blk', split_axis=0, concat_axis=0, tiled=True)  7.38 us
    ppermute x6, starting transfers between devices, gathered(): travelling = lax.ppermute(travelling, 'blk', ring)  3.77 us
    pallas_call x1, Pallas kernels, packed_rows(): pl.pallas_call(pack_kernel, grid=(steps,), out_shape=jax.ShapeDtypeStruct...  3.56 us
  transfers between devices with their start and end apart: 14, of which 8 were waited for; matrix products, arithmetic and copies ran while one was open for 23% of the time, Pallas kernels for 5%

profile of v1, /device:TPU:0, one launch (start us, length us, event | category | flops | bytes accessed | tf_op | source)
XLA Modules:
  0.0 84.3 jit_solution(3215524303613953231)
XLA Ops:
  0.0 1.5 %copy.9.pin_ref = bf16[4096,64]{1,0:T(8,128)(2,1)S(1)} copy(bf16[4096,64]{0,1:T(8,128)(2,1)} %param.10) | data formatting | bytes 1048576 | tf_op args[2]
  1.5 1.5 %copy.10.pout_ref = bf16[4096,64]{1,0:T(8,128)(2,1)S(1)} copy(bf16[4096,64]{0,1:T(8,128)(2,1)} %param.11) | data formatting | bytes 1048576 | tf_op args[3]
  3.9 1.6 %copy-done = bf16[256,4096]{1,0:T(8,128)(2,1)S(1)} copy-done((bf16[256,4096]{1,0:T(8,128)(2,1)S(1)}, bf16[256,4096]{1,0:T(8,128)(2,1)}, u32[]{:S(2)}) %copy-start) | copy-done | bytes 2097176
  5.5 1.6 %copy-done.1 = bf16[256,4096]{1,0:T(8,128)(2,1)S(1)} copy-done((bf16[256,4096]{1,0:T(8,128)(2,1)S(1)}, bf16[256,4096]{1,0:T(8,128)(2,1)}, u32[]{:S(2)}) %copy-start.1) | copy-done | bytes 2097176
  7.7 3.6 %shard_map.82 = bf16[16,80,128]{2,1,0:T(8,128)(2,1)} custom-call(bf16[256,4096]{1,0:T(8,128)(2,1)S(1)} %copy-done, bf16[256,4096]{1,0:T(8,128)(2,1)S(1)} %copy-done.1, bf16[4096,64]{1,0:T(8,128)(2,1)S(1)} %copy.9.pin_ref, bf16[4096,64]{1,0:T(8,128)(2,1)S(1)} %copy.10.pout_ref, s32[256,1]{1,0:T(8,128)S(1)} %copy.11.owner_ref, s32[1,256]{1,0:T(1,128)S(1)} %bitcast.25), custom_call_target="tpu_custom_call" | custom-call | tf_op jit(solution)/shard_map/pallas_call | solution.py:65
  11.3 7.4 %all-to-all-start = ((bf16[16,80,128]{2,1,0:T(8,128)(2,1)}), bf16[16,80,128]{2,1,0:T(8,128)(2,1)S(1)}, u32[]{:S(2)}, u32[]{:S(2)}) async-start(bf16[16,80,128]{2,1,0:T(8,128)(2,1)} %shard_map.82), calls=%async_computation | async-start | bytes 655360 | tf_op jit(solution)/shard_map/all_to_all | solution.py:278
  18.7 11.1 %all-to-all-done.recv_ref = bf16[16,80,128]{2,1,0:T(8,128)(2,1)S(1)} async-done(((bf16[16,80,128]{2,1,0:T(8,128)(2,1)}), bf16[16,80,128]{2,1,0:T(8,128)(2,1)S(1)}, u32[]{:S(2)}, u32[]{:S(2)}) %all-to-all-start) | async-done | bytes 327712 | tf_op jit(solution)/shard_map/all_to_all | solution.py:278
  29.8 4.6 %shard_map.83 = bf16[16,64,64]{2,1,0:T(8,128)(2,1)S(1)} custom-call(bf16[16,80,128]{2,1,0:T(8,128)(2,1)S(1)} %all-to-all-done.recv_ref), custom_call_target="tpu_custom_call" | custom-call | flops 4000000000 | bytes 1048576 | tf_op jit(solution)/shard_map/pallas_call | solution.py:196
  34.8 4.6 %shard_map.84 = bf16[16,64,64]{2,1,0:T(8,128)(2,1)S(1)} custom-call(bf16[16,80,128]{2,1,0:T(8,128)(2,1)S(1)} %all-to-all-done.recv_ref), custom_call_target="tpu_custom_call" | custom-call | flops 4000000000 | bytes 1048576 | tf_op jit(solution)/shard_map/pallas_call | solution.py:196
  43.0 3.6 %collective-permute-done.2 = bf16[32,4096]{1,0:T(8,128)(2,1)S(1)} collective-permute-done((bf16[32,4096]{1,0:T(8,128)(2,1)S(1)}, bf16[32,4096]{1,0:T(8,128)(2,1)S(1)}, u32[]{:S(2)}, u32[]{:S(2)}) %collective-permute-start.2) | collective-permute-done | bytes 262176 | tf_op jit(solution)/shard_map/ppermute | solution.py:296
  47.2 2.3 %collective-permute-done.8 = bf16[32,4096]{1,0:T(8,128)(2,1)S(1)} collective-permute-done((bf16[32,4096]{1,0:T(8,128)(2,1)}, bf16[32,4096]{1,0:T(8,128)(2,1)S(1)}, u32[]{:S(2)}, u32[]{:S(2)}) %collective-permute-start.8) | collective-permute-done | bytes 262176 | tf_op jit(solution)/shard_map/ppermute | solution.py:296
  50.0 3.1 %collective-permute-done.3 = bf16[32,4096]{1,0:T(8,128)(2,1)} collective-permute-done((bf16[32,4096]{1,0:T(8,128)(2,1)S(1)}, bf16[32,4096]{1,0:T(8,128)(2,1)}, u32[]{:S(2)}, u32[]{:S(2)}) %collective-permute-start.3) | collective-permute-done | bytes 262176 | tf_op jit(solution)/shard_map/ppermute | solution.py:296
  53.9 2.0 %collective-permute-done.9 = bf16[32,4096]{1,0:T(8,128)(2,1)S(1)} collective-permute-done((bf16[32,4096]{1,0:T(8,128)(2,1)S(1)}, bf16[32,4096]{1,0:T(8,128)(2,1)S(1)}, u32[]{:S(2)}, u32[]{:S(2)}) %collective-permute-start.9) | collective-permute-done | bytes 262176 | tf_op jit(solution)/shard_map/ppermute | solution.py:296
  56.3 3.4 %collective-permute-done.4 = bf16[32,4096]{1,0:T(8,128)(2,1)S(1)} collective-permute-done((bf16[32,4096]{1,0:T(8,128)(2,1)}, bf16[32,4096]{1,0:T(8,128)(2,1)S(1)}, u32[]{:S(2)}, u32[]{:S(2)}) %collective-permute-start.4) | collective-permute-done | bytes 262176 | tf_op jit(solution)/shard_map/ppermute | solution.py:296
  60.3 2.2 %collective-permute-done.10 = bf16[32,4096]{1,0:T(8,128)(2,1)S(1)} collective-permute-done((bf16[32,4096]{1,0:T(8,128)(2,1)S(1)}, bf16[32,4096]{1,0:T(8,128)(2,1)S(1)}, u32[]{:S(2)}, u32[]{:S(2)}) %collective-permute-start.10) | collective-permute-done | bytes 262176 | tf_op jit(solution)/shard_map/ppermute | solution.py:296
  63.1 1.7 %constant_dynamic-update-slice_fusion = bf16[512,4096]{1,0:T(8,128)(2,1)S(1)} fusion(bf16[512,4096]{1,0:T(8,128)(2,1)S(1)} %constant_dynamic-update-slice_fusion.1, bf16[256,4096]{1,0:T(8,128)(2,1)} %collective-permute-done), kind=kLoop, calls=%fused_computation.28 | loop fusion | bytes 4194304 | tf_op jit(solution)/shard_map/concatenate | solution.py:275
  66.0 1.4 %fusion.5 = bf16[128,512]{1,0:T(8,128)(2,1)S(1)} fusion(bf16[128,512]{1,0:T(8,128)(2,1)S(1)} %fusion.9, bf16[32,4096]{1,0:T(8,128)(2,1)S(1)} %collective-permute-done.2, bf16[512,4096]{1,0:T(8,128)(2,1)S(1)} %constant_dynamic-update-slice_fusion), kind=kOutput, calls=%fused_computation.11 | convolution fusion | flops 134234112 | bytes 4489216 | tf_op jit(solution)/shard_map/dot_general | solution.py:281
  67.4 2.3 %fusion.4 = bf16[128,512]{1,0:T(8,128)(2,1)S(1)} fusion(bf16[128,512]{1,0:T(8,128)(2,1)S(1)} %fusion.5, bf16[32,4096]{1,0:T(8,128)(2,1)} %collective-permute-done.3, bf16[512,4096]{1,0:T(8,128)(2,1)S(1)} %constant_dynamic-update-slice_fusion), kind=kOutput, calls=%fused_computation.9 | convolution fusion | flops 134234112 | bytes 4489216 | tf_op jit(solution)/shard_map/dot_general | solution.py:281
  69.7 1.4 %fusion.3 = bf16[128,512]{1,0:T(8,128)(2,1)S(1)} fusion(bf16[128,512]{1,0:T(8,128)(2,1)S(1)} %fusion.4, bf16[32,4096]{1,0:T(8,128)(2,1)S(1)} %collective-permute-done.4, bf16[512,4096]{1,0:T(8,128)(2,1)S(1)} %constant_dynamic-update-slice_fusion), kind=kOutput, calls=%fused_computation.7 | convolution fusion | flops 134234112 | bytes 4489216 | tf_op jit(solution)/shard_map/dot_general | solution.py:281
  74.1 1.3 %fusion.2 = bf16[128,512]{1,0:T(8,128)(2,1)S(1)} fusion(bf16[128,512]{1,0:T(8,128)(2,1)S(1)} %fusion.7, bf16[32,4096]{1,0:T(8,128)(2,1)S(1)} %collective-permute-done.8, bf16[512,4096]{1,0:T(8,128)(2,1)S(1)} %constant_dynamic-update-slice_fusion), kind=kOutput, calls=%fused_computation.5 | convolution fusion | flops 134234112 | bytes 4489216 | tf_op jit(solution)/shard_map/dot_general | solution.py:281
  75.5 1.4 %fusion.1 = bf16[128,512]{1,0:T(8,128)(2,1)S(1)} fusion(bf16[128,512]{1,0:T(8,128)(2,1)S(1)} %fusion.2, bf16[32,4096]{1,0:T(8,128)(2,1)S(1)} %collective-permute-done.9, bf16[512,4096]{1,0:T(8,128)(2,1)S(1)} %constant_dynamic-update-slice_fusion), kind=kOutput, calls=%fused_computation.3 | convolution fusion | flops 134234112 | bytes 4489216 | tf_op jit(solution)/shard_map/dot_general | solution.py:281
  76.8 1.4 %fusion = bf16[128,512]{1,0:T(8,128)(2,1)S(1)} fusion(bf16[128,512]{1,0:T(8,128)(2,1)S(1)} %fusion.1, bf16[32,4096]{1,0:T(8,128)(2,1)S(1)} %collective-permute-done.10, bf16[512,4096]{1,0:T(8,128)(2,1)S(1)} %constant_dynamic-update-slice_fusion), kind=kOutput, calls=%fused_computation.1 | convolution fusion | flops 134234112 | bytes 4489216 | tf_op jit(solution)/shard_map/dot_general | solution.py:281
  80.6 1.3 %dynamic-slice_bitcast_fusion.from_ref = s32[12]{0:T(128)} fusion(s32[16,12]{1,0:T(8,128)} %constant.15.clone, s32[]{:T(128)S(6)} %select_n.31), kind=kLoop, calls=%fused_computation.30 | loop fusion | bytes 100 | tf_op jit(solution)/shard_map/squeeze | solution.py:272
  82.5 1.8 %shard_map.85 = bf16[12,32,256]{2,1,0:T(8,128)(2,1)} custom-call(s32[12]{0:T(128)} %dynamic-slice_bitcast_fusion.from_ref, bf16[8,16,256]{2,1,0:T(8,128)(2,1)} %get-tuple-element.12.refs_0_, bf16[8,16,256]{2,1,0:T(8,128)(2,1)} %copy-done.4, bf16[8,16,256]{2,1,0:T(8,128)(2,1)} %get-tuple-element.10.refs_2_, bf16[8,16,256]{2,1,0:T(8,128)(2,1)} %copy-done.5), custom_call_target="tpu_custom_call" | custom-call | tf_op jit(solution)/shard_map/pallas_call | solution.py:303
  (46 shorter events, 16.2 us)
Async XLA Ops:
  3.9 1.6 %copy-start = (bf16[256,4096]{1,0:T(8,128)(2,1)S(1)}, bf16[256,4096]{1,0:T(8,128)(2,1)}, u32[]{:S(2)}) copy-start(bf16[256,4096]{1,0:T(8,128)(2,1)} %inputs_ref.1) | copy-start | bytes 6291460
  5.5 1.6 %copy-start.1 = (bf16[256,4096]{1,0:T(8,128)(2,1)S(1)}, bf16[256,4096]{1,0:T(8,128)(2,1)}, u32[]{:S(2)}) copy-start(bf16[256,4096]{1,0:T(8,128)(2,1)} %grads_ref.1) | copy-start | bytes 6291460
  7.1 0.7 copy-start.2
  11.3 18.5 %all-to-all-start = ((bf16[16,80,128]{2,1,0:T(8,128)(2,1)}), bf16[16,80,128]{2,1,0:T(8,128)(2,1)S(1)}, u32[]{:S(2)}, u32[]{:S(2)}) async-start(bf16[16,80,128]{2,1,0:T(8,128)(2,1)} %shard_map.82), calls=%async_computation | async-start | bytes 655360 | tf_op jit(solution)/shard_map/all_to_all | solution.py:278
  34.6 12.5 %copy-start.3 = (bf16[256,4096]{1,0:T(8,128)(2,1)S(1)}, bf16[256,4096]{1,0:T(8,128)(2,1)}, u32[]{:S(2)}) copy-start(bf16[256,4096]{1,0:T(8,128)(2,1)} %param.12) | copy-start | bytes 6291460
  34.7 5.5 %collective-permute-start.1 = (bf16[16,4096]{1,0:T(8,128)(2,1)S(1)}, bf16[16,4096]{1,0:T(8,128)(2,1)S(1)}, u32[]{:S(2)}, u32[]{:S(2)}) collective-permute-start(bf16[16,4096]{1,0:T(8,128)(2,1)S(1)} %reshape.16), channel_id=1, source_target_pairs={{0,1},{1,0},{2,3},{3,2},{4,5},{5,4},{6,7},{7,6},{8,9},{9,8},{10,11... | collective-permute-start | bytes 393224 | tf_op jit(solution)/shard_map/ppermute | solution.py:290
  39.7 1.4 %collective-permute-start.7 = (bf16[16,4096]{1,0:T(8,128)(2,1)S(1)}, bf16[16,4096]{1,0:T(8,128)(2,1)S(1)}, u32[]{:S(2)}, u32[]{:S(2)}) collective-permute-start(bf16[16,4096]{1,0:T(8,128)(2,1)S(1)} %reshape.18), channel_id=1, source_target_pairs={{0,1},{1,0},{2,3},{3,2},{4,5},{5,4},{6,7},{7,6},{8,9},{9,8},{10,11... | collective-permute-start | bytes 393224 | tf_op jit(solution)/shard_map/ppermute | solution.py:290
  40.2 6.4 %collective-permute-start.2 = (bf16[32,4096]{1,0:T(8,128)(2,1)S(1)}, bf16[32,4096]{1,0:T(8,128)(2,1)S(1)}, u32[]{:S(2)}, u32[]{:S(2)}) collective-permute-start(bf16[32,4096]{1,0:T(8,128)(2,1)S(1)} %pad_maximum_fusion), channel_id=1, source_target_pairs={{0,4},{1,3},{4,8},{5,1},{8,12},{9,5},{12,14},{13,9},{14,10},{15,13... | collective-permute-start | bytes 786440 | tf_op jit(solution)/shard_map/ppermute | solution.py:296
  41.9 7.6 %collective-permute-start.8 = (bf16[32,4096]{1,0:T(8,128)(2,1)}, bf16[32,4096]{1,0:T(8,128)(2,1)S(1)}, u32[]{:S(2)}, u32[]{:S(2)}) collective-permute-start(bf16[32,4096]{1,0:T(8,128)(2,1)} %pad_maximum_fusion.1), channel_id=1, source_target_pairs={{0,4},{1,3},{4,8},{5,1},{8,12},{9,5},{12,14},{13,9},{14,10},{15,13... | collective-permute-start | bytes 786440 | tf_op jit(solution)/shard_map/ppermute | solution.py:296
  46.6 6.5 %collective-permute-start.3 = (bf16[32,4096]{1,0:T(8,128)(2,1)S(1)}, bf16[32,4096]{1,0:T(8,128)(2,1)}, u32[]{:S(2)}, u32[]{:S(2)}) collective-permute-start(bf16[32,4096]{1,0:T(8,128)(2,1)S(1)} %collective-permute-done.2), channel_id=1, source_target_pairs={{0,4},{1,3},{4,8},{5,1},{8,12},{9,5},{12,14},{13,9},{14,10},{15,13... | collective-permute-start | bytes 786440 | tf_op jit(solution)/shard_map/ppermute | solution.py:296
  47.2 15.9 %collective-permute-start = (bf16[256,4096]{1,0:T(8,128)(2,1)S(1)}, bf16[256,4096]{1,0:T(8,128)(2,1)}, u32[]{:S(2)}, u32[]{:S(2)}) collective-permute-start(bf16[256,4096]{1,0:T(8,128)(2,1)S(1)} %copy-done.3), channel_id=1, source_target_pairs={{0,1},{1,0},{2,3},{3,2},{4,5},{5,4},{6,7},{7,6},{8,9},{9,8},{10,11... | collective-permute-start | bytes 6291464 | tf_op jit(solution)/shard_map/ppermute | solution.py:274
  49.5 6.4 %collective-permute-start.9 = (bf16[32,4096]{1,0:T(8,128)(2,1)S(1)}, bf16[32,4096]{1,0:T(8,128)(2,1)S(1)}, u32[]{:S(2)}, u32[]{:S(2)}) collective-permute-start(bf16[32,4096]{1,0:T(8,128)(2,1)S(1)} %collective-permute-done.8), channel_id=1, source_target_pairs={{0,4},{1,3},{4,8},{5,1},{8,12},{9,5},{12,14},{13,9},{14,10},{15,13... | collective-permute-start | bytes 786440 | tf_op jit(solution)/shard_map/ppermute | solution.py:296
  53.1 6.6 %collective-permute-start.4 = (bf16[32,4096]{1,0:T(8,128)(2,1)}, bf16[32,4096]{1,0:T(8,128)(2,1)S(1)}, u32[]{:S(2)}, u32[]{:S(2)}) collective-permute-start(bf16[32,4096]{1,0:T(8,128)(2,1)} %collective-permute-done.3), channel_id=1, source_target_pairs={{0,4},{1,3},{4,8},{5,1},{8,12},{9,5},{12,14},{13,9},{14,10},{15,13... | collective-permute-start | bytes 786440 | tf_op jit(solution)/shard_map/ppermute | solution.py:296
  55.8 6.7 %collective-permute-start.10 = (bf16[32,4096]{1,0:T(8,128)(2,1)S(1)}, bf16[32,4096]{1,0:T(8,128)(2,1)S(1)}, u32[]{:S(2)}, u32[]{:S(2)}) collective-permute-start(bf16[32,4096]{1,0:T(8,128)(2,1)S(1)} %collective-permute-done.9), channel_id=1, source_target_pairs={{0,4},{1,3},{4,8},{5,1},{8,12},{9,5},{12,14},{13,9},{14,10},{15,13... | collective-permute-start | bytes 786440 | tf_op jit(solution)/shard_map/ppermute | solution.py:296
  59.7 12.5 %collective-permute-start.5 = (bf16[16,4096]{1,0:T(8,128)(2,1)S(1)}, bf16[16,4096]{1,0:T(8,128)(2,1)S(1)}, u32[]{:S(2)}, u32[]{:S(2)}) collective-permute-start(bf16[16,4096]{1,0:T(8,128)(2,1)S(1)} %slice_select_fusion.1), channel_id=1, source_target_pairs={{0,4},{1,3},{4,8},{5,1},{8,12},{9,5},{12,14},{13,9},{14,10},{15,13... | collective-permute-start | bytes 393224 | tf_op jit(solution)/shard_map/ppermute | solution.py:299
  62.5 15.7 %collective-permute-start.11 = (bf16[16,4096]{1,0:T(8,128)(2,1)S(1)}, bf16[16,4096]{1,0:T(8,128)(2,1)S(1)}, u32[]{:S(2)}, u32[]{:S(2)}) collective-permute-start(bf16[16,4096]{1,0:T(8,128)(2,1)S(1)} %slice_select_fusion), channel_id=1, source_target_pairs={{0,4},{1,3},{4,8},{5,1},{8,12},{9,5},{12,14},{13,9},{14,10},{15,13... | collective-permute-start | bytes 393224 | tf_op jit(solution)/shard_map/ppermute | solution.py:299
  74.1 7.7 %collective-permute-start.6 = (bf16[8,16,256]{2,1,0:T(8,128)(2,1)S(1)}, bf16[8,16,256]{2,1,0:T(8,128)(2,1)S(1)}, u32[]{:S(2)}, u32[]{:S(2)}) collective-permute-start(bf16[8,16,256]{2,1,0:T(8,128)(2,1)S(1)} %get-tuple-element.11), channel_id=1, source_target_pairs={{0,1},{1,0},{2,3},{3,2},{4,5},{5,4},{6,7},{7,6},{8,9},{9,8},{10,11... | collective-permute-start | bytes 196616 | tf_op jit(solution)/shard_map/ppermute | solution.py:302
  80.1 1.8 %collective-permute-start.12 = (bf16[8,16,256]{2,1,0:T(8,128)(2,1)S(1)}, bf16[8,16,256]{2,1,0:T(8,128)(2,1)S(1)}, u32[]{:S(2)}, u32[]{:S(2)}) collective-permute-start(bf16[8,16,256]{2,1,0:T(8,128)(2,1)S(1)} %get-tuple-element.9), channel_id=1, source_target_pairs={{0,1},{1,0},{2,3},{3,2},{4,5},{5,4},{6,7},{7,6},{8,9},{9,8},{10,11... | collective-permute-start | bytes 196616 | tf_op jit(solution)/shard_map/ppermute | solution.py:302
  81.8 0.6 copy-start.4
  81.8 0.7 copy-start.5

commit v2 on v1

--- a/solution.py
+++ b/solution.py
@@ -1,7 +1,6 @@
 import functools
 import jax
 import jax.numpy as jnp
-import numpy as np
 from jax import lax
 from jax.experimental import pallas as pl
 from jax.experimental.pallas import tpu as pltpu
@@ -15,6 +14,7 @@
 F32 = jnp.float32
 BF16 = jnp.bfloat16
 HIGHEST_PRECISION = lax.Precision.HIGHEST
+LAST_DIMS = (((1,), (1,)), ((), ()))
 
 
 def pack_kernel(inputs_ref, grads_ref, pin_ref, pout_ref, owner_ref, slot_ref, send_ref, ilow_ref, glow_ref):
@@ -25,8 +25,8 @@
         ilow_ref[...] = jnp.zeros_like(ilow_ref)
         glow_ref[...] = jnp.zeros_like(glow_ref)
 
-    ilow_ref[...] += jnp.dot(inputs_ref[...], pin_ref[...], preferred_element_type=F32)
-    glow_ref[...] += jnp.dot(grads_ref[...], pout_ref[...], preferred_element_type=F32)
+    ilow_ref[...] += lax.dot_general(inputs_ref[...], pin_ref[...], LAST_DIMS, preferred_element_type=F32)
+    glow_ref[...] += lax.dot_general(grads_ref[...], pout_ref[...], LAST_DIMS, preferred_element_type=F32)
 
     @pl.when(step == pl.num_programs(0) - 1)
     def _():
@@ -34,27 +34,20 @@
         cap = per - TAIL
         toks = slot_ref.shape[1]
         low = jnp.concatenate([glow_ref[...], ilow_ref[...]], axis=1).astype(BF16)
-        owner_col = owner_ref[...]
-        hot = (owner_col == lax.broadcasted_iota(jnp.int32, (toks, owners), 1)).astype(F32)
-        tri = lax.broadcasted_iota(jnp.int32, (toks, toks), 0) > lax.broadcasted_iota(jnp.int32, (toks, toks), 1)
-        before = jnp.dot(tri.astype(F32).astype(BF16), hot.astype(BF16), preferred_element_type=F32)
-        rank = jnp.sum(before * hot, axis=1, keepdims=True)
-        both = jnp.concatenate(
-            [jnp.broadcast_to(rank, (toks, wide)), jnp.broadcast_to(owner_col.astype(F32), (toks, wide))], axis=1
-        ).T
-        rank_row = both[:1]
-        owner_row = both[wide : wide + 1]
-        position = (owner_row * cap + rank_row).astype(jnp.int32)
+        owner = owner_ref[...]
+        hot = (owner == lax.broadcasted_iota(jnp.int32, (owners, toks), 0)).astype(F32)
+        earlier = lax.broadcasted_iota(jnp.int32, (toks, toks), 0) < lax.broadcasted_iota(jnp.int32, (toks, toks), 1)
+        before = jnp.dot(hot.astype(BF16), earlier.astype(F32).astype(BF16), preferred_element_type=F32)
+        rank = jnp.sum(before * hot, axis=0, keepdims=True).astype(jnp.int32)
+        position = owner * cap + rank
         placed = lax.broadcasted_iota(jnp.int32, (owners * cap, toks), 0) == position
         rows = jnp.dot(placed.astype(F32).astype(BF16), low, preferred_element_type=F32).astype(BF16)
-        hot_row = owner_row == lax.broadcasted_iota(jnp.int32, (owners, toks), 0).astype(F32)
-        named = jnp.where(hot_row, slot_ref[...].astype(F32) + 1.0, 0.0).astype(BF16)
-        lane = lax.broadcasted_iota(jnp.int32, (toks, wide), 1) % cap
-        at_lane = (rank.astype(jnp.int32) == lane).astype(F32).astype(BF16)
-        slots = jnp.dot(named, at_lane, preferred_element_type=F32).astype(BF16)
+        named = (hot * (slot_ref[...].astype(F32) + 1.0)).astype(BF16)
+        at_lane = lax.broadcasted_iota(jnp.int32, (wide, toks), 0) % cap == rank
+        slots = lax.dot_general(named, at_lane.astype(F32).astype(BF16), LAST_DIMS, preferred_element_type=F32)
         for o in range(owners):
             send_ref[o, :cap, :] = rows[o * cap : (o + 1) * cap]
-            send_ref[o, cap:, :] = jnp.broadcast_to(slots.astype(F32)[o : o + 1], (TAIL, wide)).astype(BF16)
+            send_ref[o, cap:, :] = jnp.broadcast_to(slots[o : o + 1], (TAIL, wide)).astype(BF16)
 
 
 def packed_rows(query_inputs, query_grads, proj_in, proj_out, token_owner, token_slot, owners, cap):
@@ -69,15 +62,15 @@
         in_specs=[
             pl.BlockSpec((toks, part), lambda i: (0, i)),
             pl.BlockSpec((toks, part), lambda i: (0, i)),
-            pl.BlockSpec((part, low), lambda i: (i, 0)),
-            pl.BlockSpec((part, low), lambda i: (i, 0)),
-            pl.BlockSpec((toks, 1), lambda i: (0, 0)),
+            pl.BlockSpec((low, part), lambda i: (0, i)),
+            pl.BlockSpec((low, part), lambda i: (0, i)),
+            pl.BlockSpec((1, toks), lambda i: (0, 0)),
             pl.BlockSpec((1, toks), lambda i: (0, 0)),
         ],
         out_specs=pl.BlockSpec((owners, cap + TAIL, 2 * low), lambda i: (0, 0, 0)),
         scratch_shapes=[pltpu.VMEM((toks, low), F32), pltpu.VMEM((toks, low), F32)],
         compiler_params=pltpu.CompilerParams(vmem_limit_bytes=40 * 2**20),
-    )(query_inputs, query_grads, proj_in, proj_out, token_owner, token_slot.reshape(1, toks))
+    )(query_inputs, query_grads, proj_in.T, proj_out.T, token_owner.reshape(1, toks), token_slot.reshape(1, toks))
 
 
 def split(value, parts):
@@ -209,54 +202,39 @@
     return found.reshape(docs, low * low)
 
 
-def order_kernel(from_ref, *refs):
+def order_kernel(owners, *refs):
     chunks = (len(refs) - 1) // 2
     out_ref = refs[-1]
     docs = refs[0].shape[1]
-    blocks = refs[0].shape[0]
+    chips = owners // 2
+    device = lax.axis_index("blk")
+
+    def spot(chip):
+        line, row = lax.div(chip, 2), lax.rem(chip, 2)
+        return jnp.where(row == 0, line, chips - 1 - line)
+
+    here, core = spot(lax.div(device, 2)), lax.rem(device, 2)
     for k in range(out_ref.shape[0]):
-        place = from_ref[k]
-
-        @pl.when(place < blocks)
-        def _():
-            for c in range(chunks):
-                out_ref[k, c * docs : (c + 1) * docs, :] = refs[2 * c][place]
-
-        @pl.when(place >= blocks)
-        def _():
-            for c in range(chunks):
-                out_ref[k, c * docs : (c + 1) * docs, :] = refs[2 * c + 1][place - blocks]
-
-
-def ring_tables(owners):
+        owner = lax.rem(device + LEAD - k + owners, owners)
+        second = lax.rem(owner, 2)
+        hops = lax.rem(here - spot(lax.div(owner, 2)) + chips, chips)
+        by_core = jnp.where((hops == 0) | (hops == chips // 2), second, jnp.where(hops < chips // 2, 0, 1))
+        away = jnp.where(hops > chips // 2, chips - hops, hops)
+        index = jnp.where(away == 0, 0, jnp.where(away == chips // 2, chips - 1, 2 * away - 1 + second))
+        own = by_core == core
+        for c in range(chunks):
+            out_ref[k, c * docs : (c + 1) * docs, :] = jnp.where(own, refs[2 * c][index], refs[2 * c + 1][index])
+
+
+def ring_pairs(owners):
     chips = owners // 2
     line = chips // 2
     chip_at = [2 * p if p < line else 2 * (chips - 1 - p) + 1 for p in range(chips)]
-    spot = {m: p for p, m in enumerate(chip_at)}
     pairs = []
     for p in range(chips):
         pairs.append((2 * chip_at[p], 2 * chip_at[(p + 1) % chips]))
         pairs.append((2 * chip_at[p] + 1, 2 * chip_at[(p - 1) % chips] + 1))
-    held = {}
-    for device in range(owners):
-        m, core = divmod(device, 2)
-        sign = -1 if core == 0 else 1
-        listed = [device]
-        for hop in range(1, chips // 2):
-            there = chip_at[(spot[m] + sign * hop) % chips]
-            listed += [2 * there, 2 * there + 1]
-        listed.append(2 * chip_at[(spot[m] + sign * (chips // 2)) % chips] + core)
-        held[device] = listed
-    where = np.zeros((owners, STOPS), np.int32)
-    for device in range(owners):
-        for k in range(STOPS):
-            owner = (device + LEAD - k) % owners
-            if owner in held[device]:
-                where[device, k] = held[device].index(owner)
-            else:
-                where[device, k] = chips + held[device ^ 1].index(owner)
-    swap = [(device, device ^ 1) for device in range(owners)]
-    return pairs, swap, where
+    return pairs, [(device, device ^ 1) for device in range(owners)]
 
 
 def gathered(query_inputs, query_grads, proj_in, proj_out, train_rows, token_owner, token_slot):
@@ -266,46 +244,66 @@
     chips = owners // 2
     train = train_rows.shape[0]
     cap = 4 * toks // owners
-    ring, swap, where = ring_tables(owners)
-    place = lax.axis_index("blk")
-    odd = lax.rem(place, 2) == 1
-    from_where = jnp.asarray(where)[place]
-
+    ring, swap = ring_pairs(owners)
+    odd = lax.rem(lax.axis_index("blk"), 2) == 1
+
+    send = packed_rows(query_inputs, query_grads, proj_in, proj_out, token_owner, token_slot, owners, cap)
     other_rows = lax.ppermute(train_rows, "blk", swap)
-    both_rows = jnp.concatenate([train_rows, other_rows], axis=0)
-
-    send = packed_rows(query_inputs, query_grads, proj_in, proj_out, token_owner, token_slot, owners, cap)
     recv = lax.all_to_all(send, "blk", split_axis=0, concat_axis=0, tiled=True)
+    recv, other_rows = lax.optimization_barrier((recv, other_rows))
 
     def scoring(block):
-        return lax.dot_general(
-            block, both_rows, (((1,), (1,)), ((), ())), preferred_element_type=F32
-        ).astype(BF16)
+        return tuple(
+            lax.dot_general(block, rows, LAST_DIMS, preferred_element_type=F32).astype(BF16)
+            for rows in (train_rows, other_rows)
+        )
+
+    def pair_up(mine):
+        theirs = lax.ppermute(mine, "blk", swap)
+        return jnp.concatenate([jnp.where(odd, theirs, mine), jnp.where(odd, mine, theirs)], axis=0)
 
     chunks = 2
     docs = DOC_DEV // chunks
+    def onward(block, hop):
+        if hop == chips // 2:
+            block = jnp.where(odd, block[docs:], block[:docs])
+        return lax.ppermute(block, "blk", ring)
+
+    moving, tiles, came = [], [], []
+    for c in range(chunks):
+        mine = queries_of(recv, c * docs, docs, low)
+        if c > 0:
+            moving[c - 1] = onward(moving[c - 1], 1)
+            mine, moving[c - 1] = lax.optimization_barrier((mine, moving[c - 1]))
+            came.append(scoring(moving[c - 1]))
+        tiles.append([scoring(mine)])
+        moving.append(pair_up(mine))
+        if c + 1 < chunks:
+            recv, moving[c], tiles[c][0] = lax.optimization_barrier((recv, moving[c], tiles[c][0]))
+    for hop in range(1, chips // 2 + 1):
+        for c in range(chunks):
+            if hop == 1 and c + 1 < chunks:
+                continue
+            block = moving[c]
+            behind = len(came) - chunks - 1
+            if behind >= 0:
+                block, came[behind] = lax.optimization_barrier((block, came[behind]))
+            moving[c] = onward(block, hop)
+            came.append(scoring(moving[c]))
+    for number, tile in enumerate(came):
+        tiles[number % chunks].append(tile)
     results = []
     for c in range(chunks):
-        mine = queries_of(recv, c * docs, docs, low)
-        theirs = lax.ppermute(mine, "blk", swap)
-        even_block = jnp.where(odd, theirs, mine)
-        odd_block = jnp.where(odd, mine, theirs)
-        travelling = jnp.concatenate([even_block, odd_block], axis=0)
-        tiles = [scoring(mine)]
-        for hop in range(1, chips // 2):
-            travelling = lax.ppermute(travelling, "blk", ring)
-            tiles.append(scoring(travelling))
-        last = jnp.where(odd, travelling[docs:], travelling[:docs])
-        tiles.append(scoring(lax.ppermute(last, "blk", ring)))
-        tiles = jnp.concatenate(tiles, axis=0).reshape(chips, docs, 2 * train)
-        own_tiles = tiles[:, :, :train]
-        results += [own_tiles, lax.ppermute(tiles[:, :, train:], "blk", swap)]
+        own, other = (jnp.concatenate(part, axis=0).reshape(chips, docs, train) for part in zip(*tiles[c]))
+        results += [own, lax.ppermute(other, "blk", swap)]
     return pl.pallas_call(
-        order_kernel,
+        functools.partial(order_kernel, owners),
         out_shape=jax.ShapeDtypeStruct((STOPS, DOC_DEV, train), BF16),
-        in_specs=[pl.BlockSpec(memory_space=pltpu.SMEM)] + [pl.BlockSpec(memory_space=pltpu.VMEM)] * (2 * chunks),
+        in_specs=[pl.BlockSpec(memory_space=pltpu.VMEM)] * (2 * chunks),
         out_specs=pl.BlockSpec(memory_space=pltpu.VMEM),
-    )(from_where, *results)
+    )(*results)
+
+
 def passed_along(value, axis, steps):
     count = lax.axis_size(axis)
     pairs = [(source, (source + steps) % count) for source in range(count)]

time: 84.8 us -> 88.1 us (1.039)
  matrix products: 13.9 us -> 29.9 us
  waiting for transfers between devices: 28.1 us -> 19.2 us
  local copies, waits for them, and re-layouts: 13.4 us -> 7.81 us
  starting transfers between devices: 13.4 us -> 15.9 us
    dot_general x10 -> x20, matrix products: 13.9 us -> 29.9 us  [scoring(): lax.dot_general(block, rows, LAST_DIMS, preferred_element_type=F32)]
    ppermute x12, waiting for transfers between devices: 17 us -> 8.09 us  [the longest x8 7.62 us: onward(): return lax.ppermute(block, 'blk', ring)]
    ppermute x12, starting transfers between devices: 6.06 us -> 8.42 us  [the longest x8 8.16 us: onward(): return lax.ppermute(block, 'blk', ring)]
    concatenate x1 -> x0, local copies, waits for them, and re-layouts: 1.73 us -> none  [gathered(): both_rows = jnp.concatenate([train_rows, other_rows], axis=0)]
    slice x2 -> x0, local copies, waits for them, and re-layouts: 1.31 us -> none  [gathered(): results += [own_tiles, lax.ppermute(tiles[:, :, train:], 'blk', swap)]]
    unnamed x16 -> x32, local copies, waits for them, and re-layouts: 8.58 us -> 7.27 us
    squeeze x1 -> x0, local copies, waits for them, and re-layouts: 1.25 us -> none  [gathered(): from_where = jnp.asarray(where)[place]]
  transfers between devices with their start and end apart: 14 -> 14, of which waited for: 8 -> 7; matrix products, arithmetic and copies ran while one was open for 23% -> 27% of each run, Pallas kernels for 5% -> 9%
where the time goes in v2:
time: 88.1 us; the launch traced here: 87.4 us
  matrix products  29.9 us (34%)
  waiting for transfers between devices  19.2 us (22%)
  starting transfers between devices  15.9 us (18%)
  Pallas kernels  14.3 us (16%)
  local copies, waits for them, and re-layouts  7.81 us (9%)
    dot_general x20, matrix products, scoring(): lax.dot_general(block, rows, LAST_DIMS, preferred_element_type=F32)  29.9 us
    all_to_all x1, waiting for transfers between devices, gathered(): recv = lax.all_to_all(send, 'blk', split_axis=0, concat_axis=0, tiled=True)  11.1 us
    pallas_call x2, Pallas kernels, queries_of(): pl.pallas_call(functools.partial(query_kernel, first_doc), out_shape=jax....  9.17 us
    ppermute x8, starting transfers between devices, onward(): return lax.ppermute(block, 'blk', ring)  8.16 us
    ppermute x8, waiting for transfers between devices, onward(): return lax.ppermute(block, 'blk', ring)  7.62 us
    unnamed x32, local copies, waits for them, and re-layouts  7.27 us
    all_to_all x1, starting transfers between devices, gathered(): recv = lax.all_to_all(send, 'blk', split_axis=0, concat_axis=0, tiled=True)  7.03 us
    pallas_call x1, Pallas kernels, packed_rows(): pl.pallas_call(pack_kernel, grid=(steps,), out_shape=jax.ShapeDtypeStruct...  3.34 us
  transfers between devices with their start and end apart: 14, of which 7 were waited for; matrix products, arithmetic and copies ran while one was open for 27% of the time, Pallas kernels for 9%

profile of v2, /device:TPU:0, one launch (start us, length us, event | category | flops | bytes accessed | tf_op | source)
XLA Modules:
  0.0 87.4 jit_solution(13232927104555582952)
XLA Ops:
  0.5 1.6 %copy-done = bf16[256,4096]{1,0:T(8,128)(2,1)S(1)} copy-done((bf16[256,4096]{1,0:T(8,128)(2,1)S(1)}, bf16[256,4096]{1,0:T(8,128)(2,1)}, u32[]{:S(2)}) %copy-start) | copy-done | bytes 2097176
  2.0 1.6 %copy-done.1 = bf16[256,4096]{1,0:T(8,128)(2,1)S(1)} copy-done((bf16[256,4096]{1,0:T(8,128)(2,1)S(1)}, bf16[256,4096]{1,0:T(8,128)(2,1)}, u32[]{:S(2)}) %copy-start.1) | copy-done | bytes 2097176
  3.6 1.0 %copy-done.2 = bf16[4096,64]{0,1:T(8,128)(2,1)S(1)} copy-done((bf16[4096,64]{0,1:T(8,128)(2,1)S(1)}, bf16[4096,64]{0,1:T(8,128)(2,1)}, u32[]{:S(2)}) %copy-start.2) | copy-done | bytes 524312
  4.7 1.0 %copy-done.3 = bf16[4096,64]{0,1:T(8,128)(2,1)S(1)} copy-done((bf16[4096,64]{0,1:T(8,128)(2,1)S(1)}, bf16[4096,64]{0,1:T(8,128)(2,1)}, u32[]{:S(2)}) %copy-start.3) | copy-done | bytes 524312
  7.1 3.3 %shard_map.73 = bf16[16,80,128]{2,1,0:T(8,128)(2,1)} custom-call(bf16[256,4096]{1,0:T(8,128)(2,1)S(1)} %copy-done, bf16[256,4096]{1,0:T(8,128)(2,1)S(1)} %copy-done.1, bf16[64,4096]{1,0:T(8,128)(2,1)S(1)} %bitcast.48, bf16[64,4096]{1,0:T(8,128)(2,1)S(1)} %bitcast.49, s32[1,256]{1,0:T(1,128)S(1)} %bitcast.50, s32[1,256]{1,0:T(1,128)S(1)} %bitcast.51), custom_call_target="tpu_custom_call" | custom-call | tf_op jit(solution)/shard_map/pallas_call | solution.py:58
  10.4 7.0 %all-to-all-start = ((bf16[16,80,128]{2,1,0:T(8,128)(2,1)}), bf16[16,80,128]{2,1,0:T(8,128)(2,1)S(1)}, u32[]{:S(2)}, u32[]{:S(2)}) async-start(bf16[16,80,128]{2,1,0:T(8,128)(2,1)} %shard_map.73), calls=%async_computation | async-start | bytes 655360 | tf_op jit(solution)/shard_map/all_to_all | solution.py:252
  17.5 11.1 %all-to-all-done.recv_ref = bf16[16,80,128]{2,1,0:T(8,128)(2,1)S(1)} async-done(((bf16[16,80,128]{2,1,0:T(8,128)(2,1)}), bf16[16,80,128]{2,1,0:T(8,128)(2,1)S(1)}, u32[]{:S(2)}, u32[]{:S(2)}) %all-to-all-start) | async-done | bytes 327712 | tf_op jit(solution)/shard_map/all_to_all | solution.py:252
  28.6 4.6 %shard_map.74 = bf16[16,64,64]{2,1,0:T(8,128)(2,1)S(1)} custom-call(bf16[16,80,128]{2,1,0:T(8,128)(2,1)S(1)} %all-to-all-done.recv_ref), custom_call_target="tpu_custom_call" | custom-call | flops 4000000000 | bytes 1048576 | tf_op jit(solution)/shard_map/pallas_call | solution.py:189
  34.2 2.2 %convolution_convert_fusion.18 = bf16[16,256]{1,0:T(8,128)(2,1)S(1)} fusion(bf16[16,4096]{1,0:T(8,128)(2,1)S(1)} %reshape.26, bf16[256,4096]{1,0:T(8,128)(2,1)} %collective-permute-done), kind=kOutput, calls=%fused_computation.26 | convolution fusion | flops 33558528 | bytes 2236416 | tf_op jit(solution)/shard_map/dot_general | solution.py:257
  36.5 1.1 %collective-permute-start.2 = (bf16[32,4096]{1,0:T(8,128)(2,1)S(1)}, bf16[32,4096]{1,0:T(8,128)(2,1)S(1)}, u32[]{:S(2)}, u32[]{:S(2)}) collective-permute-start(bf16[32,4096]{1,0:T(8,128)(2,1)S(1)} %pad_maximum_fusion), channel_id=1, source_target_pairs={{0,4},{1,3},{4,8},{5,1},{8,12},{9,5},{12,14},{13,9},{14,10},{15,13... | collective-permute-start | bytes 786440 | tf_op jit(solution)/shard_map/ppermute | solution.py:270
  37.7 4.6 %shard_map.75 = bf16[16,64,64]{2,1,0:T(8,128)(2,1)S(1)} custom-call(bf16[16,80,128]{2,1,0:T(8,128)(2,1)S(1)} %all-to-all-done.recv_ref), custom_call_target="tpu_custom_call" | custom-call | flops 4000000000 | bytes 1048576 | tf_op jit(solution)/shard_map/pallas_call | solution.py:189
  43.1 2.3 %convolution_convert_fusion.10 = bf16[32,256]{1,0:T(8,128)(2,1)S(1)} fusion(bf16[32,4096]{1,0:T(8,128)(2,1)S(1)} %collective-permute-done.2, bf16[256,4096]{1,0:T(8,128)(2,1)} %collective-permute-done), kind=kOutput, calls=%fused_computation.12 | convolution fusion | flops 67117056 | bytes 2375680 | tf_op jit(solution)/shard_map/dot_general | solution.py:257
  46.8 2.3 %fusion.3 = bf16[128,256]{1,0:T(8,128)(2,1)S(1)} fusion(bf16[16,4096]{1,0:T(8,128)(2,1)S(1)} %reshape.27, bf16[256,4096]{1,0:T(8,128)(2,1)} %collective-permute-done), kind=kOutput, calls=%fused_computation.17 | convolution fusion | flops 33558528 | bytes 2236416 | tf_op jit(solution)/shard_map/dot_general | solution.py:257
  51.1 4.4 %collective-permute-done.6 = bf16[32,4096]{1,0:T(8,128)(2,1)S(1)} collective-permute-done((bf16[32,4096]{1,0:T(8,128)(2,1)S(1)}, bf16[32,4096]{1,0:T(8,128)(2,1)S(1)}, u32[]{:S(2)}, u32[]{:S(2)}) %collective-permute-start.6) | collective-permute-done | bytes 262176 | tf_op jit(solution)/shard_map/ppermute | solution.py:270
  55.5 2.3 %convolution_convert_fusion.8 = bf16[32,256]{1,0:T(8,128)(2,1)S(1)} fusion(bf16[32,4096]{1,0:T(8,128)(2,1)S(1)} %collective-permute-done.6, bf16[256,4096]{1,0:T(8,128)(2,1)} %collective-permute-done), kind=kOutput, calls=%fused_computation.10 | convolution fusion | flops 67117056 | bytes 2375680 | tf_op jit(solution)/shard_map/dot_general | solution.py:257
  59.5 2.3 %convolution_convert_fusion.6 = bf16[32,256]{1,0:T(8,128)(2,1)S(1)} fusion(bf16[32,4096]{1,0:T(8,128)(2,1)S(1)} %collective-permute-done.4, bf16[256,4096]{1,0:T(8,128)(2,1)} %collective-permute-done), kind=kOutput, calls=%fused_computation.8 | convolution fusion | flops 67117056 | bytes 2375680 | tf_op jit(solution)/shard_map/dot_general | solution.py:257
  63.6 1.4 %collective-permute-done.5 = bf16[32,4096]{1,0:T(8,128)(2,1)S(1)} collective-permute-done((bf16[32,4096]{1,0:T(8,128)(2,1)S(1)}, bf16[32,4096]{1,0:T(8,128)(2,1)S(1)}, u32[]{:S(2)}, u32[]{:S(2)}) %collective-permute-start.5) | collective-permute-done | bytes 262176 | tf_op jit(solution)/shard_map/ppermute | solution.py:270
  65.9 2.3 %convolution_convert_fusion.2 = bf16[32,256]{1,0:T(8,128)(2,1)S(1)} fusion(bf16[32,4096]{1,0:T(8,128)(2,1)S(1)} %collective-permute-done.5, bf16[256,4096]{1,0:T(8,128)(2,1)} %collective-permute-done), kind=kOutput, calls=%fused_computation.4 | convolution fusion | flops 67117056 | bytes 2375680 | tf_op jit(solution)/shard_map/dot_general | solution.py:257
  69.0 1.2 %collective-permute-start.9 = (bf16[16,4096]{1,0:T(8,128)(2,1)S(1)}, bf16[16,4096]{1,0:T(8,128)(2,1)S(1)}, u32[]{:S(2)}, u32[]{:S(2)}) collective-permute-start(bf16[16,4096]{1,0:T(8,128)(2,1)S(1)} %slice_select_fusion.1), channel_id=1, source_target_pairs={{0,4},{1,3},{4,8},{5,1},{8,12},{9,5},{12,14},{13,9},{14,10},{15,13... | collective-permute-start | bytes 393224 | tf_op jit(solution)/shard_map/ppermute | solution.py:270
  70.2 2.3 %convolution_convert_fusion.4 = bf16[32,256]{1,0:T(8,128)(2,1)S(1)} fusion(bf16[32,4096]{1,0:T(8,128)(2,1)S(1)} %collective-permute-done.8, bf16[256,4096]{1,0:T(8,128)(2,1)} %collective-permute-done), kind=kOutput, calls=%fused_computation.6 | convolution fusion | flops 67117056 | bytes 2375680 | tf_op jit(solution)/shard_map/dot_general | solution.py:257
  74.2 2.2 %fusion.6 = bf16[128,256]{1,0:T(8,128)(2,1)S(1)} fusion(bf16[128,256]{1,0:T(8,128)(2,1)S(1)} %constant_dynamic-update-slice_fusion.4, bf16[16,4096]{1,0:T(8,128)(2,1)S(1)} %collective-permute-done.9, bf16[256,4096]{1,0:T(8,128)(2,1)} %collective-permute-done), kind=kOutput, calls=%fused_computation.23 | convolution fusion | flops 33558528 | bytes 2236416 | tf_op jit(solution)/shard_map/dot_general | solution.py:257
  78.2 2.3 %fusion = bf16[128,256]{1,0:T(8,128)(2,1)S(1)} fusion(bf16[128,256]{1,0:T(8,128)(2,1)S(1)} %get-tuple-element.58, bf16[32,4096]{1,0:T(8,128)(2,1)S(1)} %collective-permute-done.7, bf16[256,4096]{1,0:T(8,128)(2,1)} %collective-permute-done), kind=kOutput, calls=%fused_computation.1 | convolution fusion | flops 67117056 | bytes 2375680 | tf_op jit(solution)/shard_map/dot_general | solution.py:257
  81.5 2.2 %fusion.2 = bf16[128,256]{1,0:T(8,128)(2,1)S(1)} fusion(bf16[128,256]{1,0:T(8,128)(2,1)S(1)} %fusion, bf16[16,4096]{1,0:T(8,128)(2,1)S(1)} %collective-permute-done.11, bf16[256,4096]{1,0:T(8,128)(2,1)} %collective-permute-done), kind=kOutput, calls=%fused_computation.15 | convolution fusion | flops 33558528 | bytes 2236416 | tf_op jit(solution)/shard_map/dot_general | solution.py:257
  85.6 1.8 %shard_map.76 = bf16[12,32,256]{2,1,0:T(8,128)(2,1)} custom-call(bf16[8,16,256]{2,1,0:T(8,128)(2,1)} %bitcast.53, bf16[8,16,256]{2,1,0:T(8,128)(2,1)} %copy-done.9, bf16[8,16,256]{2,1,0:T(8,128)(2,1)} %bitcast.52, bf16[8,16,256]{2,1,0:T(8,128)(2,1)} %copy-done.10), custom_call_target="tpu_custom_call" | custom-call | tf_op jit(solution)/shard_map/pallas_call | solution.py:299
  (68 shorter events, 18.5 us)
Async XLA Ops:
  0.0 28.6 %collective-permute-start = (bf16[256,4096]{1,0:T(8,128)(2,1)}, bf16[256,4096]{1,0:T(8,128)(2,1)}, u32[]{:S(2)}, u32[]{:S(2)}) collective-permute-start(bf16[256,4096]{1,0:T(8,128)(2,1)} %param.11), channel_id=1, source_target_pairs={{0,1},{1,0},{2,3},{3,2},{4,5},{5,4},{6,7},{7,6},{8,9},{9,8},{10,11... | collective-permute-start | bytes 6291464 | tf_op jit(solution)/shard_map/ppermute | solution.py:251
  0.5 1.6 %copy-start = (bf16[256,4096]{1,0:T(8,128)(2,1)S(1)}, bf16[256,4096]{1,0:T(8,128)(2,1)}, u32[]{:S(2)}) copy-start(bf16[256,4096]{1,0:T(8,128)(2,1)} %inputs_ref.1) | copy-start | bytes 6291460
  2.0 1.6 %copy-start.1 = (bf16[256,4096]{1,0:T(8,128)(2,1)S(1)}, bf16[256,4096]{1,0:T(8,128)(2,1)}, u32[]{:S(2)}) copy-start(bf16[256,4096]{1,0:T(8,128)(2,1)} %grads_ref.1) | copy-start | bytes 6291460
  3.6 1.0 %copy-start.2 = (bf16[4096,64]{0,1:T(8,128)(2,1)S(1)}, bf16[4096,64]{0,1:T(8,128)(2,1)}, u32[]{:S(2)}) copy-start(bf16[4096,64]{0,1:T(8,128)(2,1)} %param.9) | copy-start | bytes 1572868
  4.7 1.0 %copy-start.3 = (bf16[4096,64]{0,1:T(8,128)(2,1)S(1)}, bf16[4096,64]{0,1:T(8,128)(2,1)}, u32[]{:S(2)}) copy-start(bf16[4096,64]{0,1:T(8,128)(2,1)} %param.10) | copy-start | bytes 1572868
  5.7 0.7 copy-start.4
  6.4 0.7 copy-start.5
  10.4 18.1 %all-to-all-start = ((bf16[16,80,128]{2,1,0:T(8,128)(2,1)}), bf16[16,80,128]{2,1,0:T(8,128)(2,1)S(1)}, u32[]{:S(2)}, u32[]{:S(2)}) async-start(bf16[16,80,128]{2,1,0:T(8,128)(2,1)} %shard_map.73), calls=%async_computation | async-start | bytes 655360 | tf_op jit(solution)/shard_map/all_to_all | solution.py:252
  17.5 16.0 %copy-start.6 = (bf16[256,4096]{1,0:T(8,128)(2,1)S(1)}, bf16[256,4096]{1,0:T(8,128)(2,1)}, u32[]{:S(2)}) copy-start(bf16[256,4096]{1,0:T(8,128)(2,1)} %param.11) | copy-start | bytes 6291460
  34.1 2.4 %collective-permute-start.1 = (bf16[16,4096]{1,0:T(8,128)(2,1)S(1)}, bf16[16,4096]{1,0:T(8,128)(2,1)S(1)}, u32[]{:S(2)}, u32[]{:S(2)}) collective-permute-start(bf16[16,4096]{1,0:T(8,128)(2,1)S(1)} %reshape.26), channel_id=1, source_target_pairs={{0,1},{1,0},{2,3},{3,2},{4,5},{5,4},{6,7},{7,6},{8,9},{9,8},{10,11... | collective-permute-start | bytes 393224 | tf_op jit(solution)/shard_map/ppermute | solution.py:262
  36.5 6.6 %collective-permute-start.2 = (bf16[32,4096]{1,0:T(8,128)(2,1)S(1)}, bf16[32,4096]{1,0:T(8,128)(2,1)S(1)}, u32[]{:S(2)}, u32[]{:S(2)}) collective-permute-start(bf16[32,4096]{1,0:T(8,128)(2,1)S(1)} %pad_maximum_fusion), channel_id=1, source_target_pairs={{0,4},{1,3},{4,8},{5,1},{8,12},{9,5},{12,14},{13,9},{14,10},{15,13... | collective-permute-start | bytes 786440 | tf_op jit(solution)/shard_map/ppermute | solution.py:270
  46.8 3.2 %collective-permute-start.3 = (bf16[16,4096]{1,0:T(8,128)(2,1)S(1)}, bf16[16,4096]{1,0:T(8,128)(2,1)S(1)}, u32[]{:S(2)}, u32[]{:S(2)}) collective-permute-start(bf16[16,4096]{1,0:T(8,128)(2,1)S(1)} %reshape.27), channel_id=1, source_target_pairs={{0,1},{1,0},{2,3},{3,2},{4,5},{5,4},{6,7},{7,6},{8,9},{9,8},{10,11... | collective-permute-start | bytes 393224 | tf_op jit(solution)/shard_map/ppermute | solution.py:262
  49.1 6.4 %collective-permute-start.6 = (bf16[32,4096]{1,0:T(8,128)(2,1)S(1)}, bf16[32,4096]{1,0:T(8,128)(2,1)S(1)}, u32[]{:S(2)}, u32[]{:S(2)}) collective-permute-start(bf16[32,4096]{1,0:T(8,128)(2,1)S(1)} %collective-permute-done.2), channel_id=1, source_target_pairs={{0,4},{1,3},{4,8},{5,1},{8,12},{9,5},{12,14},{13,9},{14,10},{15,13... | collective-permute-start | bytes 786440 | tf_op jit(solution)/shard_map/ppermute | solution.py:270
  50.1 8.5 %collective-permute-start.4 = (bf16[32,4096]{1,0:T(8,128)(2,1)S(1)}, bf16[32,4096]{1,0:T(8,128)(2,1)S(1)}, u32[]{:S(2)}, u32[]{:S(2)}) collective-permute-start(bf16[32,4096]{1,0:T(8,128)(2,1)S(1)} %pad_maximum_fusion.1), channel_id=1, source_target_pairs={{0,4},{1,3},{4,8},{5,1},{8,12},{9,5},{12,14},{13,9},{14,10},{15,13... | collective-permute-start | bytes 786440 | tf_op jit(solution)/shard_map/ppermute | solution.py:270
  58.6 6.4 %collective-permute-start.5 = (bf16[32,4096]{1,0:T(8,128)(2,1)S(1)}, bf16[32,4096]{1,0:T(8,128)(2,1)S(1)}, u32[]{:S(2)}, u32[]{:S(2)}) collective-permute-start(bf16[32,4096]{1,0:T(8,128)(2,1)S(1)} %collective-permute-done.4), channel_id=1, source_target_pairs={{0,4},{1,3},{4,8},{5,1},{8,12},{9,5},{12,14},{13,9},{14,10},{15,13... | collective-permute-start | bytes 786440 | tf_op jit(solution)/shard_map/ppermute | solution.py:270
  62.6 6.4 %collective-permute-start.8 = (bf16[32,4096]{1,0:T(8,128)(2,1)S(1)}, bf16[32,4096]{1,0:T(8,128)(2,1)S(1)}, u32[]{:S(2)}, u32[]{:S(2)}) collective-permute-start(bf16[32,4096]{1,0:T(8,128)(2,1)S(1)} %collective-permute-done.6), channel_id=1, source_target_pairs={{0,4},{1,3},{4,8},{5,1},{8,12},{9,5},{12,14},{13,9},{14,10},{15,13... | collective-permute-start | bytes 786440 | tf_op jit(solution)/shard_map/ppermute | solution.py:270
  65.0 8.3 %collective-permute-start.7 = (bf16[32,4096]{1,0:T(8,128)(2,1)S(1)}, bf16[32,4096]{1,0:T(8,128)(2,1)S(1)}, u32[]{:S(2)}, u32[]{:S(2)}) collective-permute-start(bf16[32,4096]{1,0:T(8,128)(2,1)S(1)} %collective-permute-done.5), channel_id=1, source_target_pairs={{0,4},{1,3},{4,8},{5,1},{8,12},{9,5},{12,14},{13,9},{14,10},{15,13... | collective-permute-start | bytes 786440 | tf_op jit(solution)/shard_map/ppermute | solution.py:270
  69.0 5.2 %collective-permute-start.9 = (bf16[16,4096]{1,0:T(8,128)(2,1)S(1)}, bf16[16,4096]{1,0:T(8,128)(2,1)S(1)}, u32[]{:S(2)}, u32[]{:S(2)}) collective-permute-start(bf16[16,4096]{1,0:T(8,128)(2,1)S(1)} %slice_select_fusion.1), channel_id=1, source_target_pairs={{0,4},{1,3},{4,8},{5,1},{8,12},{9,5},{12,14},{13,9},{14,10},{15,13... | collective-permute-start | bytes 393224 | tf_op jit(solution)/shard_map/ppermute | solution.py:270
  76.5 8.0 %collective-permute-start.10 = (bf16[8,16,256]{2,1,0:T(8,128)(2,1)S(1)}, bf16[8,16,256]{2,1,0:T(8,128)(2,1)S(1)}, u32[]{:S(2)}, u32[]{:S(2)}) collective-permute-start(bf16[8,16,256]{2,1,0:T(8,128)(2,1)S(1)} %bitcast.55), channel_id=1, source_target_pairs={{0,1},{1,0},{2,3},{3,2},{4,5},{5,4},{6,7},{7,6},{8,9},{9,8},{10,11... | collective-permute-start | bytes 196616 | tf_op jit(solution)/shard_map/ppermute | solution.py:298
  76.5 5.0 %collective-permute-start.11 = (bf16[16,4096]{1,0:T(8,128)(2,1)S(1)}, bf16[16,4096]{1,0:T(8,128)(2,1)S(1)}, u32[]{:S(2)}, u32[]{:S(2)}) collective-permute-start(bf16[16,4096]{1,0:T(8,128)(2,1)S(1)} %slice_select_fusion), channel_id=1, source_target_pairs={{0,4},{1,3},{4,8},{5,1},{8,12},{9,5},{12,14},{13,9},{14,10},{15,13... | collective-permute-start | bytes 393224 | tf_op jit(solution)/shard_map/ppermute | solution.py:270
  81.2 3.3 %copy-start.8 = (bf16[128,256]{1,0:T(8,128)(2,1)}, bf16[128,256]{1,0:T(8,128)(2,1)S(1)}, u32[]{:S(2)}) copy-start(bf16[128,256]{1,0:T(8,128)(2,1)S(1)} %fusion.7) | copy-start | bytes 196612
  83.7 1.3 %collective-permute-start.12 = (bf16[8,16,256]{2,1,0:T(8,128)(2,1)S(1)}, bf16[8,16,256]{2,1,0:T(8,128)(2,1)S(1)}, u32[]{:S(2)}, u32[]{:S(2)}) collective-permute-start(bf16[8,16,256]{2,1,0:T(8,128)(2,1)S(1)} %bitcast.54), channel_id=1, source_target_pairs={{0,1},{1,0},{2,3},{3,2},{4,5},{5,4},{6,7},{7,6},{8,9},{9,8},{10,11... | collective-permute-start | bytes 196616 | tf_op jit(solution)/shard_map/ppermute | solution.py:298
  84.5 0.6 copy-start.7
  84.5 0.6 copy-start.9
  (1 other events, 0.6 us)

commit v3 on v2

--- a/solution.py
+++ b/solution.py
@@ -17,59 +17,77 @@
 LAST_DIMS = (((1,), (1,)), ((), ()))
 
 
-def pack_kernel(inputs_ref, grads_ref, pin_ref, pout_ref, owner_ref, slot_ref, send_ref, ilow_ref, glow_ref):
-    step = pl.program_id(0)
-
-    @pl.when(step == 0)
-    def _():
-        ilow_ref[...] = jnp.zeros_like(ilow_ref)
-        glow_ref[...] = jnp.zeros_like(glow_ref)
-
-    ilow_ref[...] += lax.dot_general(inputs_ref[...], pin_ref[...], LAST_DIMS, preferred_element_type=F32)
-    glow_ref[...] += lax.dot_general(grads_ref[...], pout_ref[...], LAST_DIMS, preferred_element_type=F32)
-
-    @pl.when(step == pl.num_programs(0) - 1)
-    def _():
-        owners, per, wide = send_ref.shape
-        cap = per - TAIL
-        toks = slot_ref.shape[1]
-        low = jnp.concatenate([glow_ref[...], ilow_ref[...]], axis=1).astype(BF16)
-        owner = owner_ref[...]
-        hot = (owner == lax.broadcasted_iota(jnp.int32, (owners, toks), 0)).astype(F32)
-        earlier = lax.broadcasted_iota(jnp.int32, (toks, toks), 0) < lax.broadcasted_iota(jnp.int32, (toks, toks), 1)
-        before = jnp.dot(hot.astype(BF16), earlier.astype(F32).astype(BF16), preferred_element_type=F32)
-        rank = jnp.sum(before * hot, axis=0, keepdims=True).astype(jnp.int32)
-        position = owner * cap + rank
-        placed = lax.broadcasted_iota(jnp.int32, (owners * cap, toks), 0) == position
-        rows = jnp.dot(placed.astype(F32).astype(BF16), low, preferred_element_type=F32).astype(BF16)
-        named = (hot * (slot_ref[...].astype(F32) + 1.0)).astype(BF16)
-        at_lane = lax.broadcasted_iota(jnp.int32, (wide, toks), 0) % cap == rank
-        slots = lax.dot_general(named, at_lane.astype(F32).astype(BF16), LAST_DIMS, preferred_element_type=F32)
-        for o in range(owners):
-            send_ref[o, :cap, :] = rows[o * cap : (o + 1) * cap]
-            send_ref[o, cap:, :] = jnp.broadcast_to(slots[o : o + 1], (TAIL, wide)).astype(BF16)
+def pack_kernel(
+    inputs_hbm, grads_hbm, pin_hbm, pout_hbm, owner_hbm, slot_hbm, send_ref, inputs_ref, grads_ref, pin_ref, pout_ref, owner_ref, slot_ref, sems
+):
+    owners, per, wide = send_ref.shape
+    cap = per - TAIL
+    toks, width = inputs_ref.shape
+    low = pin_ref.shape[0]
+    parts = sems.shape[1] - 1
+    part = width // parts
+    small = [
+        pltpu.make_async_copy(owner_hbm, owner_ref, sems.at[0, parts]),
+        pltpu.make_async_copy(slot_hbm, slot_ref, sems.at[1, parts]),
+    ]
+    large = []
+    for i in range(parts):
+        at = pl.ds(i * part, part)
+        for j, (source, target) in enumerate(
+            ((pin_hbm, pin_ref), (inputs_hbm, inputs_ref), (pout_hbm, pout_ref), (grads_hbm, grads_ref))
+        ):
+            large.append(pltpu.make_async_copy(source.at[:, at], target.at[:, at], sems.at[j, i]))
+    for copy in small + large:
+        copy.start()
+
+    for copy in small:
+        copy.wait()
+    owner = owner_ref[...]
+    hot = (owner == lax.broadcasted_iota(jnp.int32, (owners, toks), 0)).astype(F32)
+    earlier = lax.broadcasted_iota(jnp.int32, (toks, toks), 0) < lax.broadcasted_iota(jnp.int32, (toks, toks), 1)
+    before = jnp.dot(hot.astype(BF16), earlier.astype(F32).astype(BF16), preferred_element_type=F32)
+    rank = jnp.sum(before * hot, axis=0, keepdims=True).astype(jnp.int32)
+    position = owner * cap + rank
+    placed = lax.broadcasted_iota(jnp.int32, (owners * cap, toks), 0) == position
+    placed = placed.astype(F32).astype(BF16)
+    named = (hot * (slot_ref[...].astype(F32) + 1.0)).astype(BF16)
+    at_lane = lax.broadcasted_iota(jnp.int32, (wide, toks), 0) % cap == rank
+    slots = lax.dot_general(named, at_lane.astype(F32).astype(BF16), LAST_DIMS, preferred_element_type=F32)
+    for o in range(owners):
+        send_ref[o, cap:, :] = jnp.broadcast_to(slots[o : o + 1], (TAIL, wide)).astype(BF16)
+
+    inputs_low = jnp.zeros((toks, low), F32)
+    grads_low = jnp.zeros((toks, low), F32)
+    for i in range(parts):
+        at = slice(i * part, (i + 1) * part)
+        for copy in large[4 * i : 4 * i + 4]:
+            copy.wait()
+        inputs_low += lax.dot_general(inputs_ref[:, at], pin_ref[:, at], LAST_DIMS, preferred_element_type=F32)
+        grads_low += lax.dot_general(grads_ref[:, at], pout_ref[:, at], LAST_DIMS, preferred_element_type=F32)
+    both = jnp.concatenate([grads_low, inputs_low], axis=1).astype(BF16)
+    rows = jnp.dot(placed, both, preferred_element_type=F32).astype(BF16)
+    for o in range(owners):
+        send_ref[o, :cap, :] = rows[o * cap : (o + 1) * cap]
 
 
 def packed_rows(query_inputs, query_grads, proj_in, proj_out, token_owner, token_slot, owners, cap):
     toks, width = query_inputs.shape
     low = proj_in.shape[1]
-    steps = 4
-    part = width // steps
     return pl.pallas_call(
         pack_kernel,
-        grid=(steps,),
         out_shape=jax.ShapeDtypeStruct((owners, cap + TAIL, 2 * low), BF16),
-        in_specs=[
-            pl.BlockSpec((toks, part), lambda i: (0, i)),
-            pl.BlockSpec((toks, part), lambda i: (0, i)),
-            pl.BlockSpec((low, part), lambda i: (0, i)),
-            pl.BlockSpec((low, part), lambda i: (0, i)),
-            pl.BlockSpec((1, toks), lambda i: (0, 0)),
-            pl.BlockSpec((1, toks), lambda i: (0, 0)),
+        in_specs=[pl.BlockSpec(memory_space=pltpu.HBM)] * 6,
+        out_specs=pl.BlockSpec(memory_space=pltpu.VMEM),
+        scratch_shapes=[
+            pltpu.VMEM((toks, width), BF16),
+            pltpu.VMEM((toks, width), BF16),
+            pltpu.VMEM((low, width), BF16),
+            pltpu.VMEM((low, width), BF16),
+            pltpu.VMEM((1, toks), jnp.int32),
+            pltpu.VMEM((1, toks), jnp.int32),
+            pltpu.SemaphoreType.DMA((4, 5)),
         ],
-        out_specs=pl.BlockSpec((owners, cap + TAIL, 2 * low), lambda i: (0, 0, 0)),
-        scratch_shapes=[pltpu.VMEM((toks, low), F32), pltpu.VMEM((toks, low), F32)],
-        compiler_params=pltpu.CompilerParams(vmem_limit_bytes=40 * 2**20),
+        compiler_params=pltpu.CompilerParams(vmem_limit_bytes=60 * 2**20),
     )(query_inputs, query_grads, proj_in.T, proj_out.T, token_owner.reshape(1, toks), token_slot.reshape(1, toks))
 
 
@@ -197,33 +215,83 @@
             pltpu.VMEM((docs, wide), F32),
         ],
         cost_estimate=pl.CostEstimate(flops=4 * 10**9, bytes_accessed=2**20, transcendentals=0),
-        compiler_params=pltpu.CompilerParams(vmem_limit_bytes=40 * 2**20),
+        compiler_params=pltpu.CompilerParams(vmem_limit_bytes=16 * 2**20),
     )(recv)
     return found.reshape(docs, low * low)
 
 
-def order_kernel(owners, *refs):
-    chunks = (len(refs) - 1) // 2
-    out_ref = refs[-1]
-    docs = refs[0].shape[1]
+def score_kernel(*refs):
+    own_rows, other_rows, own_ref, other_ref = refs[-4:]
+    blocks = jnp.concatenate([ref[...] for ref in refs[:-4]], axis=0)
+    own_ref[...] = lax.dot_general(blocks, own_rows[...], LAST_DIMS, preferred_element_type=F32).astype(BF16)
+    other_ref[...] = lax.dot_general(blocks, other_rows[...], LAST_DIMS, preferred_element_type=F32).astype(BF16)
+
+
+def scores_of(blocks, own_rows, other_rows):
+    count = sum(block.shape[0] for block in blocks)
+    shape = jax.ShapeDtypeStruct((count, own_rows.shape[0]), BF16)
+    return pl.pallas_call(
+        score_kernel,
+        out_shape=(shape, shape),
+        in_specs=[pl.BlockSpec(memory_space=pltpu.VMEM)] * (len(blocks) + 2),
+        out_specs=(pl.BlockSpec(memory_space=pltpu.VMEM),) * 2,
+        cost_estimate=pl.CostEstimate(flops=1, bytes_accessed=1, transcendentals=0),
+        compiler_params=pltpu.CompilerParams(vmem_limit_bytes=16 * 2**20),
+    )(*blocks, own_rows, other_rows)
+
+
+def order_kernel(owners, docs, places, *refs):
+    out_ref, sems = refs[-2:]
     chips = owners // 2
     device = lax.axis_index("blk")
-
-    def spot(chip):
-        line, row = lax.div(chip, 2), lax.rem(chip, 2)
-        return jnp.where(row == 0, line, chips - 1 - line)
-
-    here, core = spot(lax.div(device, 2)), lax.rem(device, 2)
-    for k in range(out_ref.shape[0]):
-        owner = lax.rem(device + LEAD - k + owners, owners)
-        second = lax.rem(owner, 2)
-        hops = lax.rem(here - spot(lax.div(owner, 2)) + chips, chips)
-        by_core = jnp.where((hops == 0) | (hops == chips // 2), second, jnp.where(hops < chips // 2, 0, 1))
-        away = jnp.where(hops > chips // 2, chips - hops, hops)
-        index = jnp.where(away == 0, 0, jnp.where(away == chips // 2, chips - 1, 2 * away - 1 + second))
-        own = by_core == core
-        for c in range(chunks):
-            out_ref[k, c * docs : (c + 1) * docs, :] = jnp.where(own, refs[2 * c][index], refs[2 * c + 1][index])
+    chip, core = lax.div(device, 2), lax.rem(device, 2)
+    spot = jnp.where(lax.rem(chip, 2) == 0, lax.div(chip, 2), chips - 1 - lax.div(chip, 2))
+    copies = []
+    for ref, (own, listed) in zip(refs, places):
+        scorer = core if own else 1 - core
+        for number, (chunk, hop, second) in enumerate(listed):
+            there = lax.rem(spot + jnp.where(scorer == 0, chips - hop, hop), chips)
+            where = jnp.where(there < chips // 2, 2 * there, 2 * (chips - 1 - there) + 1)
+            owner = 2 * where + (scorer if hop in (0, chips // 2) else second)
+            stop = lax.rem(device + LEAD - owner + owners, owners)
+            wanted = stop < out_ref.shape[0]
+            copy = pltpu.make_async_copy(
+                ref.at[pl.ds(number * docs, docs), :],
+                out_ref.at[jnp.minimum(stop, out_ref.shape[0] - 1), pl.ds(chunk * docs, docs), :],
+                sems.at[len(copies)],
+            )
+            copies.append((wanted, copy))
+            pl.when(wanted)(copy.start)
+    for wanted, copy in copies:
+        pl.when(wanted)(copy.wait)
+
+
+def put_in_order(tiles, owners, docs, placed):
+    refs = [ref for ref, _, _ in tiles]
+    places = [(own, listing) for _, own, listing in tiles]
+    shape = jax.ShapeDtypeStruct((STOPS, DOC_DEV, refs[0].shape[1]), BF16)
+    kernel = functools.partial(order_kernel, owners, docs, places)
+    aliases = {}
+    if placed is not None:
+        aliases = {len(refs): 0}
+        refs = refs + [placed]
+    specs = [pl.BlockSpec(memory_space=pltpu.VMEM)] * len(tiles) + [pl.BlockSpec(memory_space=pltpu.HBM)] * len(aliases)
+    if aliases:
+        inner = kernel
+
+        def kernel(*args):
+            inner(*args[: len(tiles)], *args[len(tiles) + 1 :])
+
+    return pl.pallas_call(
+        kernel,
+        out_shape=shape,
+        in_specs=specs,
+        out_specs=pl.BlockSpec(memory_space=pltpu.HBM),
+        input_output_aliases=aliases,
+        scratch_shapes=[pltpu.SemaphoreType.DMA((sum(len(listing) for _, _, listing in tiles),))],
+        cost_estimate=pl.CostEstimate(flops=1, bytes_accessed=1, transcendentals=0),
+        compiler_params=pltpu.CompilerParams(vmem_limit_bytes=4 * 2**20),
+    )(*refs)
 
 
 def ring_pairs(owners):
@@ -241,9 +309,10 @@
     toks = query_inputs.shape[0]
     low = proj_in.shape[1]
     owners = lax.axis_size("blk")
-    chips = owners // 2
+    hops = owners // 4
     train = train_rows.shape[0]
     cap = 4 * toks // owners
+    docs = DOC_DEV // 2
     ring, swap = ring_pairs(owners)
     odd = lax.rem(lax.axis_index("blk"), 2) == 1
 
@@ -252,56 +321,46 @@
     recv = lax.all_to_all(send, "blk", split_axis=0, concat_axis=0, tiled=True)
     recv, other_rows = lax.optimization_barrier((recv, other_rows))
 
-    def scoring(block):
-        return tuple(
-            lax.dot_general(block, rows, LAST_DIMS, preferred_element_type=F32).astype(BF16)
-            for rows in (train_rows, other_rows)
-        )
-
     def pair_up(mine):
         theirs = lax.ppermute(mine, "blk", swap)
         return jnp.concatenate([jnp.where(odd, theirs, mine), jnp.where(odd, mine, theirs)], axis=0)
 
-    chunks = 2
-    docs = DOC_DEV // chunks
     def onward(block, hop):
-        if hop == chips // 2:
+        if hop == hops:
             block = jnp.where(odd, block[docs:], block[:docs])
         return lax.ppermute(block, "blk", ring)
 
-    moving, tiles, came = [], [], []
-    for c in range(chunks):
-        mine = queries_of(recv, c * docs, docs, low)
-        if c > 0:
-            moving[c - 1] = onward(moving[c - 1], 1)
-            mine, moving[c - 1] = lax.optimization_barrier((mine, moving[c - 1]))
-            came.append(scoring(moving[c - 1]))
-        tiles.append([scoring(mine)])
-        moving.append(pair_up(mine))
-        if c + 1 < chunks:
-            recv, moving[c], tiles[c][0] = lax.optimization_barrier((recv, moving[c], tiles[c][0]))
-    for hop in range(1, chips // 2 + 1):
-        for c in range(chunks):
-            if hop == 1 and c + 1 < chunks:
-                continue
-            block = moving[c]
-            behind = len(came) - chunks - 1
-            if behind >= 0:
-                block, came[behind] = lax.optimization_barrier((block, came[behind]))
-            moving[c] = onward(block, hop)
-            came.append(scoring(moving[c]))
-    for number, tile in enumerate(came):
-        tiles[number % chunks].append(tile)
-    results = []
-    for c in range(chunks):
-        own, other = (jnp.concatenate(part, axis=0).reshape(chips, docs, train) for part in zip(*tiles[c]))
-        results += [own, lax.ppermute(other, "blk", swap)]
-    return pl.pallas_call(
-        functools.partial(order_kernel, owners),
-        out_shape=jax.ShapeDtypeStruct((STOPS, DOC_DEV, train), BF16),
-        in_specs=[pl.BlockSpec(memory_space=pltpu.VMEM)] * (2 * chunks),
-        out_specs=pl.BlockSpec(memory_space=pltpu.VMEM),
-    )(*results)
+    def listed(chunk, hop):
+        return [(chunk, hop, second) for second in ((0,) if hop in (0, hops) else (0, 1))]
+
+    first_own = queries_of(recv, 0, docs, low)
+    first = pair_up(first_own)
+    recv, first = lax.optimization_barrier((recv, first))
+    last_own = queries_of(recv, docs, docs, low)
+    first = onward(first, 1)
+    last_own, first = lax.optimization_barrier((last_own, first))
+    last = pair_up(last_own)
+    waiting = [first_own, last_own, first]
+    lists = listed(0, 0) + listed(1, 0) + listed(0, 1)
+    scored, places = [], []
+    for hop in range(1, hops + 1):
+        ahead = onward(first, hop + 1) if hop < hops else None
+        came = onward(last, hop)
+        scored.append(scores_of(waiting, train_rows, other_rows))
+        places.append(lists)
+        if hop < hops - 1:
+            ahead, scored[-1] = lax.optimization_barrier((ahead, scored[-1]))
+        elif hop == hops - 1:
+            came, scored[-1] = lax.optimization_barrier((came, scored[-1]))
+        waiting = [came] if ahead is None else [ahead, came]
+        lists = ([] if ahead is None else listed(0, hop + 1)) + listed(1, hop)
+        first, last = ahead, came
+    early = lax.ppermute(jnp.concatenate([other for _, other in scored], axis=0), "blk", swap)
+    final = scores_of(waiting, train_rows, other_rows)
+    late = lax.ppermute(final[1], "blk", swap)
+    most = [(own, True, listing) for (own, _), listing in zip(scored, places)] + [(early, False, sum(places, []))]
+    placed = put_in_order(most, owners, docs, None)
+    return put_in_order([(final[0], True, lists), (late, False, lists)], owners, docs, placed)
 
 
 def passed_along(value, axis, steps):

time: 88.1 us -> 67.3 us (0.76)
  matrix products: 29.9 us -> 0 us
  blocking collectives: 0 us -> 18.2 us
  starting transfers between devices: 15.9 us -> 7.06 us
  Pallas kernels: 14.3 us -> 21.8 us
  local copies, waits for them, and re-layouts: 7.81 us -> 3.47 us
  waiting for transfers between devices: 19.2 us -> 16.2 us
    dot_general x20 -> x0, matrix products: 29.9 us -> none  [scoring(): lax.dot_general(block, rows, LAST_DIMS, preferred_element_type=F32)]
    all_to_all x0 -> x1, blocking collectives: none -> 18.2 us  [gathered(): recv = lax.all_to_all(send, 'blk', split_axis=0, concat_axis=0, tiled=True)]
    all_to_all x1 -> x0, waiting for transfers between devices: 11.1 us -> none  [gathered(): recv = lax.all_to_all(send, 'blk', split_axis=0, concat_axis=0, tiled=True)]
    pallas_call x2 -> x8, Pallas kernels: 5.1 us -> 12.6 us  [the longest x5 6.68 us: scores_of(): pl.pallas_call(score_kernel, out_shape=(shape, shape), in_specs=[pl.Block...]
    all_to_all x1 -> x0, starting transfers between devices: 7.03 us -> none  [gathered(): recv = lax.all_to_all(send, 'blk', split_axis=0, concat_axis=0, tiled=True)]
    ppermute x8, waiting for transfers between devices: 7.62 us -> 14.2 us  [onward(): return lax.ppermute(block, 'blk', ring)]
    unnamed x32 -> x8, local copies, waits for them, and re-layouts: 7.27 us -> 2.92 us
    ppermute x2, waiting for transfers between devices: 0.01 us -> 1.91 us  [pair_up(): theirs = lax.ppermute(mine, 'blk', swap)]
  transfers between devices with their start and end apart: 14 -> 13, of which waited for: 7 -> 11; matrix products, arithmetic and copies ran while one was open for 27% -> 1% of each run, Pallas kernels for 9% -> 25%
where the time goes in v3:
time: 67.3 us; the launch traced here: 67.1 us
  Pallas kernels  21.8 us (32%)
  blocking collectives  18.2 us (27%)
  waiting for transfers between devices  16.2 us (24%)
  starting transfers between devices  7.06 us (10%)
  local copies, waits for them, and re-layouts  3.47 us (5%)
    all_to_all x1, blocking collectives, gathered(): recv = lax.all_to_all(send, 'blk', split_axis=0, concat_axis=0, tiled=True)  18.2 us
    ppermute x8, waiting for transfers between devices, onward(): return lax.ppermute(block, 'blk', ring)  14.2 us
    pallas_call x2, Pallas kernels, queries_of(): pl.pallas_call(functools.partial(query_kernel, first_doc), out_shape=jax....  9.16 us
    pallas_call x5, Pallas kernels, scores_of(): pl.pallas_call(score_kernel, out_shape=(shape, shape), in_specs=[pl.Block...  6.68 us
    ppermute x8, starting transfers between devices, onward(): return lax.ppermute(block, 'blk', ring)  6.35 us
    pallas_call x1, Pallas kernels, packed_rows(): pl.pallas_call(pack_kernel, out_shape=jax.ShapeDtypeStruct((owners, cap +...  4.27 us
    unnamed x8, local copies, waits for them, and re-layouts  2.92 us
    ppermute x2, waiting for transfers between devices, pair_up(): theirs = lax.ppermute(mine, 'blk', swap)  1.91 us
  transfers between devices with their start and end apart: 13, of which 11 were waited for; matrix products, arithmetic and copies ran while one was open for 1% of the time, Pallas kernels for 25%

profile of v3, /device:TPU:0, one launch (start us, length us, event | category | flops | bytes accessed | tf_op | source)
XLA Modules:
  0.0 67.1 jit_solution(3528113824101262992)
XLA Ops:
  0.5 4.3 %shard_map.73 = bf16[16,80,128]{2,1,0:T(8,128)(2,1)} custom-call(bf16[256,4096]{1,0:T(8,128)(2,1)} %inputs_hbm.1, bf16[256,4096]{1,0:T(8,128)(2,1)} %grads_hbm.1, bf16[64,4096]{1,0:T(8,128)(2,1)} %bitcast.4, bf16[64,4096]{1,0:T(8,128)(2,1)} %bitcast.5, s32[1,256]{1,0:T(1,128)} %bitcast.6, s32[1,256]{1,0:T(1,128)} %bitcast.7), custom_call_target="tpu_custom_call" | custom-call | tf_op jit(solution)/shard_map/pallas_call | solution.py:76
  4.7 18.2 %all_to_all.5.recv_ref = bf16[16,80,128]{2,1,0:T(8,128)(2,1)S(1)} all-to-all(bf16[16,80,128]{2,1,0:T(8,128)(2,1)} %shard_map.73), channel_id=1, replica_groups=mesh['groups'=2,'blk'=16] {'blk'}, dimensions={0} | all-to-all | bytes 655360 | tf_op jit(solution)/shard_map/all_to_all | solution.py:321
  22.9 1.3 %copy-done.1 = bf16[256,4096]{1,0:T(8,128)(2,1)} copy-done((bf16[256,4096]{1,0:T(8,128)(2,1)}, bf16[256,4096]{1,0:T(8,128)(2,1)S(1)}, u32[]{:S(2)}) %copy-start.1) | copy-done | bytes 2097176
  24.2 4.6 %shard_map.74 = bf16[16,64,64]{2,1,0:T(8,128)(2,1)S(1)} custom-call(bf16[16,80,128]{2,1,0:T(8,128)(2,1)S(1)} %all_to_all.5.recv_ref), custom_call_target="tpu_custom_call" | custom-call | flops 4000000000 | bytes 1048576 | tf_op jit(solution)/shard_map/pallas_call | solution.py:207
  29.3 1.2 %collective-permute-done.1 = bf16[16,4096]{1,0:T(8,128)(2,1)S(1)} collective-permute-done((bf16[16,4096]{1,0:T(8,128)(2,1)S(1)}, bf16[16,4096]{1,0:T(8,128)(2,1)S(1)}, u32[]{:S(2)}, u32[]{:S(2)}) %collective-permute-start.1) | collective-permute-done | bytes 131104 | tf_op jit(solution)/shard_map/ppermute | solution.py:325
  30.5 0.7 %collective-permute-start.2 = (bf16[32,4096]{1,0:T(8,128)(2,1)S(1)}, bf16[32,4096]{1,0:T(8,128)(2,1)S(1)}, u32[]{:S(2)}, u32[]{:S(2)}) collective-permute-start(bf16[32,4096]{1,0:T(8,128)(2,1)S(1)} %pad_maximum_fusion), channel_id=1, source_target_pairs={{0,4},{1,3},{4,8},{5,1},{8,12},{9,5},{12,14},{13,9},{14,10},{15,13... | collective-permute-start | bytes 786440 | tf_op jit(solution)/shard_map/ppermute | solution.py:331
  31.3 4.6 %shard_map.75 = bf16[16,64,64]{2,1,0:T(8,128)(2,1)S(1)} custom-call(bf16[16,80,128]{2,1,0:T(8,128)(2,1)S(1)} %all_to_all.5.recv_ref), custom_call_target="tpu_custom_call" | custom-call | flops 4000000000 | bytes 1048576 | tf_op jit(solution)/shard_map/pallas_call | solution.py:207
  36.1 0.8 %collective-permute-done.2.refs_2_ = bf16[32,4096]{1,0:T(8,128)(2,1)S(1)} collective-permute-done((bf16[32,4096]{1,0:T(8,128)(2,1)S(1)}, bf16[32,4096]{1,0:T(8,128)(2,1)S(1)}, u32[]{:S(2)}, u32[]{:S(2)}) %collective-permute-start.2) | collective-permute-done | bytes 262176 | tf_op jit(solution)/shard_map/ppermute | solution.py:331
  38.4 0.9 %collective-permute-start.4 = (bf16[32,4096]{1,0:T(8,128)(2,1)S(1)}, bf16[32,4096]{1,0:T(8,128)(2,1)S(1)}, u32[]{:S(2)}, u32[]{:S(2)}) collective-permute-start(bf16[32,4096]{1,0:T(8,128)(2,1)S(1)} %pad_maximum_fusion.1), channel_id=1, source_target_pairs={{0,4},{1,3},{4,8},{5,1},{8,12},{9,5},{12,14},{13,9},{14,10},{15,13... | collective-permute-start | bytes 786440 | tf_op jit(solution)/shard_map/ppermute | solution.py:331
  39.3 1.6 %copy-done.2 = bf16[256,4096]{1,0:T(8,128)(2,1)S(1)} copy-done((bf16[256,4096]{1,0:T(8,128)(2,1)S(1)}, bf16[256,4096]{1,0:T(8,128)(2,1)}, u32[]{:S(2)}) %copy-start.2) | copy-done | bytes 2097176
  40.9 1.4 %shard_map.76 = (bf16[64,256]{1,0:T(8,128)(2,1)S(1)}, bf16[64,256]{1,0:T(8,128)(2,1)S(1)}) custom-call(bf16[16,4096]{1,0:T(8,128)(2,1)S(1)} %reshape.14.refs_0_, bf16[16,4096]{1,0:T(8,128)(2,1)S(1)} %reshape.15.refs_1_, bf16[32,4096]{1,0:T(8,128)(2,1)S(1)} %collective-permute-done.2.refs_2_, bf16[256,4096]{1,0:T(8,128)(2,1)S(1)} %copy-done, ...), custom_call_target="tpu_custom_call" | custom-call | flops 1 | bytes 1 | tf_op jit(solution)/shard_map/pallas_call | solution.py:233
  42.2 1.1 %collective-permute-done.7.refs_0_ = bf16[32,4096]{1,0:T(8,128)(2,1)S(1)} collective-permute-done((bf16[32,4096]{1,0:T(8,128)(2,1)S(1)}, bf16[32,4096]{1,0:T(8,128)(2,1)S(1)}, u32[]{:S(2)}, u32[]{:S(2)}) %collective-permute-start.7) | collective-permute-done | bytes 262176 | tf_op jit(solution)/shard_map/ppermute | solution.py:331
  44.0 2.1 %collective-permute-done.4.refs_1_ = bf16[32,4096]{1,0:T(8,128)(2,1)S(1)} collective-permute-done((bf16[32,4096]{1,0:T(8,128)(2,1)S(1)}, bf16[32,4096]{1,0:T(8,128)(2,1)S(1)}, u32[]{:S(2)}, u32[]{:S(2)}) %collective-permute-start.4) | collective-permute-done | bytes 262176 | tf_op jit(solution)/shard_map/ppermute | solution.py:331
  46.8 1.4 %shard_map.77 = (bf16[64,256]{1,0:T(8,128)(2,1)S(1)}, bf16[64,256]{1,0:T(8,128)(2,1)S(1)}) custom-call(bf16[32,4096]{1,0:T(8,128)(2,1)S(1)} %collective-permute-done.7.refs_0_, bf16[32,4096]{1,0:T(8,128)(2,1)S(1)} %collective-permute-done.4.refs_1_, bf16[256,4096]{1,0:T(8,128)(2,1)S(1)} %copy-done, bf16[256,4096]{1,0:T(8,128)(2,1)S(1)} %copy-done.2), custom_call_target="tpu_custom_call" | custom-call | flops 1 | bytes 1 | tf_op jit(solution)/shard_map/pallas_call | solution.py:233
  48.2 1.5 %collective-permute-done.8.refs_0_ = bf16[32,4096]{1,0:T(8,128)(2,1)S(1)} collective-permute-done((bf16[32,4096]{1,0:T(8,128)(2,1)S(1)}, bf16[32,4096]{1,0:T(8,128)(2,1)S(1)}, u32[]{:S(2)}, u32[]{:S(2)}) %collective-permute-start.8) | collective-permute-done | bytes 262176 | tf_op jit(solution)/shard_map/ppermute | solution.py:331
  49.7 2.8 %collective-permute-done.5.refs_1_ = bf16[32,4096]{1,0:T(8,128)(2,1)S(1)} collective-permute-done((bf16[32,4096]{1,0:T(8,128)(2,1)S(1)}, bf16[32,4096]{1,0:T(8,128)(2,1)S(1)}, u32[]{:S(2)}, u32[]{:S(2)}) %collective-permute-start.5) | collective-permute-done | bytes 262176 | tf_op jit(solution)/shard_map/ppermute | solution.py:331
  53.2 1.4 %collective-permute-start.11 = (bf16[16,4096]{1,0:T(8,128)(2,1)S(1)}, bf16[16,4096]{1,0:T(8,128)(2,1)S(1)}, u32[]{:S(2)}, u32[]{:S(2)}) collective-permute-start(bf16[16,4096]{1,0:T(8,128)(2,1)S(1)} %slice_select_fusion), channel_id=1, source_target_pairs={{0,4},{1,3},{4,8},{5,1},{8,12},{9,5},{12,14},{13,9},{14,10},{15,13... | collective-permute-start | bytes 393224 | tf_op jit(solution)/shard_map/ppermute | solution.py:331
  54.6 1.4 %shard_map.78 = (bf16[64,256]{1,0:T(8,128)(2,1)S(1)}, bf16[64,256]{1,0:T(8,128)(2,1)S(1)}) custom-call(bf16[32,4096]{1,0:T(8,128)(2,1)S(1)} %collective-permute-done.8.refs_0_, bf16[32,4096]{1,0:T(8,128)(2,1)S(1)} %collective-permute-done.5.refs_1_, bf16[256,4096]{1,0:T(8,128)(2,1)S(1)} %copy-done, bf16[256,4096]{1,0:T(8,128)(2,1)S(1)} %copy-done.2), custom_call_target="tpu_custom_call" | custom-call | flops 1 | bytes 1 | tf_op jit(solution)/shard_map/pallas_call | solution.py:233
  56.0 2.9 %collective-permute-done.6.refs_1_ = bf16[32,4096]{1,0:T(8,128)(2,1)S(1)} collective-permute-done((bf16[32,4096]{1,0:T(8,128)(2,1)S(1)}, bf16[32,4096]{1,0:T(8,128)(2,1)S(1)}, u32[]{:S(2)}, u32[]{:S(2)}) %collective-permute-start.6) | collective-permute-done | bytes 262176 | tf_op jit(solution)/shard_map/ppermute | solution.py:331
  58.9 0.7 %collective-permute-start.9 = (bf16[16,4096]{1,0:T(8,128)(2,1)S(1)}, bf16[16,4096]{1,0:T(8,128)(2,1)S(1)}, u32[]{:S(2)}, u32[]{:S(2)}) collective-permute-start(bf16[16,4096]{1,0:T(8,128)(2,1)S(1)} %slice_select_fusion.1), channel_id=1, source_target_pairs={{0,4},{1,3},{4,8},{5,1},{8,12},{9,5},{12,14},{13,9},{14,10},{15,13... | collective-permute-start | bytes 393224 | tf_op jit(solution)/shard_map/ppermute | solution.py:331
  60.3 1.4 %shard_map.80 = (bf16[48,256]{1,0:T(8,128)(2,1)S(1)}, bf16[48,256]{1,0:T(8,128)(2,1)S(1)}) custom-call(bf16[16,4096]{1,0:T(8,128)(2,1)S(1)} %collective-permute-done.11.refs_0_, bf16[32,4096]{1,0:T(8,128)(2,1)S(1)} %collective-permute-done.6.refs_1_, bf16[256,4096]{1,0:T(8,128)(2,1)S(1)} %copy-done, bf16[256,4096]{1,0:T(8,128)(2,1)S(1)} %copy-done.2), custom_call_target="tpu_custom_call" | custom-call | flops 1 | bytes 1 | tf_op jit(solution)/shard_map/pallas_call | solution.py:233
  61.8 2.2 %collective-permute-done.9.refs_0_ = bf16[16,4096]{1,0:T(8,128)(2,1)S(1)} collective-permute-done((bf16[16,4096]{1,0:T(8,128)(2,1)S(1)}, bf16[16,4096]{1,0:T(8,128)(2,1)S(1)}, u32[]{:S(2)}, u32[]{:S(2)}) %collective-permute-start.9) | collective-permute-done | bytes 131104 | tf_op jit(solution)/shard_map/ppermute | solution.py:331
  64.0 1.2 %shard_map.79 = (bf16[16,256]{1,0:T(8,128)(2,1)S(1)}, bf16[16,256]{1,0:T(8,128)(2,1)S(1)}) custom-call(bf16[16,4096]{1,0:T(8,128)(2,1)S(1)} %collective-permute-done.9.refs_0_, bf16[256,4096]{1,0:T(8,128)(2,1)S(1)} %copy-done, bf16[256,4096]{1,0:T(8,128)(2,1)S(1)} %copy-done.3), custom_call_target="tpu_custom_call" | custom-call | flops 1 | bytes 1 | tf_op jit(solution)/shard_map/pallas_call | solution.py:233
  65.2 1.0 %shard_map.81.args_2_ = bf16[12,32,256]{2,1,0:T(8,128)(2,1)} custom-call(bf16[64,256]{1,0:T(8,128)(2,1)S(1)} %get-tuple-element.47.refs_0_, bf16[64,256]{1,0:T(8,128)(2,1)S(1)} %get-tuple-element.48.refs_1_, bf16[64,256]{1,0:T(8,128)(2,1)S(1)} %get-tuple-element.49.refs_2_, bf16[48,256]{1,0:T(8,128)(2,1)S(1)} %get-tuple-element.50.refs_3_, ...), custom_call_target="tpu_custom_call" | custom-call | flops 1 | bytes 1 | tf_op jit(solution)/shard_map/pallas_call | solution.py:285
  (30 shorter events, 6.1 us)
Async XLA Ops:
  0.0 22.9 %collective-permute-start = (bf16[256,4096]{1,0:T(8,128)(2,1)}, bf16[256,4096]{1,0:T(8,128)(2,1)S(1)}, u32[]{:S(2)}, u32[]{:S(2)}) collective-permute-start(bf16[256,4096]{1,0:T(8,128)(2,1)} %refs_2_.5), channel_id=1, source_target_pairs={{0,1},{1,0},{2,3},{3,2},{4,5},{5,4},{6,7},{7,6},{8,9},{9,8},{10,11... | collective-permute-start | bytes 6291464 | tf_op jit(solution)/shard_map/ppermute | solution.py:320
  22.9 1.3 %copy-start.1 = (bf16[256,4096]{1,0:T(8,128)(2,1)}, bf16[256,4096]{1,0:T(8,128)(2,1)S(1)}, u32[]{:S(2)}) copy-start(bf16[256,4096]{1,0:T(8,128)(2,1)S(1)} %collective-permute-done.refs_4_.refs_3_.refs_2_) | copy-start | bytes 6291460
  29.1 1.4 %collective-permute-start.1 = (bf16[16,4096]{1,0:T(8,128)(2,1)S(1)}, bf16[16,4096]{1,0:T(8,128)(2,1)S(1)}, u32[]{:S(2)}, u32[]{:S(2)}) collective-permute-start(bf16[16,4096]{1,0:T(8,128)(2,1)S(1)} %reshape.14.refs_0_), channel_id=1, source_target_pairs={{0,1},{1,0},{2,3},{3,2},{4,5},{5,4},{6,7},{7,6},{8,9},{9,8},{10,11... | collective-permute-start | bytes 393224 | tf_op jit(solution)/shard_map/ppermute | solution.py:325
  30.5 6.4 %collective-permute-start.2 = (bf16[32,4096]{1,0:T(8,128)(2,1)S(1)}, bf16[32,4096]{1,0:T(8,128)(2,1)S(1)}, u32[]{:S(2)}, u32[]{:S(2)}) collective-permute-start(bf16[32,4096]{1,0:T(8,128)(2,1)S(1)} %pad_maximum_fusion), channel_id=1, source_target_pairs={{0,4},{1,3},{4,8},{5,1},{8,12},{9,5},{12,14},{13,9},{14,10},{15,13... | collective-permute-start | bytes 786440 | tf_op jit(solution)/shard_map/ppermute | solution.py:331
  31.3 8.0 %copy-start = (bf16[256,4096]{1,0:T(8,128)(2,1)S(1)}, bf16[256,4096]{1,0:T(8,128)(2,1)}, u32[]{:S(2)}) copy-start(bf16[256,4096]{1,0:T(8,128)(2,1)} %refs_2_.5) | copy-start | bytes 6291460
  37.0 1.3 %collective-permute-start.3 = (bf16[16,4096]{1,0:T(8,128)(2,1)S(1)}, bf16[16,4096]{1,0:T(8,128)(2,1)S(1)}, u32[]{:S(2)}, u32[]{:S(2)}) collective-permute-start(bf16[16,4096]{1,0:T(8,128)(2,1)S(1)} %reshape.15.refs_1_), channel_id=1, source_target_pairs={{0,1},{1,0},{2,3},{3,2},{4,5},{5,4},{6,7},{7,6},{8,9},{9,8},{10,11... | collective-permute-start | bytes 393224 | tf_op jit(solution)/shard_map/ppermute | solution.py:325
  37.0 6.4 %collective-permute-start.7 = (bf16[32,4096]{1,0:T(8,128)(2,1)S(1)}, bf16[32,4096]{1,0:T(8,128)(2,1)S(1)}, u32[]{:S(2)}, u32[]{:S(2)}) collective-permute-start(bf16[32,4096]{1,0:T(8,128)(2,1)S(1)} %collective-permute-done.2.refs_2_), channel_id=1, source_target_pairs={{0,4},{1,3},{4,8},{5,1},{8,12},{9,5},{12,14},{13,9},{14,10},{15,13... | collective-permute-start | bytes 786440 | tf_op jit(solution)/shard_map/ppermute | solution.py:331
  38.4 7.8 %collective-permute-start.4 = (bf16[32,4096]{1,0:T(8,128)(2,1)S(1)}, bf16[32,4096]{1,0:T(8,128)(2,1)S(1)}, u32[]{:S(2)}, u32[]{:S(2)}) collective-permute-start(bf16[32,4096]{1,0:T(8,128)(2,1)S(1)} %pad_maximum_fusion.1), channel_id=1, source_target_pairs={{0,4},{1,3},{4,8},{5,1},{8,12},{9,5},{12,14},{13,9},{14,10},{15,13... | collective-permute-start | bytes 786440 | tf_op jit(solution)/shard_map/ppermute | solution.py:331
  39.3 1.6 %copy-start.2 = (bf16[256,4096]{1,0:T(8,128)(2,1)S(1)}, bf16[256,4096]{1,0:T(8,128)(2,1)}, u32[]{:S(2)}) copy-start(bf16[256,4096]{1,0:T(8,128)(2,1)} %copy-done.1) | copy-start | bytes 6291460
  43.3 6.4 %collective-permute-start.8 = (bf16[32,4096]{1,0:T(8,128)(2,1)S(1)}, bf16[32,4096]{1,0:T(8,128)(2,1)S(1)}, u32[]{:S(2)}, u32[]{:S(2)}) collective-permute-start(bf16[32,4096]{1,0:T(8,128)(2,1)S(1)} %collective-permute-done.7.refs_0_), channel_id=1, source_target_pairs={{0,4},{1,3},{4,8},{5,1},{8,12},{9,5},{12,14},{13,9},{14,10},{15,13... | collective-permute-start | bytes 786440 | tf_op jit(solution)/shard_map/ppermute | solution.py:331
  46.2 6.4 %collective-permute-start.5 = (bf16[32,4096]{1,0:T(8,128)(2,1)S(1)}, bf16[32,4096]{1,0:T(8,128)(2,1)S(1)}, u32[]{:S(2)}, u32[]{:S(2)}) collective-permute-start(bf16[32,4096]{1,0:T(8,128)(2,1)S(1)} %collective-permute-done.4.refs_1_), channel_id=1, source_target_pairs={{0,4},{1,3},{4,8},{5,1},{8,12},{9,5},{12,14},{13,9},{14,10},{15,13... | collective-permute-start | bytes 786440 | tf_op jit(solution)/shard_map/ppermute | solution.py:331
  52.5 6.4 %collective-permute-start.6 = (bf16[32,4096]{1,0:T(8,128)(2,1)S(1)}, bf16[32,4096]{1,0:T(8,128)(2,1)S(1)}, u32[]{:S(2)}, u32[]{:S(2)}) collective-permute-start(bf16[32,4096]{1,0:T(8,128)(2,1)S(1)} %collective-permute-done.5.refs_1_), channel_id=1, source_target_pairs={{0,4},{1,3},{4,8},{5,1},{8,12},{9,5},{12,14},{13,9},{14,10},{15,13... | collective-permute-start | bytes 786440 | tf_op jit(solution)/shard_map/ppermute | solution.py:331
  53.2 7.1 %collective-permute-start.11 = (bf16[16,4096]{1,0:T(8,128)(2,1)S(1)}, bf16[16,4096]{1,0:T(8,128)(2,1)S(1)}, u32[]{:S(2)}, u32[]{:S(2)}) collective-permute-start(bf16[16,4096]{1,0:T(8,128)(2,1)S(1)} %slice_select_fusion), channel_id=1, source_target_pairs={{0,4},{1,3},{4,8},{5,1},{8,12},{9,5},{12,14},{13,9},{14,10},{15,13... | collective-permute-start | bytes 393224 | tf_op jit(solution)/shard_map/ppermute | solution.py:331
  58.9 5.0 %copy-start.3 = (bf16[256,4096]{1,0:T(8,128)(2,1)S(1)}, bf16[256,4096]{1,0:T(8,128)(2,1)}, u32[]{:S(2)}) copy-start(bf16[256,4096]{1,0:T(8,128)(2,1)} %copy-done.1) | copy-start | bytes 6291460
  58.9 5.0 %collective-permute-start.9 = (bf16[16,4096]{1,0:T(8,128)(2,1)S(1)}, bf16[16,4096]{1,0:T(8,128)(2,1)S(1)}, u32[]{:S(2)}, u32[]{:S(2)}) collective-permute-start(bf16[16,4096]{1,0:T(8,128)(2,1)S(1)} %slice_select_fusion.1), channel_id=1, source_target_pairs={{0,4},{1,3},{4,8},{5,1},{8,12},{9,5},{12,14},{13,9},{14,10},{15,13... | collective-permute-start | bytes 393224 | tf_op jit(solution)/shard_map/ppermute | solution.py:331
  61.7 3.5 %collective-permute-start.12 = (bf16[240,256]{1,0:T(8,128)(2,1)S(1)}, bf16[240,256]{1,0:T(8,128)(2,1)S(1)}, u32[]{:S(2)}, u32[]{:S(2)}) collective-permute-start(bf16[240,256]{1,0:T(8,128)(2,1)S(1)} %pad_maximum_fusion.2), channel_id=1, source_target_pairs={{0,1},{1,0},{2,3},{3,2},{4,5},{5,4},{6,7},{7,6},{8,9},{9,8},{10,11... | collective-permute-start | bytes 368648 | tf_op jit(solution)/shard_map/ppermute | solution.py:358
  65.1 1.2 %collective-permute-start.10 = (bf16[16,256]{1,0:T(8,128)(2,1)S(1)}, bf16[16,256]{1,0:T(8,128)(2,1)S(1)}, u32[]{:S(2)}, u32[]{:S(2)}) collective-permute-start(bf16[16,256]{1,0:T(8,128)(2,1)S(1)} %get-tuple-element.46), channel_id=1, source_target_pairs={{0,1},{1,0},{2,3},{3,2},{4,5},{5,4},{6,7},{7,6},{8,9},{9,8},{10,11... | collective-permute-start | bytes 24584 | tf_op jit(solution)/shard_map/ppermute | solution.py:360

commit v4 on v3

--- a/solution.py
+++ b/solution.py
@@ -11,6 +11,8 @@
 NEWTON_STEPS = 6
 LEAD = 5
 TAIL = 16
+GRAM_DOCS = 2
+SCORE_COST = 6 * 10**9
 F32 = jnp.float32
 BF16 = jnp.bfloat16
 HIGHEST_PRECISION = lax.Precision.HIGHEST
@@ -146,10 +148,14 @@
     named = [recv_ref[s, cap:, :].astype(F32)[:1] for s in range(sources)]
     slot = jnp.concatenate([jnp.where(half, named[s], named[s + 1]) for s in range(0, sources, 2)], axis=1)
     across = rows_ref[...]
-    for d in range(docs):
-        mine = (slot == (first_doc + d + 1)).astype(F32)
-        gram_ref[d] = jnp.dot(across * mine.astype(BF16), rows, preferred_element_type=F32)
-        count_ref[d : d + 1, :] = jnp.broadcast_to(jnp.sum(mine, axis=1, keepdims=True), (1, wide))
+    for d in range(0, docs, GRAM_DOCS):
+        picked = []
+        for e in range(d, d + GRAM_DOCS):
+            mine = (slot == (first_doc + e + 1)).astype(F32)
+            picked.append(across * mine.astype(BF16))
+            count_ref[e : e + 1, :] = jnp.broadcast_to(jnp.sum(mine, axis=1, keepdims=True), (1, wide))
+        gram = jnp.dot(jnp.concatenate(picked, axis=0), rows, preferred_element_type=F32)
+        gram_ref[d : d + GRAM_DOCS] = gram.reshape(GRAM_DOCS, wide, wide)
 
     row_at = lax.broadcasted_iota(jnp.int32, (low, wide), 0)
     lane_at = lax.broadcasted_iota(jnp.int32, (low, wide), 1)
@@ -227,15 +233,38 @@
     other_ref[...] = lax.dot_general(blocks, other_rows[...], LAST_DIMS, preferred_element_type=F32).astype(BF16)
 
 
-def scores_of(blocks, own_rows, other_rows):
+def bring_and_score_kernel(*refs):
+    own_rows, other_hbm, own_ref, other_ref, kept_ref, sems = refs[-6:]
+    parts = sems.shape[0]
+    part = kept_ref.shape[1] // parts
+    places = [slice(i * part, (i + 1) * part) for i in range(parts)]
+    copies = [
+        pltpu.make_async_copy(other_hbm.at[:, pl.ds(i * part, part)], kept_ref.at[:, pl.ds(i * part, part)], sems.at[i])
+        for i in range(parts)
+    ]
+    for copy in copies:
+        copy.start()
+    blocks = jnp.concatenate([ref[...] for ref in refs[:-6]], axis=0)
+    own_ref[...] = lax.dot_general(blocks, own_rows[...], LAST_DIMS, preferred_element_type=F32).astype(BF16)
+    total = jnp.zeros(other_ref.shape, F32)
+    for at, copy in zip(places, copies):
+        copy.wait()
+        total += lax.dot_general(blocks[:, at], kept_ref[:, at], LAST_DIMS, preferred_element_type=F32)
+    other_ref[...] = total.astype(BF16)
+
+
+def scores_of(blocks, own_rows, other_rows, bring):
     count = sum(block.shape[0] for block in blocks)
     shape = jax.ShapeDtypeStruct((count, own_rows.shape[0]), BF16)
+    vmem = pl.BlockSpec(memory_space=pltpu.VMEM)
+    kept = [jax.ShapeDtypeStruct(other_rows.shape, BF16)] if bring else []
     return pl.pallas_call(
-        score_kernel,
-        out_shape=(shape, shape),
-        in_specs=[pl.BlockSpec(memory_space=pltpu.VMEM)] * (len(blocks) + 2),
-        out_specs=(pl.BlockSpec(memory_space=pltpu.VMEM),) * 2,
-        cost_estimate=pl.CostEstimate(flops=1, bytes_accessed=1, transcendentals=0),
+        bring_and_score_kernel if bring else score_kernel,
+        out_shape=[shape, shape] + kept,
+        in_specs=[vmem] * (len(blocks) + 1) + [pl.BlockSpec(memory_space=pltpu.HBM) if bring else vmem],
+        out_specs=[vmem] * (2 + len(kept)),
+        scratch_shapes=[pltpu.SemaphoreType.DMA((4,))] if bring else [],
+        cost_estimate=pl.CostEstimate(flops=SCORE_COST, bytes_accessed=2**20, transcendentals=0),
         compiler_params=pltpu.CompilerParams(vmem_limit_bytes=16 * 2**20),
     )(*blocks, own_rows, other_rows)
 
@@ -249,10 +278,10 @@
     copies = []
     for ref, (own, listed) in zip(refs, places):
         scorer = core if own else 1 - core
-        for number, (chunk, hop, second) in enumerate(listed):
+        for number, (chunk, hop, partner) in enumerate(listed):
             there = lax.rem(spot + jnp.where(scorer == 0, chips - hop, hop), chips)
             where = jnp.where(there < chips // 2, 2 * there, 2 * (chips - 1 - there) + 1)
-            owner = 2 * where + (scorer if hop in (0, chips // 2) else second)
+            owner = 2 * where + (1 - scorer if partner else scorer)
             stop = lax.rem(device + LEAD - owner + owners, owners)
             wanted = stop < out_ref.shape[0]
             copy = pltpu.make_async_copy(
@@ -314,53 +343,56 @@
     cap = 4 * toks // owners
     docs = DOC_DEV // 2
     ring, swap = ring_pairs(owners)
-    odd = lax.rem(lax.axis_index("blk"), 2) == 1
 
     send = packed_rows(query_inputs, query_grads, proj_in, proj_out, token_owner, token_slot, owners, cap)
+    recv = lax.all_to_all(send, "blk", split_axis=0, concat_axis=0, tiled=True)
+
+    def ring_on(block, links=ring):
+        return lax.ppermute(block, "blk", links)
+
+    following = dict(ring)
+    second_next = [(device, following[step]) for device, step in ring]
+
+    first_own = queries_of(recv, 0, docs, low)
+    first_next, first_second = ring_on(first_own), ring_on(first_own, second_next)
+    first_given = lax.ppermute(first_own, "blk", swap)
+    recv, train_rows, first_own = lax.optimization_barrier((recv, train_rows, first_own))
     other_rows = lax.ppermute(train_rows, "blk", swap)
-    recv = lax.all_to_all(send, "blk", split_axis=0, concat_axis=0, tiled=True)
-    recv, other_rows = lax.optimization_barrier((recv, other_rows))
-
-    def pair_up(mine):
-        theirs = lax.ppermute(mine, "blk", swap)
-        return jnp.concatenate([jnp.where(odd, theirs, mine), jnp.where(odd, mine, theirs)], axis=0)
-
-    def onward(block, hop):
-        if hop == hops:
-            block = jnp.where(odd, block[docs:], block[:docs])
-        return lax.ppermute(block, "blk", ring)
-
-    def listed(chunk, hop):
-        return [(chunk, hop, second) for second in ((0,) if hop in (0, hops) else (0, 1))]
-
-    first_own = queries_of(recv, 0, docs, low)
-    first = pair_up(first_own)
-    recv, first = lax.optimization_barrier((recv, first))
     last_own = queries_of(recv, docs, docs, low)
-    first = onward(first, 1)
-    last_own, first = lax.optimization_barrier((last_own, first))
-    last = pair_up(last_own)
-    waiting = [first_own, last_own, first]
-    lists = listed(0, 0) + listed(1, 0) + listed(0, 1)
-    scored, places = [], []
-    for hop in range(1, hops + 1):
-        ahead = onward(first, hop + 1) if hop < hops else None
-        came = onward(last, hop)
-        scored.append(scores_of(waiting, train_rows, other_rows))
-        places.append(lists)
-        if hop < hops - 1:
-            ahead, scored[-1] = lax.optimization_barrier((ahead, scored[-1]))
-        elif hop == hops - 1:
-            came, scored[-1] = lax.optimization_barrier((came, scored[-1]))
-        waiting = [came] if ahead is None else [ahead, came]
-        lists = ([] if ahead is None else listed(0, hop + 1)) + listed(1, hop)
-        first, last = ahead, came
-    early = lax.ppermute(jnp.concatenate([other for _, other in scored], axis=0), "blk", swap)
-    final = scores_of(waiting, train_rows, other_rows)
-    late = lax.ppermute(final[1], "blk", swap)
-    most = [(own, True, listing) for (own, _), listing in zip(scored, places)] + [(early, False, sum(places, []))]
-    placed = put_in_order(most, owners, docs, None)
-    return put_in_order([(final[0], True, lists), (late, False, lists)], owners, docs, placed)
+    last_own, first_next, first_second, first_given = lax.optimization_barrier(
+        (last_own, first_next, first_second, first_given)
+    )
+    waiting = [first_own, last_own, first_next, first_second]
+    lists = [(0, 0, 0), (1, 0, 0), (0, 1, 0), (0, 2, 0)]
+    first = jnp.concatenate([first_second, first_given], axis=0)
+    last = jnp.concatenate([last_own, lax.ppermute(last_own, "blk", swap)], axis=0)
+    for hop in range(1, hops):
+        near = hop < hops - 1
+        first = ring_on(first if near else first[docs:])
+        if near:
+            waiting.append(first)
+            lists = lists + [(0, hop + 2, 0), (0, hop, 1)]
+        else:
+            most, most_lists, waiting, lists = waiting, lists, before, before_lists
+            waiting = waiting + [first]
+            lists = lists + [(0, hop, 1)]
+        last = ring_on(last)
+        came, listed = [last], [(1, hop + 1, 0), (1, hop, 1)]
+        if hop == 1:
+            last_second = ring_on(last_own, second_next)
+            came, listed = [last, last_second], [(1, 1, 0), (1, 1, 1), (1, 2, 0)]
+            last = jnp.concatenate([last_second, last[docs:]], axis=0)
+        if hop == hops - 2:
+            before, before_lists = came, listed
+        else:
+            waiting = waiting + came
+            lists = lists + listed
+    own_most, other_most, other_rows = scores_of(most, train_rows, other_rows, True)
+    early = lax.ppermute(other_most, "blk", swap)
+    own_late, other_late = scores_of(waiting, train_rows, other_rows, False)
+    late = lax.ppermute(other_late, "blk", swap)
+    placed = put_in_order([(own_most, True, most_lists), (early, False, most_lists)], owners, docs, None)
+    return put_in_order([(own_late, True, lists), (late, False, lists)], owners, docs, placed)
 
 
 def passed_along(value, axis, steps):

time: 67.3 us -> 64.9 us (0.964)
  starting transfers between devices: 7.06 us -> 11.3 us
  local copies, waits for them, and re-layouts: 3.47 us -> 0.56 us
  waiting for transfers between devices: 16.2 us -> 13.7 us
  Pallas kernels: 21.8 us -> 20.2 us
    ppermute x12 -> x13, starting transfers between devices: 6.61 us -> 10.8 us  [the longest x9 10.6 us: ring_on(): return lax.ppermute(block, 'blk', links)]
    unnamed x8 -> x2, local copies, waits for them, and re-layouts: 2.92 us -> 0.01 us
    ppermute x12 -> x13, waiting for transfers between devices: 16.2 us -> 13.7 us  [the longest x9 13.4 us: ring_on(): return lax.ppermute(block, 'blk', links)]
    pallas_call x5 -> x2, Pallas kernels: 6.68 us -> 5.11 us  [scores_of(): pl.pallas_call(bring_and_score_kernel if bring else score_kernel, out_sha...]
  transfers between devices with their start and end apart: 13 -> 14, of which waited for: 11 -> 7; matrix products, arithmetic and copies ran while one was open for 1% -> 1% of each run, Pallas kernels for 25% -> 16%
where the time goes in v4:
time: 64.9 us; the launch traced here: 64.7 us
  Pallas kernels  20.2 us (31%)
  blocking collectives  18.5 us (29%)
  waiting for transfers between devices  13.7 us (21%)
  starting transfers between devices  11.3 us (17%)
    all_to_all x1, blocking collectives, gathered(): recv = lax.all_to_all(send, 'blk', split_axis=0, concat_axis=0, tiled=True)  18.5 us
    ppermute x9, waiting for transfers between devices, ring_on(): return lax.ppermute(block, 'blk', links)  13.4 us
    ppermute x9, starting transfers between devices, ring_on(): return lax.ppermute(block, 'blk', links)  10.6 us
    pallas_call x2, Pallas kernels, queries_of(): pl.pallas_call(functools.partial(query_kernel, first_doc), out_shape=jax....  9.19 us
    pallas_call x2, Pallas kernels, scores_of(): pl.pallas_call(bring_and_score_kernel if bring else score_kernel, out_sha...  5.11 us
    pallas_call x1, Pallas kernels, packed_rows(): pl.pallas_call(pack_kernel, out_shape=jax.ShapeDtypeStruct((owners, cap +...  4.28 us
    pallas_call x2, Pallas kernels, put_in_order(): pl.pallas_call(kernel, out_shape=shape, in_specs=specs, out_specs=pl.Bloc...  1.65 us
  transfers between devices with their start and end apart: 14, of which 7 were waited for; matrix products, arithmetic and copies ran while one was open for 1% of the time, Pallas kernels for 16%

profile of v4, /device:TPU:0, one launch (start us, length us, event | category | flops | bytes accessed | tf_op | source)
XLA Modules:
  0.0 64.7 jit_solution(3903793078162343832)
XLA Ops:
  0.0 4.3 %shard_map.73 = bf16[16,80,128]{2,1,0:T(8,128)(2,1)} custom-call(bf16[256,4096]{1,0:T(8,128)(2,1)} %inputs_hbm.1, bf16[256,4096]{1,0:T(8,128)(2,1)} %grads_hbm.1, bf16[64,4096]{1,0:T(8,128)(2,1)} %bitcast.4, bf16[64,4096]{1,0:T(8,128)(2,1)} %bitcast.5, s32[1,256]{1,0:T(1,128)} %bitcast.6, s32[1,256]{1,0:T(1,128)} %bitcast.7), custom_call_target="tpu_custom_call" | custom-call | tf_op jit(solution)/shard_map/pallas_call | solution.py:78
  4.3 18.5 %all_to_all.5.recv_ref = bf16[16,80,128]{2,1,0:T(8,128)(2,1)S(1)} all-to-all(bf16[16,80,128]{2,1,0:T(8,128)(2,1)} %shard_map.73), channel_id=1, replica_groups=mesh['groups'=2,'blk'=16] {'blk'}, dimensions={0} | all-to-all | bytes 655360 | tf_op jit(solution)/shard_map/all_to_all | solution.py:348
  22.8 4.6 %shard_map.74 = bf16[16,64,64]{2,1,0:T(8,128)(2,1)S(1)} custom-call(bf16[16,80,128]{2,1,0:T(8,128)(2,1)S(1)} %all_to_all.5.recv_ref), custom_call_target="tpu_custom_call" | custom-call | flops 4000000000 | bytes 1048576 | tf_op jit(solution)/shard_map/pallas_call | solution.py:213
  27.4 0.3 reshape.14.refs_0_
  27.7 0.3 collective-permute-start
  28.0 1.4 %collective-permute-start.1 = (bf16[16,4096]{1,0:T(8,128)(2,1)S(1)}, bf16[16,4096]{1,0:T(8,128)(2,1)S(1)}, u32[]{:S(2)}, u32[]{:S(2)}) collective-permute-start(bf16[16,4096]{1,0:T(8,128)(2,1)S(1)} %reshape.14.refs_0_), channel_id=1, source_target_pairs={{0,8},{1,7},{4,12},{5,3},{8,14},{9,1},{12,10},{13,5},{14,6},{15,9}... | collective-permute-start | bytes 393224 | tf_op jit(solution)/shard_map/ppermute | solution.py:351
  29.4 0.5 collective-permute-start.11
  29.9 4.6 %shard_map.75 = bf16[16,64,64]{2,1,0:T(8,128)(2,1)S(1)} custom-call(bf16[16,80,128]{2,1,0:T(8,128)(2,1)S(1)} %all_to_all.5.recv_ref), custom_call_target="tpu_custom_call" | custom-call | flops 4000000000 | bytes 1048576 | tf_op jit(solution)/shard_map/pallas_call | solution.py:213
  34.5 0.3 reshape.15.refs_1_
  34.9 1.4 %collective-permute-start.7 = (bf16[32,4096]{1,0:T(8,128)(2,1)S(1)}, bf16[32,4096]{1,0:T(8,128)(2,1)S(1)}, u32[]{:S(2)}, u32[]{:S(2)}) collective-permute-start(bf16[32,4096]{1,0:T(8,128)(2,1)S(1)} %pad_maximum_fusion.2), channel_id=1, source_target_pairs={{0,4},{1,3},{4,8},{5,1},{8,12},{9,5},{12,14},{13,9},{14,10},{15,13... | collective-permute-start | bytes 786440 | tf_op jit(solution)/shard_map/ppermute | solution.py:351
  36.3 1.3 %collective-permute-start.5 = (bf16[32,4096]{1,0:T(8,128)(2,1)S(1)}, bf16[32,4096]{1,0:T(8,128)(2,1)S(1)}, u32[]{:S(2)}, u32[]{:S(2)}) collective-permute-start(bf16[32,4096]{1,0:T(8,128)(2,1)S(1)} %pad_maximum_fusion), channel_id=1, source_target_pairs={{0,4},{1,3},{4,8},{5,1},{8,12},{9,5},{12,14},{13,9},{14,10},{15,13... | collective-permute-start | bytes 786440 | tf_op jit(solution)/shard_map/ppermute | solution.py:351
  37.6 2.2 %collective-permute-start.3 = (bf16[16,4096]{1,0:T(8,128)(2,1)S(1)}, bf16[16,4096]{1,0:T(8,128)(2,1)S(1)}, u32[]{:S(2)}, u32[]{:S(2)}) collective-permute-start(bf16[16,4096]{1,0:T(8,128)(2,1)S(1)} %reshape.15.refs_1_), channel_id=1, source_target_pairs={{0,8},{1,7},{4,12},{5,3},{8,14},{9,1},{12,10},{13,5},{14,6},{15,9}... | collective-permute-start | bytes 393224 | tf_op jit(solution)/shard_map/ppermute | solution.py:351
  39.8 1.5 %collective-permute-done.7.refs_4_ = bf16[32,4096]{1,0:T(8,128)(2,1)S(1)} collective-permute-done((bf16[32,4096]{1,0:T(8,128)(2,1)S(1)}, bf16[32,4096]{1,0:T(8,128)(2,1)S(1)}, u32[]{:S(2)}, u32[]{:S(2)}) %collective-permute-start.7) | collective-permute-done | bytes 262176 | tf_op jit(solution)/shard_map/ppermute | solution.py:351
  41.3 1.9 %collective-permute-start.8 = (bf16[32,4096]{1,0:T(8,128)(2,1)S(1)}, bf16[32,4096]{1,0:T(8,128)(2,1)S(1)}, u32[]{:S(2)}, u32[]{:S(2)}) collective-permute-start(bf16[32,4096]{1,0:T(8,128)(2,1)S(1)} %collective-permute-done.7.refs_4_), channel_id=1, source_target_pairs={{0,4},{1,3},{4,8},{5,1},{8,12},{9,5},{12,14},{13,9},{14,10},{15,13... | collective-permute-start | bytes 786440 | tf_op jit(solution)/shard_map/ppermute | solution.py:351
  43.2 1.2 %collective-permute-done.5.refs_5_ = bf16[32,4096]{1,0:T(8,128)(2,1)S(1)} collective-permute-done((bf16[32,4096]{1,0:T(8,128)(2,1)S(1)}, bf16[32,4096]{1,0:T(8,128)(2,1)S(1)}, u32[]{:S(2)}, u32[]{:S(2)}) %collective-permute-start.5) | collective-permute-done | bytes 262176 | tf_op jit(solution)/shard_map/ppermute | solution.py:351
  44.4 3.9 %collective-permute-done.3.refs_6_ = bf16[16,4096]{1,0:T(8,128)(2,1)S(1)} collective-permute-done((bf16[16,4096]{1,0:T(8,128)(2,1)S(1)}, bf16[16,4096]{1,0:T(8,128)(2,1)S(1)}, u32[]{:S(2)}, u32[]{:S(2)}) %collective-permute-start.3) | collective-permute-done | bytes 131104 | tf_op jit(solution)/shard_map/ppermute | solution.py:351
  48.4 0.7 %collective-permute-done.8.refs_7_ = bf16[32,4096]{1,0:T(8,128)(2,1)S(1)} collective-permute-done((bf16[32,4096]{1,0:T(8,128)(2,1)S(1)}, bf16[32,4096]{1,0:T(8,128)(2,1)S(1)}, u32[]{:S(2)}, u32[]{:S(2)}) %collective-permute-start.8) | collective-permute-done | bytes 262176 | tf_op jit(solution)/shard_map/ppermute | solution.py:351
  49.1 2.1 %collective-permute-start.9 = (bf16[16,4096]{1,0:T(8,128)(2,1)S(1)}, bf16[16,4096]{1,0:T(8,128)(2,1)S(1)}, u32[]{:S(2)}, u32[]{:S(2)}) collective-permute-start(bf16[16,4096]{1,0:T(8,128)(2,1)S(1)} %slice.9), channel_id=1, source_target_pairs={{0,4},{1,3},{4,8},{5,1},{8,12},{9,5},{12,14},{13,9},{14,10},{15,13... | collective-permute-start | bytes 393224 | tf_op jit(solution)/shard_map/ppermute | solution.py:351
  51.2 3.6 %collective-permute-done.6.refs_0_ = bf16[32,4096]{1,0:T(8,128)(2,1)S(1)} collective-permute-done((bf16[32,4096]{1,0:T(8,128)(2,1)S(1)}, bf16[32,4096]{1,0:T(8,128)(2,1)S(1)}, u32[]{:S(2)}, u32[]{:S(2)}) %collective-permute-start.6) | collective-permute-done | bytes 262176 | tf_op jit(solution)/shard_map/ppermute | solution.py:351
  54.8 3.7 %shard_map.76 = (bf16[176,256]{1,0:T(8,128)(2,1)S(1)}, bf16[176,256]{1,0:T(8,128)(2,1)S(1)}, bf16[256,4096]{1,0:T(8,128)(2,1)S(1)}) custom-call(bf16[16,4096]{1,0:T(8,128)(2,1)S(1)} %reshape.14.refs_0_, bf16[16,4096]{1,0:T(8,128)(2,1)S(1)} %reshape.15.refs_1_, bf16[16,4096]{1,0:T(8,128)(2,1)S(1)} %collective-permute-done.refs_2_, ...), custom_call_target="tpu_custom_call" | custom-call | flops 6000000000 | bytes 1048576 | tf_op jit(solution)/shard_map/pallas_call | solution.py:261
  58.6 2.5 %collective-permute-done.10.refs_2_ = bf16[32,4096]{1,0:T(8,128)(2,1)S(1)} collective-permute-done((bf16[32,4096]{1,0:T(8,128)(2,1)S(1)}, bf16[32,4096]{1,0:T(8,128)(2,1)S(1)}, u32[]{:S(2)}, u32[]{:S(2)}) %collective-permute-start.10) | collective-permute-done | bytes 262176 | tf_op jit(solution)/shard_map/ppermute | solution.py:351
  61.1 1.4 %shard_map.77 = (bf16[80,256]{1,0:T(8,128)(2,1)S(1)}, bf16[80,256]{1,0:T(8,128)(2,1)S(1)}) custom-call(bf16[32,4096]{1,0:T(8,128)(2,1)S(1)} %collective-permute-done.6.refs_0_, bf16[16,4096]{1,0:T(8,128)(2,1)S(1)} %collective-permute-done.9.refs_1_, bf16[32,4096]{1,0:T(8,128)(2,1)S(1)} %collective-permute-done.10.refs_2_, bf16[256,4096]{1,0:T(8,128)(2,1)S(1)} %copy-done, ...), custom_call_target="tpu_custom_call" | custom-call | flops 6000000000 | bytes 1048576 | tf_op jit(solution)/shard_map/pallas_call | solution.py:261
  62.6 0.9 %shard_map.78.args_2_ = bf16[12,32,256]{2,1,0:T(8,128)(2,1)} custom-call(bf16[176,256]{1,0:T(8,128)(2,1)S(1)} %get-tuple-element.27.refs_0_, bf16[176,256]{1,0:T(8,128)(2,1)S(1)} %collective-permute-done.13.refs_1_), custom_call_target="tpu_custom_call" | custom-call | flops 1 | bytes 1 | tf_op jit(solution)/shard_map/pallas_call | solution.py:314
  63.8 0.7 %shard_map.79 = bf16[12,32,256]{2,1,0:T(8,128)(2,1)} custom-call(bf16[80,256]{1,0:T(8,128)(2,1)S(1)} %get-tuple-element.25.args_0_, bf16[80,256]{1,0:T(8,128)(2,1)S(1)} %collective-permute-done.12.args_1_, bf16[12,32,256]{2,1,0:T(8,128)(2,1)} %shard_map.78.args_2_), custom_call_target="tpu_custom_call", output_to_operand_aliasing={{}: (2, {})} | custom-call | flops 1 | bytes 1 | tf_op jit(solution)/shard_map/pallas_call | solution.py:314
  (21 shorter events, 0.6 us)
Async XLA Ops:
  22.8 6.6 %copy-start = (bf16[256,4096]{1,0:T(8,128)(2,1)S(1)}, bf16[256,4096]{1,0:T(8,128)(2,1)}, u32[]{:S(2)}) copy-start(bf16[256,4096]{1,0:T(8,128)(2,1)} %refs_3_) | copy-start | bytes 6291460
  27.7 7.1 %collective-permute-start = (bf16[16,4096]{1,0:T(8,128)(2,1)S(1)}, bf16[16,4096]{1,0:T(8,128)(2,1)S(1)}, u32[]{:S(2)}, u32[]{:S(2)}) collective-permute-start(bf16[16,4096]{1,0:T(8,128)(2,1)S(1)} %reshape.14.refs_0_), channel_id=1, source_target_pairs={{0,4},{1,3},{4,8},{5,1},{8,12},{9,5},{12,14},{13,9},{14,10},{15,13... | collective-permute-start | bytes 393224 | tf_op jit(solution)/shard_map/ppermute | solution.py:351
  28.0 6.8 %collective-permute-start.1 = (bf16[16,4096]{1,0:T(8,128)(2,1)S(1)}, bf16[16,4096]{1,0:T(8,128)(2,1)S(1)}, u32[]{:S(2)}, u32[]{:S(2)}) collective-permute-start(bf16[16,4096]{1,0:T(8,128)(2,1)S(1)} %reshape.14.refs_0_), channel_id=1, source_target_pairs={{0,8},{1,7},{4,12},{5,3},{8,14},{9,1},{12,10},{13,5},{14,6},{15,9}... | collective-permute-start | bytes 393224 | tf_op jit(solution)/shard_map/ppermute | solution.py:351
  29.4 5.4 %collective-permute-start.2 = (bf16[16,4096]{1,0:T(8,128)(2,1)S(1)}, bf16[16,4096]{1,0:T(8,128)(2,1)S(1)}, u32[]{:S(2)}, u32[]{:S(2)}) collective-permute-start(bf16[16,4096]{1,0:T(8,128)(2,1)S(1)} %reshape.14.refs_0_), channel_id=1, source_target_pairs={{0,1},{1,0},{2,3},{3,2},{4,5},{5,4},{6,7},{7,6},{8,9},{9,8},{10,11... | collective-permute-start | bytes 393224 | tf_op jit(solution)/shard_map/ppermute | solution.py:358
  29.4 25.4 %collective-permute-start.11 = (bf16[256,4096]{1,0:T(8,128)(2,1)S(1)}, bf16[256,4096]{1,0:T(8,128)(2,1)}, u32[]{:S(2)}, u32[]{:S(2)}) collective-permute-start(bf16[256,4096]{1,0:T(8,128)(2,1)S(1)} %copy-done), channel_id=1, source_target_pairs={{0,1},{1,0},{2,3},{3,2},{4,5},{5,4},{6,7},{7,6},{8,9},{9,8},{10,11... | collective-permute-start | bytes 6291464 | tf_op jit(solution)/shard_map/ppermute | solution.py:360
  34.8 1.5 %collective-permute-start.4 = (bf16[16,4096]{1,0:T(8,128)(2,1)S(1)}, bf16[16,4096]{1,0:T(8,128)(2,1)S(1)}, u32[]{:S(2)}, u32[]{:S(2)}) collective-permute-start(bf16[16,4096]{1,0:T(8,128)(2,1)S(1)} %reshape.15.refs_1_), channel_id=1, source_target_pairs={{0,1},{1,0},{2,3},{3,2},{4,5},{5,4},{6,7},{7,6},{8,9},{9,8},{10,11... | collective-permute-start | bytes 393224 | tf_op jit(solution)/shard_map/ppermute | solution.py:368
  34.9 6.4 %collective-permute-start.7 = (bf16[32,4096]{1,0:T(8,128)(2,1)S(1)}, bf16[32,4096]{1,0:T(8,128)(2,1)S(1)}, u32[]{:S(2)}, u32[]{:S(2)}) collective-permute-start(bf16[32,4096]{1,0:T(8,128)(2,1)S(1)} %pad_maximum_fusion.2), channel_id=1, source_target_pairs={{0,4},{1,3},{4,8},{5,1},{8,12},{9,5},{12,14},{13,9},{14,10},{15,13... | collective-permute-start | bytes 786440 | tf_op jit(solution)/shard_map/ppermute | solution.py:351
  36.3 8.1 %collective-permute-start.5 = (bf16[32,4096]{1,0:T(8,128)(2,1)S(1)}, bf16[32,4096]{1,0:T(8,128)(2,1)S(1)}, u32[]{:S(2)}, u32[]{:S(2)}) collective-permute-start(bf16[32,4096]{1,0:T(8,128)(2,1)S(1)} %pad_maximum_fusion), channel_id=1, source_target_pairs={{0,4},{1,3},{4,8},{5,1},{8,12},{9,5},{12,14},{13,9},{14,10},{15,13... | collective-permute-start | bytes 786440 | tf_op jit(solution)/shard_map/ppermute | solution.py:351
  37.6 10.7 %collective-permute-start.3 = (bf16[16,4096]{1,0:T(8,128)(2,1)S(1)}, bf16[16,4096]{1,0:T(8,128)(2,1)S(1)}, u32[]{:S(2)}, u32[]{:S(2)}) collective-permute-start(bf16[16,4096]{1,0:T(8,128)(2,1)S(1)} %reshape.15.refs_1_), channel_id=1, source_target_pairs={{0,8},{1,7},{4,12},{5,3},{8,14},{9,1},{12,10},{13,5},{14,6},{15,9}... | collective-permute-start | bytes 393224 | tf_op jit(solution)/shard_map/ppermute | solution.py:351
  41.3 7.8 %collective-permute-start.8 = (bf16[32,4096]{1,0:T(8,128)(2,1)S(1)}, bf16[32,4096]{1,0:T(8,128)(2,1)S(1)}, u32[]{:S(2)}, u32[]{:S(2)}) collective-permute-start(bf16[32,4096]{1,0:T(8,128)(2,1)S(1)} %collective-permute-done.7.refs_4_), channel_id=1, source_target_pairs={{0,4},{1,3},{4,8},{5,1},{8,12},{9,5},{12,14},{13,9},{14,10},{15,13... | collective-permute-start | bytes 786440 | tf_op jit(solution)/shard_map/ppermute | solution.py:351
  48.3 6.4 %collective-permute-start.6 = (bf16[32,4096]{1,0:T(8,128)(2,1)S(1)}, bf16[32,4096]{1,0:T(8,128)(2,1)S(1)}, u32[]{:S(2)}, u32[]{:S(2)}) collective-permute-start(bf16[32,4096]{1,0:T(8,128)(2,1)S(1)} %pad_maximum_fusion.1), channel_id=1, source_target_pairs={{0,4},{1,3},{4,8},{5,1},{8,12},{9,5},{12,14},{13,9},{14,10},{15,13... | collective-permute-start | bytes 786440 | tf_op jit(solution)/shard_map/ppermute | solution.py:351
  49.1 9.4 %collective-permute-start.9 = (bf16[16,4096]{1,0:T(8,128)(2,1)S(1)}, bf16[16,4096]{1,0:T(8,128)(2,1)S(1)}, u32[]{:S(2)}, u32[]{:S(2)}) collective-permute-start(bf16[16,4096]{1,0:T(8,128)(2,1)S(1)} %slice.9), channel_id=1, source_target_pairs={{0,4},{1,3},{4,8},{5,1},{8,12},{9,5},{12,14},{13,9},{14,10},{15,13... | collective-permute-start | bytes 393224 | tf_op jit(solution)/shard_map/ppermute | solution.py:351
  54.7 6.4 %collective-permute-start.10 = (bf16[32,4096]{1,0:T(8,128)(2,1)S(1)}, bf16[32,4096]{1,0:T(8,128)(2,1)S(1)}, u32[]{:S(2)}, u32[]{:S(2)}) collective-permute-start(bf16[32,4096]{1,0:T(8,128)(2,1)S(1)} %collective-permute-done.6.refs_0_), channel_id=1, source_target_pairs={{0,4},{1,3},{4,8},{5,1},{8,12},{9,5},{12,14},{13,9},{14,10},{15,13... | collective-permute-start | bytes 786440 | tf_op jit(solution)/shard_map/ppermute | solution.py:351
  58.5 4.1 %collective-permute-start.13 = (bf16[176,256]{1,0:T(8,128)(2,1)S(1)}, bf16[176,256]{1,0:T(8,128)(2,1)S(1)}, u32[]{:S(2)}, u32[]{:S(2)}) collective-permute-start(bf16[176,256]{1,0:T(8,128)(2,1)S(1)} %get-tuple-element.28), channel_id=1, source_target_pairs={{0,1},{1,0},{2,3},{3,2},{4,5},{5,4},{6,7},{7,6},{8,9},{9,8},{10,11... | collective-permute-start | bytes 270344 | tf_op jit(solution)/shard_map/ppermute | solution.py:391
  62.5 1.3 %collective-permute-start.12 = (bf16[80,256]{1,0:T(8,128)(2,1)S(1)}, bf16[80,256]{1,0:T(8,128)(2,1)S(1)}, u32[]{:S(2)}, u32[]{:S(2)}) collective-permute-start(bf16[80,256]{1,0:T(8,128)(2,1)S(1)} %get-tuple-element.26), channel_id=1, source_target_pairs={{0,1},{1,0},{2,3},{3,2},{4,5},{5,4},{6,7},{7,6},{8,9},{9,8},{10,11... | collective-permute-start | bytes 122888 | tf_op jit(solution)/shard_map/ppermute | solution.py:393

commit v5 on v4

--- a/solution.py
+++ b/solution.py
@@ -226,47 +226,24 @@
     return found.reshape(docs, low * low)
 
 
-def score_kernel(*refs):
-    own_rows, other_rows, own_ref, other_ref = refs[-4:]
-    blocks = jnp.concatenate([ref[...] for ref in refs[:-4]], axis=0)
-    own_ref[...] = lax.dot_general(blocks, own_rows[...], LAST_DIMS, preferred_element_type=F32).astype(BF16)
-    other_ref[...] = lax.dot_general(blocks, other_rows[...], LAST_DIMS, preferred_element_type=F32).astype(BF16)
-
-
-def bring_and_score_kernel(*refs):
-    own_rows, other_hbm, own_ref, other_ref, kept_ref, sems = refs[-6:]
-    parts = sems.shape[0]
-    part = kept_ref.shape[1] // parts
-    places = [slice(i * part, (i + 1) * part) for i in range(parts)]
-    copies = [
-        pltpu.make_async_copy(other_hbm.at[:, pl.ds(i * part, part)], kept_ref.at[:, pl.ds(i * part, part)], sems.at[i])
-        for i in range(parts)
-    ]
-    for copy in copies:
-        copy.start()
-    blocks = jnp.concatenate([ref[...] for ref in refs[:-6]], axis=0)
-    own_ref[...] = lax.dot_general(blocks, own_rows[...], LAST_DIMS, preferred_element_type=F32).astype(BF16)
-    total = jnp.zeros(other_ref.shape, F32)
-    for at, copy in zip(places, copies):
-        copy.wait()
-        total += lax.dot_general(blocks[:, at], kept_ref[:, at], LAST_DIMS, preferred_element_type=F32)
-    other_ref[...] = total.astype(BF16)
-
-
-def scores_of(blocks, own_rows, other_rows, bring):
+def score_kernel(count, *refs):
+    sets, outs = refs[-2 * count : -count], refs[-count:]
+    blocks = jnp.concatenate([ref[...] for ref in refs[: -2 * count]], axis=0)
+    for rows, out in zip(sets, outs):
+        out[...] = lax.dot_general(blocks, rows[...], LAST_DIMS, preferred_element_type=F32).astype(BF16)
+
+
+def scores_of(blocks, *sets):
     count = sum(block.shape[0] for block in blocks)
-    shape = jax.ShapeDtypeStruct((count, own_rows.shape[0]), BF16)
     vmem = pl.BlockSpec(memory_space=pltpu.VMEM)
-    kept = [jax.ShapeDtypeStruct(other_rows.shape, BF16)] if bring else []
     return pl.pallas_call(
-        bring_and_score_kernel if bring else score_kernel,
-        out_shape=[shape, shape] + kept,
-        in_specs=[vmem] * (len(blocks) + 1) + [pl.BlockSpec(memory_space=pltpu.HBM) if bring else vmem],
-        out_specs=[vmem] * (2 + len(kept)),
-        scratch_shapes=[pltpu.SemaphoreType.DMA((4,))] if bring else [],
+        functools.partial(score_kernel, len(sets)),
+        out_shape=[jax.ShapeDtypeStruct((count, rows.shape[0]), BF16) for rows in sets],
+        in_specs=[vmem] * (len(blocks) + len(sets)),
+        out_specs=[vmem] * len(sets),
         cost_estimate=pl.CostEstimate(flops=SCORE_COST, bytes_accessed=2**20, transcendentals=0),
         compiler_params=pltpu.CompilerParams(vmem_limit_bytes=16 * 2**20),
-    )(*blocks, own_rows, other_rows)
+    )(*blocks, *sets)
 
 
 def order_kernel(owners, docs, places, *refs):
@@ -356,8 +333,7 @@
     first_own = queries_of(recv, 0, docs, low)
     first_next, first_second = ring_on(first_own), ring_on(first_own, second_next)
     first_given = lax.ppermute(first_own, "blk", swap)
-    recv, train_rows, first_own = lax.optimization_barrier((recv, train_rows, first_own))
-    other_rows = lax.ppermute(train_rows, "blk", swap)
+    recv, first_own = lax.optimization_barrier((recv, first_own))
     last_own = queries_of(recv, docs, docs, low)
     last_own, first_next, first_second, first_given = lax.optimization_barrier(
         (last_own, first_next, first_second, first_given)
@@ -365,33 +341,27 @@
     waiting = [first_own, last_own, first_next, first_second]
     lists = [(0, 0, 0), (1, 0, 0), (0, 1, 0), (0, 2, 0)]
     first = jnp.concatenate([first_second, first_given], axis=0)
-    last = jnp.concatenate([last_own, lax.ppermute(last_own, "blk", swap)], axis=0)
+    last_given = lax.ppermute(last_own, "blk", swap)
+    other_rows = lax.ppermute(lax.optimization_barrier((train_rows, last_given))[0], "blk", swap)
+    last = jnp.concatenate([last_own, last_given], axis=0)
     for hop in range(1, hops):
         near = hop < hops - 1
         first = ring_on(first if near else first[docs:])
-        if near:
-            waiting.append(first)
-            lists = lists + [(0, hop + 2, 0), (0, hop, 1)]
-        else:
-            most, most_lists, waiting, lists = waiting, lists, before, before_lists
-            waiting = waiting + [first]
-            lists = lists + [(0, hop, 1)]
+        arrived = [(0, hop + 2, 0), (0, hop, 1)] if near else [(0, hop, 1)]
         last = ring_on(last)
-        came, listed = [last], [(1, hop + 1, 0), (1, hop, 1)]
-        if hop == 1:
-            last_second = ring_on(last_own, second_next)
-            came, listed = [last, last_second], [(1, 1, 0), (1, 1, 1), (1, 2, 0)]
-            last = jnp.concatenate([last_second, last[docs:]], axis=0)
-        if hop == hops - 2:
-            before, before_lists = came, listed
-        else:
-            waiting = waiting + came
-            lists = lists + listed
-    own_most, other_most, other_rows = scores_of(most, train_rows, other_rows, True)
+        if hop == hops - 1:
+            most, most_lists, waiting, lists = waiting, lists, [], []
+        waiting = waiting + [first, last]
+        lists = lists + arrived + [(1, hop, 0), (1, hop, 1)]
+    waiting = waiting + [ring_on(last[:docs])]
+    lists = lists + [(1, hops, 0)]
+    own_most, other_most = scores_of(most, train_rows, other_rows)
     early = lax.ppermute(other_most, "blk", swap)
-    own_late, other_late = scores_of(waiting, train_rows, other_rows, False)
+    placed = put_in_order([(own_most, True, most_lists), (early, False, most_lists)], owners, docs, None)
+    waiting[-1], placed = lax.optimization_barrier((waiting[-1], placed))
+    (other_late,) = scores_of(waiting, other_rows)
     late = lax.ppermute(other_late, "blk", swap)
-    placed = put_in_order([(own_most, True, most_lists), (early, False, most_lists)], owners, docs, None)
+    (own_late,) = scores_of(waiting, train_rows)
     return put_in_order([(own_late, True, lists), (late, False, lists)], owners, docs, placed)
 
 

time: 64.9 us -> 63.7 us (0.982)
  Pallas kernels: 20.2 us -> 18.1 us
  starting transfers between devices: 11.3 us -> 12.3 us
    ppermute x9, waiting for transfers between devices: 13.4 us -> 11.1 us  [ring_on(): return lax.ppermute(block, 'blk', links)]
    pallas_call x2 -> x3, Pallas kernels: 5.11 us -> 3.05 us  [scores_of(): pl.pallas_call(functools.partial(score_kernel, len(sets)), out_shape=[jax...]
    ppermute x1, waiting for transfers between devices: 0.01 us -> 1.29 us  [gathered(): early = lax.ppermute(other_most, 'blk', swap)]
    ppermute x2, waiting for transfers between devices: 0.01 us -> 0.99 us  [the longest x1 0.99 us: gathered(): last_given = lax.ppermute(last_own, 'blk', swap)]
  transfers between devices with their start and end apart: 14 -> 14, of which waited for: 7 -> 8; matrix products, arithmetic and copies ran while one was open for 1% -> 1% of each run, Pallas kernels for 16% -> 12%
where the time goes in v5:
time: 63.7 us; the launch traced here: 63.5 us
  blocking collectives  18.5 us (29%)
  Pallas kernels  18.1 us (28%)
  waiting for transfers between devices  13.7 us (22%)
  starting transfers between devices  12.3 us (19%)
    all_to_all x1, blocking collectives, gathered(): recv = lax.all_to_all(send, 'blk', split_axis=0, concat_axis=0, tiled=True)  18.5 us
    ppermute x9, waiting for transfers between devices, ring_on(): return lax.ppermute(block, 'blk', links)  11.1 us
    ppermute x9, starting transfers between devices, ring_on(): return lax.ppermute(block, 'blk', links)  11.1 us
    pallas_call x2, Pallas kernels, queries_of(): pl.pallas_call(functools.partial(query_kernel, first_doc), out_shape=jax....  9.19 us
    pallas_call x1, Pallas kernels, packed_rows(): pl.pallas_call(pack_kernel, out_shape=jax.ShapeDtypeStruct((owners, cap +...  4.27 us
    pallas_call x3, Pallas kernels, scores_of(): pl.pallas_call(functools.partial(score_kernel, len(sets)), out_shape=[jax...  3.05 us
    pallas_call x2, Pallas kernels, put_in_order(): pl.pallas_call(kernel, out_shape=shape, in_specs=specs, out_specs=pl.Bloc...  1.56 us
    ppermute x1, waiting for transfers between devices, gathered(): early = lax.ppermute(other_most, 'blk', swap)  1.29 us
  transfers between devices with their start and end apart: 14, of which 8 were waited for; matrix products, arithmetic and copies ran while one was open for 1% of the time, Pallas kernels for 12%

profile of v5, /device:TPU:0, one launch (start us, length us, event | category | flops | bytes accessed | tf_op | source)
XLA Modules:
  0.0 63.5 jit_solution(12533723535297597787)
XLA Ops:
  0.0 4.3 %shard_map.73 = bf16[16,80,128]{2,1,0:T(8,128)(2,1)} custom-call(bf16[256,4096]{1,0:T(8,128)(2,1)} %inputs_hbm.1, bf16[256,4096]{1,0:T(8,128)(2,1)} %grads_hbm.1, bf16[64,4096]{1,0:T(8,128)(2,1)} %bitcast.4, bf16[64,4096]{1,0:T(8,128)(2,1)} %bitcast.5, s32[1,256]{1,0:T(1,128)} %bitcast.6, s32[1,256]{1,0:T(1,128)} %bitcast.7), custom_call_target="tpu_custom_call" | custom-call | tf_op jit(solution)/shard_map/pallas_call | solution.py:78
  4.3 18.5 %all_to_all.5.recv_ref = bf16[16,80,128]{2,1,0:T(8,128)(2,1)S(1)} all-to-all(bf16[16,80,128]{2,1,0:T(8,128)(2,1)} %shard_map.73), channel_id=1, replica_groups=mesh['groups'=2,'blk'=16] {'blk'}, dimensions={0} | all-to-all | bytes 655360 | tf_op jit(solution)/shard_map/all_to_all | solution.py:325
  22.8 4.6 %shard_map.74 = bf16[16,64,64]{2,1,0:T(8,128)(2,1)S(1)} custom-call(bf16[16,80,128]{2,1,0:T(8,128)(2,1)S(1)} %all_to_all.5.recv_ref), custom_call_target="tpu_custom_call" | custom-call | flops 4000000000 | bytes 1048576 | tf_op jit(solution)/shard_map/pallas_call | solution.py:213
  28.0 1.4 %collective-permute-start.1 = (bf16[16,4096]{1,0:T(8,128)(2,1)S(1)}, bf16[16,4096]{1,0:T(8,128)(2,1)S(1)}, u32[]{:S(2)}, u32[]{:S(2)}) collective-permute-start(bf16[16,4096]{1,0:T(8,128)(2,1)S(1)} %reshape.14.refs_0_), channel_id=1, source_target_pairs={{0,8},{1,7},{4,12},{5,3},{8,14},{9,1},{12,10},{13,5},{14,6},{15,9}... | collective-permute-start | bytes 393224 | tf_op jit(solution)/shard_map/ppermute | solution.py:328
  29.4 4.6 %shard_map.75 = bf16[16,64,64]{2,1,0:T(8,128)(2,1)S(1)} custom-call(bf16[16,80,128]{2,1,0:T(8,128)(2,1)S(1)} %all_to_all.5.recv_ref), custom_call_target="tpu_custom_call" | custom-call | flops 4000000000 | bytes 1048576 | tf_op jit(solution)/shard_map/pallas_call | solution.py:213
  34.9 1.0 %collective-permute-done.6 = bf16[16,4096]{1,0:T(8,128)(2,1)S(1)} collective-permute-done((bf16[16,4096]{1,0:T(8,128)(2,1)S(1)}, bf16[16,4096]{1,0:T(8,128)(2,1)S(1)}, u32[]{:S(2)}, u32[]{:S(2)}) %collective-permute-start.6) | collective-permute-done | bytes 131104 | tf_op jit(solution)/shard_map/ppermute | solution.py:344
  36.3 1.4 %collective-permute-start.7 = (bf16[32,4096]{1,0:T(8,128)(2,1)S(1)}, bf16[32,4096]{1,0:T(8,128)(2,1)S(1)}, u32[]{:S(2)}, u32[]{:S(2)}) collective-permute-start(bf16[32,4096]{1,0:T(8,128)(2,1)S(1)} %pad_maximum_fusion.1), channel_id=1, source_target_pairs={{0,4},{1,3},{4,8},{5,1},{8,12},{9,5},{12,14},{13,9},{14,10},{15,13... | collective-permute-start | bytes 786440 | tf_op jit(solution)/shard_map/ppermute | solution.py:328
  37.6 1.4 %collective-permute-start.3 = (bf16[32,4096]{1,0:T(8,128)(2,1)S(1)}, bf16[32,4096]{1,0:T(8,128)(2,1)S(1)}, u32[]{:S(2)}, u32[]{:S(2)}) collective-permute-start(bf16[32,4096]{1,0:T(8,128)(2,1)S(1)} %pad_maximum_fusion), channel_id=1, source_target_pairs={{0,4},{1,3},{4,8},{5,1},{8,12},{9,5},{12,14},{13,9},{14,10},{15,13... | collective-permute-start | bytes 786440 | tf_op jit(solution)/shard_map/ppermute | solution.py:328
  39.0 3.7 %collective-permute-done.7.refs_5_ = bf16[32,4096]{1,0:T(8,128)(2,1)S(1)} collective-permute-done((bf16[32,4096]{1,0:T(8,128)(2,1)S(1)}, bf16[32,4096]{1,0:T(8,128)(2,1)S(1)}, u32[]{:S(2)}, u32[]{:S(2)}) %collective-permute-start.7) | collective-permute-done | bytes 262176 | tf_op jit(solution)/shard_map/ppermute | solution.py:328
  42.7 1.3 %collective-permute-start.8 = (bf16[32,4096]{1,0:T(8,128)(2,1)S(1)}, bf16[32,4096]{1,0:T(8,128)(2,1)S(1)}, u32[]{:S(2)}, u32[]{:S(2)}) collective-permute-start(bf16[32,4096]{1,0:T(8,128)(2,1)S(1)} %collective-permute-done.7.refs_5_), channel_id=1, source_target_pairs={{0,4},{1,3},{4,8},{5,1},{8,12},{9,5},{12,14},{13,9},{14,10},{15,13... | collective-permute-start | bytes 786440 | tf_op jit(solution)/shard_map/ppermute | solution.py:328
  44.0 1.5 %collective-permute-done.3.refs_4_ = bf16[32,4096]{1,0:T(8,128)(2,1)S(1)} collective-permute-done((bf16[32,4096]{1,0:T(8,128)(2,1)S(1)}, bf16[32,4096]{1,0:T(8,128)(2,1)S(1)}, u32[]{:S(2)}, u32[]{:S(2)}) %collective-permute-start.3) | collective-permute-done | bytes 262176 | tf_op jit(solution)/shard_map/ppermute | solution.py:328
  45.5 1.3 %collective-permute-start.4 = (bf16[32,4096]{1,0:T(8,128)(2,1)S(1)}, bf16[32,4096]{1,0:T(8,128)(2,1)S(1)}, u32[]{:S(2)}, u32[]{:S(2)}) collective-permute-start(bf16[32,4096]{1,0:T(8,128)(2,1)S(1)} %collective-permute-done.3.refs_4_), channel_id=1, source_target_pairs={{0,4},{1,3},{4,8},{5,1},{8,12},{9,5},{12,14},{13,9},{14,10},{15,13... | collective-permute-start | bytes 786440 | tf_op jit(solution)/shard_map/ppermute | solution.py:328
  46.8 2.3 %collective-permute-done.8.refs_7_ = bf16[32,4096]{1,0:T(8,128)(2,1)S(1)} collective-permute-done((bf16[32,4096]{1,0:T(8,128)(2,1)S(1)}, bf16[32,4096]{1,0:T(8,128)(2,1)S(1)}, u32[]{:S(2)}, u32[]{:S(2)}) %collective-permute-start.8) | collective-permute-done | bytes 262176 | tf_op jit(solution)/shard_map/ppermute | solution.py:328
  49.1 1.3 %collective-permute-start.9 = (bf16[32,4096]{1,0:T(8,128)(2,1)S(1)}, bf16[32,4096]{1,0:T(8,128)(2,1)S(1)}, u32[]{:S(2)}, u32[]{:S(2)}) collective-permute-start(bf16[32,4096]{1,0:T(8,128)(2,1)S(1)} %collective-permute-done.8.refs_7_), channel_id=1, source_target_pairs={{0,4},{1,3},{4,8},{5,1},{8,12},{9,5},{12,14},{13,9},{14,10},{15,13... | collective-permute-start | bytes 786440 | tf_op jit(solution)/shard_map/ppermute | solution.py:328
  50.4 1.5 %collective-permute-done.4.refs_6_ = bf16[32,4096]{1,0:T(8,128)(2,1)S(1)} collective-permute-done((bf16[32,4096]{1,0:T(8,128)(2,1)S(1)}, bf16[32,4096]{1,0:T(8,128)(2,1)S(1)}, u32[]{:S(2)}, u32[]{:S(2)}) %collective-permute-start.4) | collective-permute-done | bytes 262176 | tf_op jit(solution)/shard_map/ppermute | solution.py:328
  51.9 1.4 %collective-permute-start.5 = (bf16[16,4096]{1,0:T(8,128)(2,1)S(1)}, bf16[16,4096]{1,0:T(8,128)(2,1)S(1)}, u32[]{:S(2)}, u32[]{:S(2)}) collective-permute-start(bf16[16,4096]{1,0:T(8,128)(2,1)S(1)} %slice.8), channel_id=1, source_target_pairs={{0,4},{1,3},{4,8},{5,1},{8,12},{9,5},{12,14},{13,9},{14,10},{15,13... | collective-permute-start | bytes 393224 | tf_op jit(solution)/shard_map/ppermute | solution.py:328
  53.2 2.2 %collective-permute-done.9.refs_1_ = bf16[32,4096]{1,0:T(8,128)(2,1)S(1)} collective-permute-done((bf16[32,4096]{1,0:T(8,128)(2,1)S(1)}, bf16[32,4096]{1,0:T(8,128)(2,1)S(1)}, u32[]{:S(2)}, u32[]{:S(2)}) %collective-permute-start.9) | collective-permute-done | bytes 262176 | tf_op jit(solution)/shard_map/ppermute | solution.py:328
  55.4 1.4 %collective-permute-start.10 = (bf16[16,4096]{1,0:T(8,128)(2,1)S(1)}, bf16[16,4096]{1,0:T(8,128)(2,1)S(1)}, u32[]{:S(2)}, u32[]{:S(2)}) collective-permute-start(bf16[16,4096]{1,0:T(8,128)(2,1)S(1)} %slice.9), channel_id=1, source_target_pairs={{0,4},{1,3},{4,8},{5,1},{8,12},{9,5},{12,14},{13,9},{14,10},{15,13... | collective-permute-start | bytes 393224 | tf_op jit(solution)/shard_map/ppermute | solution.py:328
  56.8 1.5 %shard_map.76 = (bf16[192,256]{1,0:T(8,128)(2,1)S(1)}, bf16[192,256]{1,0:T(8,128)(2,1)S(1)}) custom-call(bf16[16,4096]{1,0:T(8,128)(2,1)S(1)} %reshape.14.refs_0_, bf16[16,4096]{1,0:T(8,128)(2,1)S(1)} %reshape.15.refs_1_, bf16[16,4096]{1,0:T(8,128)(2,1)S(1)} %collective-permute-done.refs_2_, bf16[16,4096]{1,0:T(8,128)(2,1)S(1)} %collective-permute-done.1.refs_3_, ...), custom_call_target="tpu_custom_call" | custom-call | flops 6000000000 | bytes 1048576 | tf_op jit(solution)/shard_map/pallas_call | solution.py:239
  58.4 1.3 %collective-permute-done.12.refs_1_ = bf16[192,256]{1,0:T(8,128)(2,1)S(1)} collective-permute-done((bf16[192,256]{1,0:T(8,128)(2,1)S(1)}, bf16[192,256]{1,0:T(8,128)(2,1)S(1)}, u32[]{:S(2)}, u32[]{:S(2)}) %collective-permute-start.12) | collective-permute-done | bytes 98336 | tf_op jit(solution)/shard_map/ppermute | solution.py:359
  59.7 0.9 %shard_map.77.args_2_ = bf16[12,32,256]{2,1,0:T(8,128)(2,1)} custom-call(bf16[192,256]{1,0:T(8,128)(2,1)S(1)} %get-tuple-element.23.refs_0_, bf16[192,256]{1,0:T(8,128)(2,1)S(1)} %collective-permute-done.12.refs_1_), custom_call_target="tpu_custom_call" | custom-call | flops 1 | bytes 1 | tf_op jit(solution)/shard_map/pallas_call | solution.py:291
  60.6 0.8 %shard_map.79 = bf16[64,256]{1,0:T(8,128)(2,1)S(1)} custom-call(bf16[16,4096]{1,0:T(8,128)(2,1)S(1)} %collective-permute-done.5.refs_0_, bf16[32,4096]{1,0:T(8,128)(2,1)S(1)} %collective-permute-done.9.refs_1_, bf16[16,4096]{1,0:T(8,128)(2,1)S(1)} %collective-permute-done.10.refs_2_, bf16[256,4096]{1,0:T(8,128)(2,1)S(1)} %collective-permute-done.11.refs_9_.refs_3_), custom_call_target="tpu_custom_call" | custom-call | flops 6000000000 | bytes 1048576 | tf_op jit(solution)/shard_map/pallas_call | solution.py:239
  61.6 0.8 %shard_map.78.args_0_ = bf16[64,256]{1,0:T(8,128)(2,1)S(1)} custom-call(bf16[16,4096]{1,0:T(8,128)(2,1)S(1)} %collective-permute-done.5.refs_0_, bf16[32,4096]{1,0:T(8,128)(2,1)S(1)} %collective-permute-done.9.refs_1_, bf16[16,4096]{1,0:T(8,128)(2,1)S(1)} %collective-permute-done.10.refs_2_, bf16[256,4096]{1,0:T(8,128)(2,1)S(1)} %copy-done), custom_call_target="tpu_custom_call" | custom-call | flops 6000000000 | bytes 1048576 | tf_op jit(solution)/shard_map/pallas_call | solution.py:239
  62.6 0.7 %shard_map.80 = bf16[12,32,256]{2,1,0:T(8,128)(2,1)} custom-call(bf16[64,256]{1,0:T(8,128)(2,1)S(1)} %shard_map.78.args_0_, bf16[64,256]{1,0:T(8,128)(2,1)S(1)} %collective-permute-done.13.args_1_, bf16[12,32,256]{2,1,0:T(8,128)(2,1)} %shard_map.77.args_2_), custom_call_target="tpu_custom_call", output_to_operand_aliasing={{}: (2, {})} | custom-call | flops 1 | bytes 1 | tf_op jit(solution)/shard_map/pallas_call | solution.py:291
  (21 shorter events, 2.5 us)
Async XLA Ops:
  27.7 8.2 %copy-start = (bf16[256,4096]{1,0:T(8,128)(2,1)S(1)}, bf16[256,4096]{1,0:T(8,128)(2,1)}, u32[]{:S(2)}) copy-start(bf16[256,4096]{1,0:T(8,128)(2,1)} %refs_3_.1) | copy-start | bytes 6291460
  27.7 6.6 %collective-permute-start = (bf16[16,4096]{1,0:T(8,128)(2,1)S(1)}, bf16[16,4096]{1,0:T(8,128)(2,1)S(1)}, u32[]{:S(2)}, u32[]{:S(2)}) collective-permute-start(bf16[16,4096]{1,0:T(8,128)(2,1)S(1)} %reshape.14.refs_0_), channel_id=1, source_target_pairs={{0,4},{1,3},{4,8},{5,1},{8,12},{9,5},{12,14},{13,9},{14,10},{15,13... | collective-permute-start | bytes 393224 | tf_op jit(solution)/shard_map/ppermute | solution.py:328
  28.0 6.3 %collective-permute-start.1 = (bf16[16,4096]{1,0:T(8,128)(2,1)S(1)}, bf16[16,4096]{1,0:T(8,128)(2,1)S(1)}, u32[]{:S(2)}, u32[]{:S(2)}) collective-permute-start(bf16[16,4096]{1,0:T(8,128)(2,1)S(1)} %reshape.14.refs_0_), channel_id=1, source_target_pairs={{0,8},{1,7},{4,12},{5,3},{8,14},{9,1},{12,10},{13,5},{14,6},{15,9}... | collective-permute-start | bytes 393224 | tf_op jit(solution)/shard_map/ppermute | solution.py:328
  29.4 4.9 %collective-permute-start.2 = (bf16[16,4096]{1,0:T(8,128)(2,1)S(1)}, bf16[16,4096]{1,0:T(8,128)(2,1)S(1)}, u32[]{:S(2)}, u32[]{:S(2)}) collective-permute-start(bf16[16,4096]{1,0:T(8,128)(2,1)S(1)} %reshape.14.refs_0_), channel_id=1, source_target_pairs={{0,1},{1,0},{2,3},{3,2},{4,5},{5,4},{6,7},{7,6},{8,9},{9,8},{10,11... | collective-permute-start | bytes 393224 | tf_op jit(solution)/shard_map/ppermute | solution.py:335
  34.3 1.6 %collective-permute-start.6 = (bf16[16,4096]{1,0:T(8,128)(2,1)S(1)}, bf16[16,4096]{1,0:T(8,128)(2,1)S(1)}, u32[]{:S(2)}, u32[]{:S(2)}) collective-permute-start(bf16[16,4096]{1,0:T(8,128)(2,1)S(1)} %reshape.15.refs_1_), channel_id=1, source_target_pairs={{0,1},{1,0},{2,3},{3,2},{4,5},{5,4},{6,7},{7,6},{8,9},{9,8},{10,11... | collective-permute-start | bytes 393224 | tf_op jit(solution)/shard_map/ppermute | solution.py:344
  35.9 20.9 %collective-permute-start.11 = (bf16[256,4096]{1,0:T(8,128)(2,1)S(1)}, bf16[256,4096]{1,0:T(8,128)(2,1)S(1)}, u32[]{:S(2)}, u32[]{:S(2)}) collective-permute-start(bf16[256,4096]{1,0:T(8,128)(2,1)S(1)} %copy-done), channel_id=1, source_target_pairs={{0,1},{1,0},{2,3},{3,2},{4,5},{5,4},{6,7},{7,6},{8,9},{9,8},{10,11... | collective-permute-start | bytes 6291464 | tf_op jit(solution)/shard_map/ppermute | solution.py:345
  36.3 6.4 %collective-permute-start.7 = (bf16[32,4096]{1,0:T(8,128)(2,1)S(1)}, bf16[32,4096]{1,0:T(8,128)(2,1)S(1)}, u32[]{:S(2)}, u32[]{:S(2)}) collective-permute-start(bf16[32,4096]{1,0:T(8,128)(2,1)S(1)} %pad_maximum_fusion.1), channel_id=1, source_target_pairs={{0,4},{1,3},{4,8},{5,1},{8,12},{9,5},{12,14},{13,9},{14,10},{15,13... | collective-permute-start | bytes 786440 | tf_op jit(solution)/shard_map/ppermute | solution.py:328
  37.6 7.9 %collective-permute-start.3 = (bf16[32,4096]{1,0:T(8,128)(2,1)S(1)}, bf16[32,4096]{1,0:T(8,128)(2,1)S(1)}, u32[]{:S(2)}, u32[]{:S(2)}) collective-permute-start(bf16[32,4096]{1,0:T(8,128)(2,1)S(1)} %pad_maximum_fusion), channel_id=1, source_target_pairs={{0,4},{1,3},{4,8},{5,1},{8,12},{9,5},{12,14},{13,9},{14,10},{15,13... | collective-permute-start | bytes 786440 | tf_op jit(solution)/shard_map/ppermute | solution.py:328
  42.7 6.4 %collective-permute-start.8 = (bf16[32,4096]{1,0:T(8,128)(2,1)S(1)}, bf16[32,4096]{1,0:T(8,128)(2,1)S(1)}, u32[]{:S(2)}, u32[]{:S(2)}) collective-permute-start(bf16[32,4096]{1,0:T(8,128)(2,1)S(1)} %collective-permute-done.7.refs_5_), channel_id=1, source_target_pairs={{0,4},{1,3},{4,8},{5,1},{8,12},{9,5},{12,14},{13,9},{14,10},{15,13... | collective-permute-start | bytes 786440 | tf_op jit(solution)/shard_map/ppermute | solution.py:328
  45.5 6.4 %collective-permute-start.4 = (bf16[32,4096]{1,0:T(8,128)(2,1)S(1)}, bf16[32,4096]{1,0:T(8,128)(2,1)S(1)}, u32[]{:S(2)}, u32[]{:S(2)}) collective-permute-start(bf16[32,4096]{1,0:T(8,128)(2,1)S(1)} %collective-permute-done.3.refs_4_), channel_id=1, source_target_pairs={{0,4},{1,3},{4,8},{5,1},{8,12},{9,5},{12,14},{13,9},{14,10},{15,13... | collective-permute-start | bytes 786440 | tf_op jit(solution)/shard_map/ppermute | solution.py:328
  49.1 6.4 %collective-permute-start.9 = (bf16[32,4096]{1,0:T(8,128)(2,1)S(1)}, bf16[32,4096]{1,0:T(8,128)(2,1)S(1)}, u32[]{:S(2)}, u32[]{:S(2)}) collective-permute-start(bf16[32,4096]{1,0:T(8,128)(2,1)S(1)} %collective-permute-done.8.refs_7_), channel_id=1, source_target_pairs={{0,4},{1,3},{4,8},{5,1},{8,12},{9,5},{12,14},{13,9},{14,10},{15,13... | collective-permute-start | bytes 786440 | tf_op jit(solution)/shard_map/ppermute | solution.py:328
  51.9 8.7 %collective-permute-start.5 = (bf16[16,4096]{1,0:T(8,128)(2,1)S(1)}, bf16[16,4096]{1,0:T(8,128)(2,1)S(1)}, u32[]{:S(2)}, u32[]{:S(2)}) collective-permute-start(bf16[16,4096]{1,0:T(8,128)(2,1)S(1)} %slice.8), channel_id=1, source_target_pairs={{0,4},{1,3},{4,8},{5,1},{8,12},{9,5},{12,14},{13,9},{14,10},{15,13... | collective-permute-start | bytes 393224 | tf_op jit(solution)/shard_map/ppermute | solution.py:328
  55.4 5.1 %collective-permute-start.10 = (bf16[16,4096]{1,0:T(8,128)(2,1)S(1)}, bf16[16,4096]{1,0:T(8,128)(2,1)S(1)}, u32[]{:S(2)}, u32[]{:S(2)}) collective-permute-start(bf16[16,4096]{1,0:T(8,128)(2,1)S(1)} %slice.9), channel_id=1, source_target_pairs={{0,4},{1,3},{4,8},{5,1},{8,12},{9,5},{12,14},{13,9},{14,10},{15,13... | collective-permute-start | bytes 393224 | tf_op jit(solution)/shard_map/ppermute | solution.py:328
  58.3 1.4 %collective-permute-start.12 = (bf16[192,256]{1,0:T(8,128)(2,1)S(1)}, bf16[192,256]{1,0:T(8,128)(2,1)S(1)}, u32[]{:S(2)}, u32[]{:S(2)}) collective-permute-start(bf16[192,256]{1,0:T(8,128)(2,1)S(1)} %get-tuple-element.24), channel_id=1, source_target_pairs={{0,1},{1,0},{2,3},{3,2},{4,5},{5,4},{6,7},{7,6},{8,9},{9,8},{10,11... | collective-permute-start | bytes 294920 | tf_op jit(solution)/shard_map/ppermute | solution.py:359
  61.4 1.3 %collective-permute-start.13 = (bf16[64,256]{1,0:T(8,128)(2,1)S(1)}, bf16[64,256]{1,0:T(8,128)(2,1)S(1)}, u32[]{:S(2)}, u32[]{:S(2)}) collective-permute-start(bf16[64,256]{1,0:T(8,128)(2,1)S(1)} %shard_map.79), channel_id=1, source_target_pairs={{0,1},{1,0},{2,3},{3,2},{4,5},{5,4},{6,7},{7,6},{8,9},{9,8},{10,11... | collective-permute-start | bytes 98312 | tf_op jit(solution)/shard_map/ppermute | solution.py:363

commit v6 on v5

--- a/solution.py
+++ b/solution.py
@@ -324,30 +324,25 @@
     send = packed_rows(query_inputs, query_grads, proj_in, proj_out, token_owner, token_slot, owners, cap)
     recv = lax.all_to_all(send, "blk", split_axis=0, concat_axis=0, tiled=True)
 
-    def ring_on(block, links=ring):
-        return lax.ppermute(block, "blk", links)
-
-    following = dict(ring)
-    second_next = [(device, following[step]) for device, step in ring]
+    def ring_on(block):
+        return lax.ppermute(block, "blk", ring)
 
     first_own = queries_of(recv, 0, docs, low)
-    first_next, first_second = ring_on(first_own), ring_on(first_own, second_next)
+    first_next = ring_on(first_own)
     first_given = lax.ppermute(first_own, "blk", swap)
     recv, first_own = lax.optimization_barrier((recv, first_own))
     last_own = queries_of(recv, docs, docs, low)
-    last_own, first_next, first_second, first_given = lax.optimization_barrier(
-        (last_own, first_next, first_second, first_given)
-    )
-    waiting = [first_own, last_own, first_next, first_second]
-    lists = [(0, 0, 0), (1, 0, 0), (0, 1, 0), (0, 2, 0)]
-    first = jnp.concatenate([first_second, first_given], axis=0)
+    last_own, first_next, first_given = lax.optimization_barrier((last_own, first_next, first_given))
+    waiting = [first_own, last_own, first_next]
+    lists = [(0, 0, 0), (1, 0, 0), (0, 1, 0)]
+    first = jnp.concatenate([first_next, first_given], axis=0)
     last_given = lax.ppermute(last_own, "blk", swap)
     other_rows = lax.ppermute(lax.optimization_barrier((train_rows, last_given))[0], "blk", swap)
     last = jnp.concatenate([last_own, last_given], axis=0)
     for hop in range(1, hops):
         near = hop < hops - 1
-        first = ring_on(first if near else first[docs:])
-        arrived = [(0, hop + 2, 0), (0, hop, 1)] if near else [(0, hop, 1)]
+        first = ring_on(first)
+        arrived = [(0, hop + 1, 0), (0, hop, 1)]
         last = ring_on(last)
         if hop == hops - 1:
             most, most_lists, waiting, lists = waiting, lists, [], []

time: 63.7 us -> 62.7 us (0.984)
  waiting for transfers between devices: 13.7 us -> 12.8 us
    ppermute x9 -> x8, waiting for transfers between devices: 11.1 us -> 10.1 us  [ring_on(): return lax.ppermute(block, 'blk', ring)]
    ppermute x9 -> x8, starting transfers between devices: 11.1 us -> 11.1 us  [ring_on(): return lax.ppermute(block, 'blk', ring)]
  transfers between devices with their start and end apart: 14 -> 13, of which waited for: 8 -> 8; matrix products, arithmetic and copies ran while one was open for 1% -> 1% of each run, Pallas kernels for 12% -> 12%
where the time goes in v6:
time: 62.7 us; the launch traced here: 62.5 us
  blocking collectives  18.5 us (30%)
  Pallas kernels  18.1 us (29%)
  waiting for transfers between devices  12.8 us (20%)
  starting transfers between devices  12.2 us (19%)
    all_to_all x1, blocking collectives, gathered(): recv = lax.all_to_all(send, 'blk', split_axis=0, concat_axis=0, tiled=True)  18.5 us
    ppermute x8, starting transfers between devices, ring_on(): return lax.ppermute(block, 'blk', ring)  11.1 us
    ppermute x8, waiting for transfers between devices, ring_on(): return lax.ppermute(block, 'blk', ring)  10.1 us
    pallas_call x2, Pallas kernels, queries_of(): pl.pallas_call(functools.partial(query_kernel, first_doc), out_shape=jax....  9.19 us
    pallas_call x1, Pallas kernels, packed_rows(): pl.pallas_call(pack_kernel, out_shape=jax.ShapeDtypeStruct((owners, cap +...  4.28 us
    pallas_call x3, Pallas kernels, scores_of(): pl.pallas_call(functools.partial(score_kernel, len(sets)), out_shape=[jax...  3.07 us
    pallas_call x2, Pallas kernels, put_in_order(): pl.pallas_call(kernel, out_shape=shape, in_specs=specs, out_specs=pl.Bloc...  1.56 us
    ppermute x1, waiting for transfers between devices, gathered(): early = lax.ppermute(other_most, 'blk', swap)  1.28 us
  transfers between devices with their start and end apart: 13, of which 8 were waited for; matrix products, arithmetic and copies ran while one was open for 1% of the time, Pallas kernels for 12%

profile of v6, /device:TPU:0, one launch (start us, length us, event | category | flops | bytes accessed | tf_op | source)
XLA Modules:
  0.0 62.5 jit_solution(339470633351204976)
XLA Ops:
  0.0 4.3 %shard_map.73 = bf16[16,80,128]{2,1,0:T(8,128)(2,1)} custom-call(bf16[256,4096]{1,0:T(8,128)(2,1)} %inputs_hbm.1, bf16[256,4096]{1,0:T(8,128)(2,1)} %grads_hbm.1, bf16[64,4096]{1,0:T(8,128)(2,1)} %bitcast.4, bf16[64,4096]{1,0:T(8,128)(2,1)} %bitcast.5, s32[1,256]{1,0:T(1,128)} %bitcast.6, s32[1,256]{1,0:T(1,128)} %bitcast.7), custom_call_target="tpu_custom_call" | custom-call | tf_op jit(solution)/shard_map/pallas_call | solution.py:78
  4.3 18.5 %all_to_all.5.recv_ref = bf16[16,80,128]{2,1,0:T(8,128)(2,1)S(1)} all-to-all(bf16[16,80,128]{2,1,0:T(8,128)(2,1)} %shard_map.73), channel_id=1, replica_groups=mesh['groups'=2,'blk'=16] {'blk'}, dimensions={0} | all-to-all | bytes 655360 | tf_op jit(solution)/shard_map/all_to_all | solution.py:325
  22.8 4.6 %shard_map.74 = bf16[16,64,64]{2,1,0:T(8,128)(2,1)S(1)} custom-call(bf16[16,80,128]{2,1,0:T(8,128)(2,1)S(1)} %all_to_all.5.recv_ref), custom_call_target="tpu_custom_call" | custom-call | flops 4000000000 | bytes 1048576 | tf_op jit(solution)/shard_map/pallas_call | solution.py:213
  28.2 4.6 %shard_map.75 = bf16[16,64,64]{2,1,0:T(8,128)(2,1)S(1)} custom-call(bf16[16,80,128]{2,1,0:T(8,128)(2,1)S(1)} %all_to_all.5.recv_ref), custom_call_target="tpu_custom_call" | custom-call | flops 4000000000 | bytes 1048576 | tf_op jit(solution)/shard_map/pallas_call | solution.py:213
  33.1 0.3 collective-permute-start.5
  33.5 1.1 %collective-permute-done.5 = bf16[16,4096]{1,0:T(8,128)(2,1)S(1)} collective-permute-done((bf16[16,4096]{1,0:T(8,128)(2,1)S(1)}, bf16[16,4096]{1,0:T(8,128)(2,1)S(1)}, u32[]{:S(2)}, u32[]{:S(2)}) %collective-permute-start.5) | collective-permute-done | bytes 131104 | tf_op jit(solution)/shard_map/ppermute | solution.py:339
  34.8 1.7 %collective-permute-start.6 = (bf16[32,4096]{1,0:T(8,128)(2,1)S(1)}, bf16[32,4096]{1,0:T(8,128)(2,1)S(1)}, u32[]{:S(2)}, u32[]{:S(2)}) collective-permute-start(bf16[32,4096]{1,0:T(8,128)(2,1)S(1)} %pad_maximum_fusion.1), channel_id=1, source_target_pairs={{0,4},{1,3},{4,8},{5,1},{8,12},{9,5},{12,14},{13,9},{14,10},{15,13... | collective-permute-start | bytes 786440 | tf_op jit(solution)/shard_map/ppermute | solution.py:328
  36.6 0.5 collective-permute-start.2
  37.1 4.2 %collective-permute-done.6.refs_4_ = bf16[32,4096]{1,0:T(8,128)(2,1)S(1)} collective-permute-done((bf16[32,4096]{1,0:T(8,128)(2,1)S(1)}, bf16[32,4096]{1,0:T(8,128)(2,1)S(1)}, u32[]{:S(2)}, u32[]{:S(2)}) %collective-permute-start.6) | collective-permute-done | bytes 262176 | tf_op jit(solution)/shard_map/ppermute | solution.py:328
  41.3 1.7 %collective-permute-start.7 = (bf16[32,4096]{1,0:T(8,128)(2,1)S(1)}, bf16[32,4096]{1,0:T(8,128)(2,1)S(1)}, u32[]{:S(2)}, u32[]{:S(2)}) collective-permute-start(bf16[32,4096]{1,0:T(8,128)(2,1)S(1)} %collective-permute-done.6.refs_4_), channel_id=1, source_target_pairs={{0,4},{1,3},{4,8},{5,1},{8,12},{9,5},{12,14},{13,9},{14,10},{15,13... | collective-permute-start | bytes 786440 | tf_op jit(solution)/shard_map/ppermute | solution.py:328
  43.0 1.1 %collective-permute-done.2.refs_3_ = bf16[32,4096]{1,0:T(8,128)(2,1)S(1)} collective-permute-done((bf16[32,4096]{1,0:T(8,128)(2,1)S(1)}, bf16[32,4096]{1,0:T(8,128)(2,1)S(1)}, u32[]{:S(2)}, u32[]{:S(2)}) %collective-permute-start.2) | collective-permute-done | bytes 262176 | tf_op jit(solution)/shard_map/ppermute | solution.py:328
  44.1 1.7 %collective-permute-start.3 = (bf16[32,4096]{1,0:T(8,128)(2,1)S(1)}, bf16[32,4096]{1,0:T(8,128)(2,1)S(1)}, u32[]{:S(2)}, u32[]{:S(2)}) collective-permute-start(bf16[32,4096]{1,0:T(8,128)(2,1)S(1)} %collective-permute-done.2.refs_3_), channel_id=1, source_target_pairs={{0,4},{1,3},{4,8},{5,1},{8,12},{9,5},{12,14},{13,9},{14,10},{15,13... | collective-permute-start | bytes 786440 | tf_op jit(solution)/shard_map/ppermute | solution.py:328
  45.8 1.9 %collective-permute-done.7.refs_6_ = bf16[32,4096]{1,0:T(8,128)(2,1)S(1)} collective-permute-done((bf16[32,4096]{1,0:T(8,128)(2,1)S(1)}, bf16[32,4096]{1,0:T(8,128)(2,1)S(1)}, u32[]{:S(2)}, u32[]{:S(2)}) %collective-permute-start.7) | collective-permute-done | bytes 262176 | tf_op jit(solution)/shard_map/ppermute | solution.py:328
  47.6 1.7 %collective-permute-start.8 = (bf16[32,4096]{1,0:T(8,128)(2,1)S(1)}, bf16[32,4096]{1,0:T(8,128)(2,1)S(1)}, u32[]{:S(2)}, u32[]{:S(2)}) collective-permute-start(bf16[32,4096]{1,0:T(8,128)(2,1)S(1)} %collective-permute-done.7.refs_6_), channel_id=1, source_target_pairs={{0,4},{1,3},{4,8},{5,1},{8,12},{9,5},{12,14},{13,9},{14,10},{15,13... | collective-permute-start | bytes 786440 | tf_op jit(solution)/shard_map/ppermute | solution.py:328
  49.3 1.1 %collective-permute-done.3.refs_5_ = bf16[32,4096]{1,0:T(8,128)(2,1)S(1)} collective-permute-done((bf16[32,4096]{1,0:T(8,128)(2,1)S(1)}, bf16[32,4096]{1,0:T(8,128)(2,1)S(1)}, u32[]{:S(2)}, u32[]{:S(2)}) %collective-permute-start.3) | collective-permute-done | bytes 262176 | tf_op jit(solution)/shard_map/ppermute | solution.py:328
  50.5 1.7 %collective-permute-start.4 = (bf16[32,4096]{1,0:T(8,128)(2,1)S(1)}, bf16[32,4096]{1,0:T(8,128)(2,1)S(1)}, u32[]{:S(2)}, u32[]{:S(2)}) collective-permute-start(bf16[32,4096]{1,0:T(8,128)(2,1)S(1)} %collective-permute-done.3.refs_5_), channel_id=1, source_target_pairs={{0,4},{1,3},{4,8},{5,1},{8,12},{9,5},{12,14},{13,9},{14,10},{15,13... | collective-permute-start | bytes 786440 | tf_op jit(solution)/shard_map/ppermute | solution.py:328
  52.1 1.9 %collective-permute-done.8.refs_1_ = bf16[32,4096]{1,0:T(8,128)(2,1)S(1)} collective-permute-done((bf16[32,4096]{1,0:T(8,128)(2,1)S(1)}, bf16[32,4096]{1,0:T(8,128)(2,1)S(1)}, u32[]{:S(2)}, u32[]{:S(2)}) %collective-permute-start.8) | collective-permute-done | bytes 262176 | tf_op jit(solution)/shard_map/ppermute | solution.py:328
  54.0 1.7 %collective-permute-start.9 = (bf16[16,4096]{1,0:T(8,128)(2,1)S(1)}, bf16[16,4096]{1,0:T(8,128)(2,1)S(1)}, u32[]{:S(2)}, u32[]{:S(2)}) collective-permute-start(bf16[16,4096]{1,0:T(8,128)(2,1)S(1)} %slice.4), channel_id=1, source_target_pairs={{0,4},{1,3},{4,8},{5,1},{8,12},{9,5},{12,14},{13,9},{14,10},{15,13... | collective-permute-start | bytes 393224 | tf_op jit(solution)/shard_map/ppermute | solution.py:328
  55.8 1.5 %shard_map.76 = (bf16[176,256]{1,0:T(8,128)(2,1)S(1)}, bf16[176,256]{1,0:T(8,128)(2,1)S(1)}) custom-call(bf16[16,4096]{1,0:T(8,128)(2,1)S(1)} %reshape.14.refs_0_, bf16[16,4096]{1,0:T(8,128)(2,1)S(1)} %reshape.15.refs_1_, bf16[16,4096]{1,0:T(8,128)(2,1)S(1)} %collective-permute-done.refs_2_, bf16[32,4096]{1,0:T(8,128)(2,1)S(1)} %collective-permute-done.2.refs_3_, ...), custom_call_target="tpu_custom_call" | custom-call | flops 6000000000 | bytes 1048576 | tf_op jit(solution)/shard_map/pallas_call | solution.py:239
  57.4 1.3 %collective-permute-done.11.refs_1_ = bf16[176,256]{1,0:T(8,128)(2,1)S(1)} collective-permute-done((bf16[176,256]{1,0:T(8,128)(2,1)S(1)}, bf16[176,256]{1,0:T(8,128)(2,1)S(1)}, u32[]{:S(2)}, u32[]{:S(2)}) %collective-permute-start.11) | collective-permute-done | bytes 90144 | tf_op jit(solution)/shard_map/ppermute | solution.py:354
  58.7 0.8 %shard_map.77.args_2_ = bf16[12,32,256]{2,1,0:T(8,128)(2,1)} custom-call(bf16[176,256]{1,0:T(8,128)(2,1)S(1)} %get-tuple-element.21.refs_0_, bf16[176,256]{1,0:T(8,128)(2,1)S(1)} %collective-permute-done.11.refs_1_), custom_call_target="tpu_custom_call" | custom-call | flops 1 | bytes 1 | tf_op jit(solution)/shard_map/pallas_call | solution.py:291
  59.6 0.8 %shard_map.79 = bf16[80,256]{1,0:T(8,128)(2,1)S(1)} custom-call(bf16[32,4096]{1,0:T(8,128)(2,1)S(1)} %collective-permute-done.4.refs_0_, bf16[32,4096]{1,0:T(8,128)(2,1)S(1)} %collective-permute-done.8.refs_1_, bf16[16,4096]{1,0:T(8,128)(2,1)S(1)} %collective-permute-done.9.refs_2_, bf16[256,4096]{1,0:T(8,128)(2,1)S(1)} %collective-permute-done.10.refs_8_.refs_3_), custom_call_target="tpu_custom_call" | custom-call | flops 6000000000 | bytes 1048576 | tf_op jit(solution)/shard_map/pallas_call | solution.py:239
  60.5 0.8 %shard_map.78.args_0_ = bf16[80,256]{1,0:T(8,128)(2,1)S(1)} custom-call(bf16[32,4096]{1,0:T(8,128)(2,1)S(1)} %collective-permute-done.4.refs_0_, bf16[32,4096]{1,0:T(8,128)(2,1)S(1)} %collective-permute-done.8.refs_1_, bf16[16,4096]{1,0:T(8,128)(2,1)S(1)} %collective-permute-done.9.refs_2_, bf16[256,4096]{1,0:T(8,128)(2,1)S(1)} %copy-done), custom_call_target="tpu_custom_call" | custom-call | flops 6000000000 | bytes 1048576 | tf_op jit(solution)/shard_map/pallas_call | solution.py:239
  61.6 0.7 %shard_map.80 = bf16[12,32,256]{2,1,0:T(8,128)(2,1)} custom-call(bf16[80,256]{1,0:T(8,128)(2,1)S(1)} %shard_map.78.args_0_, bf16[80,256]{1,0:T(8,128)(2,1)S(1)} %collective-permute-done.12.args_1_, bf16[12,32,256]{2,1,0:T(8,128)(2,1)} %shard_map.77.args_2_), custom_call_target="tpu_custom_call", output_to_operand_aliasing={{}: (2, {})} | custom-call | flops 1 | bytes 1 | tf_op jit(solution)/shard_map/pallas_call | solution.py:291
  (18 shorter events, 2.0 us)
Async XLA Ops:
  27.7 6.9 %copy-start = (bf16[256,4096]{1,0:T(8,128)(2,1)S(1)}, bf16[256,4096]{1,0:T(8,128)(2,1)}, u32[]{:S(2)}) copy-start(bf16[256,4096]{1,0:T(8,128)(2,1)} %refs_3_.1) | copy-start | bytes 6291460
  27.7 5.4 %collective-permute-start = (bf16[16,4096]{1,0:T(8,128)(2,1)S(1)}, bf16[16,4096]{1,0:T(8,128)(2,1)S(1)}, u32[]{:S(2)}, u32[]{:S(2)}) collective-permute-start(bf16[16,4096]{1,0:T(8,128)(2,1)S(1)} %reshape.14.refs_0_), channel_id=1, source_target_pairs={{0,4},{1,3},{4,8},{5,1},{8,12},{9,5},{12,14},{13,9},{14,10},{15,13... | collective-permute-start | bytes 393224 | tf_op jit(solution)/shard_map/ppermute | solution.py:328
  28.0 5.1 %collective-permute-start.1 = (bf16[16,4096]{1,0:T(8,128)(2,1)S(1)}, bf16[16,4096]{1,0:T(8,128)(2,1)S(1)}, u32[]{:S(2)}, u32[]{:S(2)}) collective-permute-start(bf16[16,4096]{1,0:T(8,128)(2,1)S(1)} %reshape.14.refs_0_), channel_id=1, source_target_pairs={{0,1},{1,0},{2,3},{3,2},{4,5},{5,4},{6,7},{7,6},{8,9},{9,8},{10,11... | collective-permute-start | bytes 393224 | tf_op jit(solution)/shard_map/ppermute | solution.py:332
  33.1 1.4 %collective-permute-start.5 = (bf16[16,4096]{1,0:T(8,128)(2,1)S(1)}, bf16[16,4096]{1,0:T(8,128)(2,1)S(1)}, u32[]{:S(2)}, u32[]{:S(2)}) collective-permute-start(bf16[16,4096]{1,0:T(8,128)(2,1)S(1)} %reshape.15.refs_1_), channel_id=1, source_target_pairs={{0,1},{1,0},{2,3},{3,2},{4,5},{5,4},{6,7},{7,6},{8,9},{9,8},{10,11... | collective-permute-start | bytes 393224 | tf_op jit(solution)/shard_map/ppermute | solution.py:339
  34.5 21.2 %collective-permute-start.10 = (bf16[256,4096]{1,0:T(8,128)(2,1)S(1)}, bf16[256,4096]{1,0:T(8,128)(2,1)S(1)}, u32[]{:S(2)}, u32[]{:S(2)}) collective-permute-start(bf16[256,4096]{1,0:T(8,128)(2,1)S(1)} %copy-done), channel_id=1, source_target_pairs={{0,1},{1,0},{2,3},{3,2},{4,5},{5,4},{6,7},{7,6},{8,9},{9,8},{10,11... | collective-permute-start | bytes 6291464 | tf_op jit(solution)/shard_map/ppermute | solution.py:340
  34.8 6.4 %collective-permute-start.6 = (bf16[32,4096]{1,0:T(8,128)(2,1)S(1)}, bf16[32,4096]{1,0:T(8,128)(2,1)S(1)}, u32[]{:S(2)}, u32[]{:S(2)}) collective-permute-start(bf16[32,4096]{1,0:T(8,128)(2,1)S(1)} %pad_maximum_fusion.1), channel_id=1, source_target_pairs={{0,4},{1,3},{4,8},{5,1},{8,12},{9,5},{12,14},{13,9},{14,10},{15,13... | collective-permute-start | bytes 786440 | tf_op jit(solution)/shard_map/ppermute | solution.py:328
  36.6 7.5 %collective-permute-start.2 = (bf16[32,4096]{1,0:T(8,128)(2,1)S(1)}, bf16[32,4096]{1,0:T(8,128)(2,1)S(1)}, u32[]{:S(2)}, u32[]{:S(2)}) collective-permute-start(bf16[32,4096]{1,0:T(8,128)(2,1)S(1)} %pad_maximum_fusion), channel_id=1, source_target_pairs={{0,4},{1,3},{4,8},{5,1},{8,12},{9,5},{12,14},{13,9},{14,10},{15,13... | collective-permute-start | bytes 786440 | tf_op jit(solution)/shard_map/ppermute | solution.py:328
  41.3 6.4 %collective-permute-start.7 = (bf16[32,4096]{1,0:T(8,128)(2,1)S(1)}, bf16[32,4096]{1,0:T(8,128)(2,1)S(1)}, u32[]{:S(2)}, u32[]{:S(2)}) collective-permute-start(bf16[32,4096]{1,0:T(8,128)(2,1)S(1)} %collective-permute-done.6.refs_4_), channel_id=1, source_target_pairs={{0,4},{1,3},{4,8},{5,1},{8,12},{9,5},{12,14},{13,9},{14,10},{15,13... | collective-permute-start | bytes 786440 | tf_op jit(solution)/shard_map/ppermute | solution.py:328
  44.1 6.4 %collective-permute-start.3 = (bf16[32,4096]{1,0:T(8,128)(2,1)S(1)}, bf16[32,4096]{1,0:T(8,128)(2,1)S(1)}, u32[]{:S(2)}, u32[]{:S(2)}) collective-permute-start(bf16[32,4096]{1,0:T(8,128)(2,1)S(1)} %collective-permute-done.2.refs_3_), channel_id=1, source_target_pairs={{0,4},{1,3},{4,8},{5,1},{8,12},{9,5},{12,14},{13,9},{14,10},{15,13... | collective-permute-start | bytes 786440 | tf_op jit(solution)/shard_map/ppermute | solution.py:328
  47.6 6.4 %collective-permute-start.8 = (bf16[32,4096]{1,0:T(8,128)(2,1)S(1)}, bf16[32,4096]{1,0:T(8,128)(2,1)S(1)}, u32[]{:S(2)}, u32[]{:S(2)}) collective-permute-start(bf16[32,4096]{1,0:T(8,128)(2,1)S(1)} %collective-permute-done.7.refs_6_), channel_id=1, source_target_pairs={{0,4},{1,3},{4,8},{5,1},{8,12},{9,5},{12,14},{13,9},{14,10},{15,13... | collective-permute-start | bytes 786440 | tf_op jit(solution)/shard_map/ppermute | solution.py:328
  50.5 9.1 %collective-permute-start.4 = (bf16[32,4096]{1,0:T(8,128)(2,1)S(1)}, bf16[32,4096]{1,0:T(8,128)(2,1)S(1)}, u32[]{:S(2)}, u32[]{:S(2)}) collective-permute-start(bf16[32,4096]{1,0:T(8,128)(2,1)S(1)} %collective-permute-done.3.refs_5_), channel_id=1, source_target_pairs={{0,4},{1,3},{4,8},{5,1},{8,12},{9,5},{12,14},{13,9},{14,10},{15,13... | collective-permute-start | bytes 786440 | tf_op jit(solution)/shard_map/ppermute | solution.py:328
  54.0 5.5 %collective-permute-start.9 = (bf16[16,4096]{1,0:T(8,128)(2,1)S(1)}, bf16[16,4096]{1,0:T(8,128)(2,1)S(1)}, u32[]{:S(2)}, u32[]{:S(2)}) collective-permute-start(bf16[16,4096]{1,0:T(8,128)(2,1)S(1)} %slice.4), channel_id=1, source_target_pairs={{0,4},{1,3},{4,8},{5,1},{8,12},{9,5},{12,14},{13,9},{14,10},{15,13... | collective-permute-start | bytes 393224 | tf_op jit(solution)/shard_map/ppermute | solution.py:328
  57.3 1.4 %collective-permute-start.11 = (bf16[176,256]{1,0:T(8,128)(2,1)S(1)}, bf16[176,256]{1,0:T(8,128)(2,1)S(1)}, u32[]{:S(2)}, u32[]{:S(2)}) collective-permute-start(bf16[176,256]{1,0:T(8,128)(2,1)S(1)} %get-tuple-element.22), channel_id=1, source_target_pairs={{0,1},{1,0},{2,3},{3,2},{4,5},{5,4},{6,7},{7,6},{8,9},{9,8},{10,11... | collective-permute-start | bytes 270344 | tf_op jit(solution)/shard_map/ppermute | solution.py:354
  60.3 1.3 %collective-permute-start.12 = (bf16[80,256]{1,0:T(8,128)(2,1)S(1)}, bf16[80,256]{1,0:T(8,128)(2,1)S(1)}, u32[]{:S(2)}, u32[]{:S(2)}) collective-permute-start(bf16[80,256]{1,0:T(8,128)(2,1)S(1)} %shard_map.79), channel_id=1, source_target_pairs={{0,1},{1,0},{2,3},{3,2},{4,5},{5,4},{6,7},{7,6},{8,9},{9,8},{10,11... | collective-permute-start | bytes 122888 | tf_op jit(solution)/shard_map/ppermute | solution.py:358

commit v7 on v6

--- a/solution.py
+++ b/solution.py
@@ -337,19 +337,19 @@
     lists = [(0, 0, 0), (1, 0, 0), (0, 1, 0)]
     first = jnp.concatenate([first_next, first_given], axis=0)
     last_given = lax.ppermute(last_own, "blk", swap)
-    other_rows = lax.ppermute(lax.optimization_barrier((train_rows, last_given))[0], "blk", swap)
-    last = jnp.concatenate([last_own, last_given], axis=0)
+    other_rows = lax.ppermute(lax.optimization_barrier((train_rows, last_own))[0], "blk", swap)
+    last = last_own
     for hop in range(1, hops):
         near = hop < hops - 1
         first = ring_on(first)
         arrived = [(0, hop + 1, 0), (0, hop, 1)]
-        last = ring_on(last)
+        last = ring_on(jnp.concatenate([last, last_given], axis=0) if hop == 2 else last)
         if hop == hops - 1:
             most, most_lists, waiting, lists = waiting, lists, [], []
         waiting = waiting + [first, last]
-        lists = lists + arrived + [(1, hop, 0), (1, hop, 1)]
-    waiting = waiting + [ring_on(last[:docs])]
-    lists = lists + [(1, hops, 0)]
+        lists = lists + arrived + [(1, hop, 0)] + ([(1, hop - 1, 1)] if hop > 1 else [])
+    waiting = waiting + [ring_on(last)]
+    lists = lists + [(1, hops, 0), (1, hops - 1, 1)]
     own_most, other_most = scores_of(most, train_rows, other_rows)
     early = lax.ppermute(other_most, "blk", swap)
     placed = put_in_order([(own_most, True, most_lists), (early, False, most_lists)], owners, docs, None)

time: 62.7 us -> 60.8 us (0.970)
  starting transfers between devices: 12.2 us -> 11 us
  waiting for transfers between devices: 12.8 us -> 12.1 us
    ppermute x1, waiting for transfers between devices: 1.07 us -> 0.01 us  [gathered(): last_given = lax.ppermute(last_own, 'blk', swap)]
    ppermute x8, starting transfers between devices: 11.1 us -> 10.3 us  [ring_on(): return lax.ppermute(block, 'blk', ring)]
  transfers between devices with their start and end apart: 13 -> 13, of which waited for: 8 -> 8; matrix products, arithmetic and copies ran while one was open for 1% -> 1% of each run, Pallas kernels for 12% -> 13%
where the time goes in v7:
time: 60.8 us; the launch traced here: 60.6 us
  blocking collectives  18.5 us (30%)
  Pallas kernels  18.1 us (30%)
  waiting for transfers between devices  12.1 us (20%)
  starting transfers between devices  11 us (18%)
    all_to_all x1, blocking collectives, gathered(): recv = lax.all_to_all(send, 'blk', split_axis=0, concat_axis=0, tiled=True)  18.5 us
    ppermute x8, waiting for transfers between devices, ring_on(): return lax.ppermute(block, 'blk', ring)  10.4 us
    ppermute x8, starting transfers between devices, ring_on(): return lax.ppermute(block, 'blk', ring)  10.3 us
    pallas_call x2, Pallas kernels, queries_of(): pl.pallas_call(functools.partial(query_kernel, first_doc), out_shape=jax....  9.19 us
    pallas_call x1, Pallas kernels, packed_rows(): pl.pallas_call(pack_kernel, out_shape=jax.ShapeDtypeStruct((owners, cap +...  4.28 us
    pallas_call x3, Pallas kernels, scores_of(): pl.pallas_call(functools.partial(score_kernel, len(sets)), out_shape=[jax...  3.09 us
    pallas_call x2, Pallas kernels, put_in_order(): pl.pallas_call(kernel, out_shape=shape, in_specs=specs, out_specs=pl.Bloc...  1.56 us
    ppermute x1, waiting for transfers between devices, gathered(): early = lax.ppermute(other_most, 'blk', swap)  1.26 us
  transfers between devices with their start and end apart: 13, of which 8 were waited for; matrix products, arithmetic and copies ran while one was open for 1% of the time, Pallas kernels for 13%

profile of v7, /device:TPU:0, one launch (start us, length us, event | category | flops | bytes accessed | tf_op | source)
XLA Modules:
  0.0 60.6 jit_solution(4329744196570238965)
XLA Ops:
  0.0 4.3 %shard_map.73 = bf16[16,80,128]{2,1,0:T(8,128)(2,1)} custom-call(bf16[256,4096]{1,0:T(8,128)(2,1)} %inputs_hbm.1, bf16[256,4096]{1,0:T(8,128)(2,1)} %grads_hbm.1, bf16[64,4096]{1,0:T(8,128)(2,1)} %bitcast.4, bf16[64,4096]{1,0:T(8,128)(2,1)} %bitcast.5, s32[1,256]{1,0:T(1,128)} %bitcast.6, s32[1,256]{1,0:T(1,128)} %bitcast.7), custom_call_target="tpu_custom_call" | custom-call | tf_op jit(solution)/shard_map/pallas_call | solution.py:78
  4.3 18.5 %all_to_all.5.recv_ref = bf16[16,80,128]{2,1,0:T(8,128)(2,1)S(1)} all-to-all(bf16[16,80,128]{2,1,0:T(8,128)(2,1)} %shard_map.73), channel_id=1, replica_groups=mesh['groups'=2,'blk'=16] {'blk'}, dimensions={0} | all-to-all | bytes 655360 | tf_op jit(solution)/shard_map/all_to_all | solution.py:325
  22.8 4.6 %shard_map.74 = bf16[16,64,64]{2,1,0:T(8,128)(2,1)S(1)} custom-call(bf16[16,80,128]{2,1,0:T(8,128)(2,1)S(1)} %all_to_all.5.recv_ref), custom_call_target="tpu_custom_call" | custom-call | flops 4000000000 | bytes 1048576 | tf_op jit(solution)/shard_map/pallas_call | solution.py:213
  28.2 4.6 %shard_map.75 = bf16[16,64,64]{2,1,0:T(8,128)(2,1)S(1)} custom-call(bf16[16,80,128]{2,1,0:T(8,128)(2,1)S(1)} %all_to_all.5.recv_ref), custom_call_target="tpu_custom_call" | custom-call | flops 4000000000 | bytes 1048576 | tf_op jit(solution)/shard_map/pallas_call | solution.py:213
  33.5 1.7 %collective-permute-start.5 = (bf16[16,4096]{1,0:T(8,128)(2,1)S(1)}, bf16[16,4096]{1,0:T(8,128)(2,1)S(1)}, u32[]{:S(2)}, u32[]{:S(2)}) collective-permute-start(bf16[16,4096]{1,0:T(8,128)(2,1)S(1)} %reshape.15.refs_1_), channel_id=1, source_target_pairs={{0,4},{1,3},{4,8},{5,1},{8,12},{9,5},{12,14},{13,9},{14,10},{15,13... | collective-permute-start | bytes 393224 | tf_op jit(solution)/shard_map/ppermute | solution.py:328
  35.2 0.4 collective-permute-start.2
  35.6 2.9 %collective-permute-done.5.refs_4_ = bf16[16,4096]{1,0:T(8,128)(2,1)S(1)} collective-permute-done((bf16[16,4096]{1,0:T(8,128)(2,1)S(1)}, bf16[16,4096]{1,0:T(8,128)(2,1)S(1)}, u32[]{:S(2)}, u32[]{:S(2)}) %collective-permute-start.5) | collective-permute-done | bytes 131104 | tf_op jit(solution)/shard_map/ppermute | solution.py:328
  38.5 1.7 %collective-permute-start.7 = (bf16[32,4096]{1,0:T(8,128)(2,1)S(1)}, bf16[32,4096]{1,0:T(8,128)(2,1)S(1)}, u32[]{:S(2)}, u32[]{:S(2)}) collective-permute-start(bf16[32,4096]{1,0:T(8,128)(2,1)S(1)} %pad_maximum_fusion.1), channel_id=1, source_target_pairs={{0,4},{1,3},{4,8},{5,1},{8,12},{9,5},{12,14},{13,9},{14,10},{15,13... | collective-permute-start | bytes 786440 | tf_op jit(solution)/shard_map/ppermute | solution.py:328
  40.2 1.4 %collective-permute-done.2.refs_3_ = bf16[32,4096]{1,0:T(8,128)(2,1)S(1)} collective-permute-done((bf16[32,4096]{1,0:T(8,128)(2,1)S(1)}, bf16[32,4096]{1,0:T(8,128)(2,1)S(1)}, u32[]{:S(2)}, u32[]{:S(2)}) %collective-permute-start.2) | collective-permute-done | bytes 262176 | tf_op jit(solution)/shard_map/ppermute | solution.py:328
  41.6 1.3 %collective-permute-start.3 = (bf16[32,4096]{1,0:T(8,128)(2,1)S(1)}, bf16[32,4096]{1,0:T(8,128)(2,1)S(1)}, u32[]{:S(2)}, u32[]{:S(2)}) collective-permute-start(bf16[32,4096]{1,0:T(8,128)(2,1)S(1)} %collective-permute-done.2.refs_3_), channel_id=1, source_target_pairs={{0,4},{1,3},{4,8},{5,1},{8,12},{9,5},{12,14},{13,9},{14,10},{15,13... | collective-permute-start | bytes 786440 | tf_op jit(solution)/shard_map/ppermute | solution.py:328
  43.0 1.9 %collective-permute-done.7.refs_6_ = bf16[32,4096]{1,0:T(8,128)(2,1)S(1)} collective-permute-done((bf16[32,4096]{1,0:T(8,128)(2,1)S(1)}, bf16[32,4096]{1,0:T(8,128)(2,1)S(1)}, u32[]{:S(2)}, u32[]{:S(2)}) %collective-permute-start.7) | collective-permute-done | bytes 262176 | tf_op jit(solution)/shard_map/ppermute | solution.py:328
  44.9 1.7 %collective-permute-start.8 = (bf16[32,4096]{1,0:T(8,128)(2,1)S(1)}, bf16[32,4096]{1,0:T(8,128)(2,1)S(1)}, u32[]{:S(2)}, u32[]{:S(2)}) collective-permute-start(bf16[32,4096]{1,0:T(8,128)(2,1)S(1)} %collective-permute-done.7.refs_6_), channel_id=1, source_target_pairs={{0,4},{1,3},{4,8},{5,1},{8,12},{9,5},{12,14},{13,9},{14,10},{15,13... | collective-permute-start | bytes 786440 | tf_op jit(solution)/shard_map/ppermute | solution.py:328
  46.6 1.4 %collective-permute-done.3.refs_5_ = bf16[32,4096]{1,0:T(8,128)(2,1)S(1)} collective-permute-done((bf16[32,4096]{1,0:T(8,128)(2,1)S(1)}, bf16[32,4096]{1,0:T(8,128)(2,1)S(1)}, u32[]{:S(2)}, u32[]{:S(2)}) %collective-permute-start.3) | collective-permute-done | bytes 262176 | tf_op jit(solution)/shard_map/ppermute | solution.py:328
  48.0 1.4 %collective-permute-start.4 = (bf16[32,4096]{1,0:T(8,128)(2,1)S(1)}, bf16[32,4096]{1,0:T(8,128)(2,1)S(1)}, u32[]{:S(2)}, u32[]{:S(2)}) collective-permute-start(bf16[32,4096]{1,0:T(8,128)(2,1)S(1)} %collective-permute-done.3.refs_5_), channel_id=1, source_target_pairs={{0,4},{1,3},{4,8},{5,1},{8,12},{9,5},{12,14},{13,9},{14,10},{15,13... | collective-permute-start | bytes 786440 | tf_op jit(solution)/shard_map/ppermute | solution.py:328
  49.4 1.9 %collective-permute-done.8.refs_1_ = bf16[32,4096]{1,0:T(8,128)(2,1)S(1)} collective-permute-done((bf16[32,4096]{1,0:T(8,128)(2,1)S(1)}, bf16[32,4096]{1,0:T(8,128)(2,1)S(1)}, u32[]{:S(2)}, u32[]{:S(2)}) %collective-permute-start.8) | collective-permute-done | bytes 262176 | tf_op jit(solution)/shard_map/ppermute | solution.py:328
  51.3 1.7 %collective-permute-start.9 = (bf16[32,4096]{1,0:T(8,128)(2,1)S(1)}, bf16[32,4096]{1,0:T(8,128)(2,1)S(1)}, u32[]{:S(2)}, u32[]{:S(2)}) collective-permute-start(bf16[32,4096]{1,0:T(8,128)(2,1)S(1)} %collective-permute-done.8.refs_1_), channel_id=1, source_target_pairs={{0,4},{1,3},{4,8},{5,1},{8,12},{9,5},{12,14},{13,9},{14,10},{15,13... | collective-permute-start | bytes 786440 | tf_op jit(solution)/shard_map/ppermute | solution.py:328
  53.0 1.5 %shard_map.76 = (bf16[160,256]{1,0:T(8,128)(2,1)S(1)}, bf16[160,256]{1,0:T(8,128)(2,1)S(1)}) custom-call(bf16[16,4096]{1,0:T(8,128)(2,1)S(1)} %reshape.14.refs_0_, bf16[16,4096]{1,0:T(8,128)(2,1)S(1)} %reshape.15.refs_1_, bf16[16,4096]{1,0:T(8,128)(2,1)S(1)} %collective-permute-done.refs_2_, bf16[32,4096]{1,0:T(8,128)(2,1)S(1)} %collective-permute-done.2.refs_3_, ...), custom_call_target="tpu_custom_call" | custom-call | flops 6000000000 | bytes 1048576 | tf_op jit(solution)/shard_map/pallas_call | solution.py:239
  54.6 1.3 %collective-permute-done.11.refs_1_ = bf16[160,256]{1,0:T(8,128)(2,1)S(1)} collective-permute-done((bf16[160,256]{1,0:T(8,128)(2,1)S(1)}, bf16[160,256]{1,0:T(8,128)(2,1)S(1)}, u32[]{:S(2)}, u32[]{:S(2)}) %collective-permute-start.11) | collective-permute-done | bytes 81952 | tf_op jit(solution)/shard_map/ppermute | solution.py:354
  55.9 0.8 %shard_map.77.args_2_ = bf16[12,32,256]{2,1,0:T(8,128)(2,1)} custom-call(bf16[160,256]{1,0:T(8,128)(2,1)S(1)} %get-tuple-element.21.refs_0_, bf16[160,256]{1,0:T(8,128)(2,1)S(1)} %collective-permute-done.11.refs_1_), custom_call_target="tpu_custom_call" | custom-call | flops 1 | bytes 1 | tf_op jit(solution)/shard_map/pallas_call | solution.py:291
  56.7 1.0 %collective-permute-done.9.refs_2_ = bf16[32,4096]{1,0:T(8,128)(2,1)S(1)} collective-permute-done((bf16[32,4096]{1,0:T(8,128)(2,1)S(1)}, bf16[32,4096]{1,0:T(8,128)(2,1)S(1)}, u32[]{:S(2)}, u32[]{:S(2)}) %collective-permute-start.9) | collective-permute-done | bytes 262176 | tf_op jit(solution)/shard_map/ppermute | solution.py:328
  57.6 0.8 %shard_map.79 = bf16[96,256]{1,0:T(8,128)(2,1)S(1)} custom-call(bf16[32,4096]{1,0:T(8,128)(2,1)S(1)} %collective-permute-done.4.refs_0_, bf16[32,4096]{1,0:T(8,128)(2,1)S(1)} %collective-permute-done.8.refs_1_, bf16[32,4096]{1,0:T(8,128)(2,1)S(1)} %collective-permute-done.9.refs_2_, bf16[256,4096]{1,0:T(8,128)(2,1)S(1)} %collective-permute-done.10.refs_8_.refs_3_), custom_call_target="tpu_custom_call" | custom-call | flops 6000000000 | bytes 1048576 | tf_op jit(solution)/shard_map/pallas_call | solution.py:239
  58.5 0.8 %shard_map.78.args_0_ = bf16[96,256]{1,0:T(8,128)(2,1)S(1)} custom-call(bf16[32,4096]{1,0:T(8,128)(2,1)S(1)} %collective-permute-done.4.refs_0_, bf16[32,4096]{1,0:T(8,128)(2,1)S(1)} %collective-permute-done.8.refs_1_, bf16[32,4096]{1,0:T(8,128)(2,1)S(1)} %collective-permute-done.9.refs_2_, bf16[256,4096]{1,0:T(8,128)(2,1)S(1)} %copy-done), custom_call_target="tpu_custom_call" | custom-call | flops 6000000000 | bytes 1048576 | tf_op jit(solution)/shard_map/pallas_call | solution.py:239
  59.3 0.4 collective-permute-done.12.args_1_
  59.7 0.7 %shard_map.80 = bf16[12,32,256]{2,1,0:T(8,128)(2,1)} custom-call(bf16[96,256]{1,0:T(8,128)(2,1)S(1)} %shard_map.78.args_0_, bf16[96,256]{1,0:T(8,128)(2,1)S(1)} %collective-permute-done.12.args_1_, bf16[12,32,256]{2,1,0:T(8,128)(2,1)} %shard_map.77.args_2_), custom_call_target="tpu_custom_call", output_to_operand_aliasing={{}: (2, {})} | custom-call | flops 1 | bytes 1 | tf_op jit(solution)/shard_map/pallas_call | solution.py:291
  (17 shorter events, 1.6 us)
Async XLA Ops:
  27.7 5.5 %copy-start = (bf16[256,4096]{1,0:T(8,128)(2,1)S(1)}, bf16[256,4096]{1,0:T(8,128)(2,1)}, u32[]{:S(2)}) copy-start(bf16[256,4096]{1,0:T(8,128)(2,1)} %refs_3_.1) | copy-start | bytes 6291460
  27.7 5.4 %collective-permute-start = (bf16[16,4096]{1,0:T(8,128)(2,1)S(1)}, bf16[16,4096]{1,0:T(8,128)(2,1)S(1)}, u32[]{:S(2)}, u32[]{:S(2)}) collective-permute-start(bf16[16,4096]{1,0:T(8,128)(2,1)S(1)} %reshape.14.refs_0_), channel_id=1, source_target_pairs={{0,4},{1,3},{4,8},{5,1},{8,12},{9,5},{12,14},{13,9},{14,10},{15,13... | collective-permute-start | bytes 393224 | tf_op jit(solution)/shard_map/ppermute | solution.py:328
  28.0 5.1 %collective-permute-start.1 = (bf16[16,4096]{1,0:T(8,128)(2,1)S(1)}, bf16[16,4096]{1,0:T(8,128)(2,1)S(1)}, u32[]{:S(2)}, u32[]{:S(2)}) collective-permute-start(bf16[16,4096]{1,0:T(8,128)(2,1)S(1)} %reshape.14.refs_0_), channel_id=1, source_target_pairs={{0,1},{1,0},{2,3},{3,2},{4,5},{5,4},{6,7},{7,6},{8,9},{9,8},{10,11... | collective-permute-start | bytes 393224 | tf_op jit(solution)/shard_map/ppermute | solution.py:332
  33.1 19.8 %collective-permute-start.10 = (bf16[256,4096]{1,0:T(8,128)(2,1)S(1)}, bf16[256,4096]{1,0:T(8,128)(2,1)S(1)}, u32[]{:S(2)}, u32[]{:S(2)}) collective-permute-start(bf16[256,4096]{1,0:T(8,128)(2,1)S(1)} %copy-done), channel_id=1, source_target_pairs={{0,1},{1,0},{2,3},{3,2},{4,5},{5,4},{6,7},{7,6},{8,9},{9,8},{10,11... | collective-permute-start | bytes 6291464 | tf_op jit(solution)/shard_map/ppermute | solution.py:340
  33.5 5.0 %collective-permute-start.5 = (bf16[16,4096]{1,0:T(8,128)(2,1)S(1)}, bf16[16,4096]{1,0:T(8,128)(2,1)S(1)}, u32[]{:S(2)}, u32[]{:S(2)}) collective-permute-start(bf16[16,4096]{1,0:T(8,128)(2,1)S(1)} %reshape.15.refs_1_), channel_id=1, source_target_pairs={{0,4},{1,3},{4,8},{5,1},{8,12},{9,5},{12,14},{13,9},{14,10},{15,13... | collective-permute-start | bytes 393224 | tf_op jit(solution)/shard_map/ppermute | solution.py:328
  35.2 3.3 %collective-permute-start.6 = (bf16[16,4096]{1,0:T(8,128)(2,1)S(1)}, bf16[16,4096]{1,0:T(8,128)(2,1)S(1)}, u32[]{:S(2)}, u32[]{:S(2)}) collective-permute-start(bf16[16,4096]{1,0:T(8,128)(2,1)S(1)} %reshape.15.refs_1_), channel_id=1, source_target_pairs={{0,1},{1,0},{2,3},{3,2},{4,5},{5,4},{6,7},{7,6},{8,9},{9,8},{10,11... | collective-permute-start | bytes 393224 | tf_op jit(solution)/shard_map/ppermute | solution.py:339
  35.2 6.4 %collective-permute-start.2 = (bf16[32,4096]{1,0:T(8,128)(2,1)S(1)}, bf16[32,4096]{1,0:T(8,128)(2,1)S(1)}, u32[]{:S(2)}, u32[]{:S(2)}) collective-permute-start(bf16[32,4096]{1,0:T(8,128)(2,1)S(1)} %pad_maximum_fusion), channel_id=1, source_target_pairs={{0,4},{1,3},{4,8},{5,1},{8,12},{9,5},{12,14},{13,9},{14,10},{15,13... | collective-permute-start | bytes 786440 | tf_op jit(solution)/shard_map/ppermute | solution.py:328
  38.5 6.4 %collective-permute-start.7 = (bf16[32,4096]{1,0:T(8,128)(2,1)S(1)}, bf16[32,4096]{1,0:T(8,128)(2,1)S(1)}, u32[]{:S(2)}, u32[]{:S(2)}) collective-permute-start(bf16[32,4096]{1,0:T(8,128)(2,1)S(1)} %pad_maximum_fusion.1), channel_id=1, source_target_pairs={{0,4},{1,3},{4,8},{5,1},{8,12},{9,5},{12,14},{13,9},{14,10},{15,13... | collective-permute-start | bytes 786440 | tf_op jit(solution)/shard_map/ppermute | solution.py:328
  41.6 6.4 %collective-permute-start.3 = (bf16[32,4096]{1,0:T(8,128)(2,1)S(1)}, bf16[32,4096]{1,0:T(8,128)(2,1)S(1)}, u32[]{:S(2)}, u32[]{:S(2)}) collective-permute-start(bf16[32,4096]{1,0:T(8,128)(2,1)S(1)} %collective-permute-done.2.refs_3_), channel_id=1, source_target_pairs={{0,4},{1,3},{4,8},{5,1},{8,12},{9,5},{12,14},{13,9},{14,10},{15,13... | collective-permute-start | bytes 786440 | tf_op jit(solution)/shard_map/ppermute | solution.py:328
  44.9 6.4 %collective-permute-start.8 = (bf16[32,4096]{1,0:T(8,128)(2,1)S(1)}, bf16[32,4096]{1,0:T(8,128)(2,1)S(1)}, u32[]{:S(2)}, u32[]{:S(2)}) collective-permute-start(bf16[32,4096]{1,0:T(8,128)(2,1)S(1)} %collective-permute-done.7.refs_6_), channel_id=1, source_target_pairs={{0,4},{1,3},{4,8},{5,1},{8,12},{9,5},{12,14},{13,9},{14,10},{15,13... | collective-permute-start | bytes 786440 | tf_op jit(solution)/shard_map/ppermute | solution.py:328
  48.0 9.6 %collective-permute-start.4 = (bf16[32,4096]{1,0:T(8,128)(2,1)S(1)}, bf16[32,4096]{1,0:T(8,128)(2,1)S(1)}, u32[]{:S(2)}, u32[]{:S(2)}) collective-permute-start(bf16[32,4096]{1,0:T(8,128)(2,1)S(1)} %collective-permute-done.3.refs_5_), channel_id=1, source_target_pairs={{0,4},{1,3},{4,8},{5,1},{8,12},{9,5},{12,14},{13,9},{14,10},{15,13... | collective-permute-start | bytes 786440 | tf_op jit(solution)/shard_map/ppermute | solution.py:328
  51.3 6.4 %collective-permute-start.9 = (bf16[32,4096]{1,0:T(8,128)(2,1)S(1)}, bf16[32,4096]{1,0:T(8,128)(2,1)S(1)}, u32[]{:S(2)}, u32[]{:S(2)}) collective-permute-start(bf16[32,4096]{1,0:T(8,128)(2,1)S(1)} %collective-permute-done.8.refs_1_), channel_id=1, source_target_pairs={{0,4},{1,3},{4,8},{5,1},{8,12},{9,5},{12,14},{13,9},{14,10},{15,13... | collective-permute-start | bytes 786440 | tf_op jit(solution)/shard_map/ppermute | solution.py:328
  54.5 1.3 %collective-permute-start.11 = (bf16[160,256]{1,0:T(8,128)(2,1)S(1)}, bf16[160,256]{1,0:T(8,128)(2,1)S(1)}, u32[]{:S(2)}, u32[]{:S(2)}) collective-permute-start(bf16[160,256]{1,0:T(8,128)(2,1)S(1)} %get-tuple-element.22), channel_id=1, source_target_pairs={{0,1},{1,0},{2,3},{3,2},{4,5},{5,4},{6,7},{7,6},{8,9},{9,8},{10,11... | collective-permute-start | bytes 245768 | tf_op jit(solution)/shard_map/ppermute | solution.py:354
  58.4 1.3 %collective-permute-start.12 = (bf16[96,256]{1,0:T(8,128)(2,1)S(1)}, bf16[96,256]{1,0:T(8,128)(2,1)S(1)}, u32[]{:S(2)}, u32[]{:S(2)}) collective-permute-start(bf16[96,256]{1,0:T(8,128)(2,1)S(1)} %shard_map.79), channel_id=1, source_target_pairs={{0,1},{1,0},{2,3},{3,2},{4,5},{5,4},{6,7},{7,6},{8,9},{9,8},{10,11... | collective-permute-start | bytes 147464 | tf_op jit(solution)/shard_map/ppermute | solution.py:358

commit v8 on v7

--- a/solution.py
+++ b/solution.py
@@ -138,9 +138,10 @@
     return out
 
 
-def query_kernel(first_doc, recv_ref, out_ref, gram_ref, rows_ref, count_ref):
-    docs, low, _ = out_ref.shape
+def query_kernel(first_doc, recv_ref, out_ref, gram_ref, rows_ref, count_ref, query_ref):
+    docs = out_ref.shape[0]
     sources, per, wide = recv_ref.shape
+    low = wide // 2
     cap = per - TAIL
     rows = jnp.concatenate([recv_ref[s, :cap, :] for s in range(sources)], axis=0)
     rows_ref[...] = rows.T
@@ -204,26 +205,30 @@
         tilted.append(times(total, right))
     found = [times(tilt, on_diagonal(total, 3)) for tilt, total in zip(tilted, totals)]
     for g, query in enumerate(found):
-        out_ref[2 * g] = query[:, low:wide].astype(BF16)
-        out_ref[2 * g + 1] = query[:, wide + low :].astype(BF16)
+        query_ref[2 * g * low : (2 * g + 1) * low, :] = query[:, :wide]
+        query_ref[(2 * g + 1) * low : (2 * g + 2) * low, :] = query[:, wide:]
+    for a in range(0, low, 2):
+        even = pltpu.roll(query_ref[pl.ds(a, docs, stride=low), :], low, 1)
+        after = query_ref[pl.ds(a + 1, docs, stride=low), :]
+        out_ref[:, a * low : (a + 2) * low] = jnp.where(half, even, after).astype(BF16)
 
 
 def queries_of(recv, first_doc, docs, low):
     sources, per, wide = recv.shape
-    found = pl.pallas_call(
+    return pl.pallas_call(
         functools.partial(query_kernel, first_doc),
-        out_shape=jax.ShapeDtypeStruct((docs, low, low), BF16),
+        out_shape=jax.ShapeDtypeStruct((docs, low * low), BF16),
         in_specs=[pl.BlockSpec(memory_space=pltpu.VMEM)],
         out_specs=pl.BlockSpec(memory_space=pltpu.VMEM),
         scratch_shapes=[
             pltpu.VMEM((docs, wide, wide), F32),
             pltpu.VMEM((wide, sources * (per - TAIL)), BF16),
             pltpu.VMEM((docs, wide), F32),
+            pltpu.VMEM((docs * low, wide), F32),
         ],
         cost_estimate=pl.CostEstimate(flops=4 * 10**9, bytes_accessed=2**20, transcendentals=0),
         compiler_params=pltpu.CompilerParams(vmem_limit_bytes=16 * 2**20),
     )(recv)
-    return found.reshape(docs, low * low)
 
 
 def score_kernel(count, *refs):

time: 60.8 us -> 60.6 us (level)
  transfers between devices with their start and end apart: 13 -> 13, of which waited for: 8 -> 8; matrix products, arithmetic and copies ran while one was open for 1% -> 0% of each run, Pallas kernels for 13% -> 13%
where the time goes in v8:
time: 60.6 us; the launch traced here: 60.4 us
  Pallas kernels  18.5 us (31%)
  blocking collectives  18.5 us (31%)
  waiting for transfers between devices  12.1 us (20%)
  starting transfers between devices  11 us (18%)
    all_to_all x1, blocking collectives, gathered(): recv = lax.all_to_all(send, 'blk', split_axis=0, concat_axis=0, tiled=True)  18.5 us
    ppermute x8, waiting for transfers between devices, ring_on(): return lax.ppermute(block, 'blk', ring)  10.4 us
    ppermute x8, starting transfers between devices, ring_on(): return lax.ppermute(block, 'blk', ring)  10.3 us
    pallas_call x2, Pallas kernels, queries_of(): pl.pallas_call(functools.partial(query_kernel, first_doc), out_shape=jax....  9.54 us
    pallas_call x1, Pallas kernels, packed_rows(): pl.pallas_call(pack_kernel, out_shape=jax.ShapeDtypeStruct((owners, cap +...  4.28 us
    pallas_call x3, Pallas kernels, scores_of(): pl.pallas_call(functools.partial(score_kernel, len(sets)), out_shape=[jax...  3.09 us
    pallas_call x2, Pallas kernels, put_in_order(): pl.pallas_call(kernel, out_shape=shape, in_specs=specs, out_specs=pl.Bloc...  1.56 us
    ppermute x1, waiting for transfers between devices, gathered(): early = lax.ppermute(other_most, 'blk', swap)  1.26 us
  transfers between devices with their start and end apart: 13, of which 8 were waited for; matrix products, arithmetic and copies ran while one was open for 0% of the time, Pallas kernels for 13%

profile of v8, /device:TPU:0, one launch (start us, length us, event | category | flops | bytes accessed | tf_op | source)
XLA Modules:
  0.0 60.4 jit_solution(10403029505259122020)
XLA Ops:
  0.0 4.3 %shard_map.73 = bf16[16,80,128]{2,1,0:T(8,128)(2,1)} custom-call(bf16[256,4096]{1,0:T(8,128)(2,1)} %inputs_hbm.1, bf16[256,4096]{1,0:T(8,128)(2,1)} %grads_hbm.1, bf16[64,4096]{1,0:T(8,128)(2,1)} %bitcast.4, bf16[64,4096]{1,0:T(8,128)(2,1)} %bitcast.5, s32[1,256]{1,0:T(1,128)} %bitcast.6, s32[1,256]{1,0:T(1,128)} %bitcast.7), custom_call_target="tpu_custom_call" | custom-call | tf_op jit(solution)/shard_map/pallas_call | solution.py:78
  4.3 18.5 %all_to_all.5.recv_ref = bf16[16,80,128]{2,1,0:T(8,128)(2,1)S(1)} all-to-all(bf16[16,80,128]{2,1,0:T(8,128)(2,1)} %shard_map.73), channel_id=1, replica_groups=mesh['groups'=2,'blk'=16] {'blk'}, dimensions={0} | all-to-all | bytes 655360 | tf_op jit(solution)/shard_map/all_to_all | solution.py:330
  22.8 4.8 %shard_map.74.refs_0_ = bf16[16,4096]{1,0:T(8,128)(2,1)S(1)} custom-call(bf16[16,80,128]{2,1,0:T(8,128)(2,1)S(1)} %all_to_all.5.recv_ref), custom_call_target="tpu_custom_call" | custom-call | flops 4000000000 | bytes 1048576 | tf_op jit(solution)/shard_map/pallas_call | solution.py:218
  28.1 4.8 %shard_map.75.refs_1_ = bf16[16,4096]{1,0:T(8,128)(2,1)S(1)} custom-call(bf16[16,80,128]{2,1,0:T(8,128)(2,1)S(1)} %all_to_all.5.recv_ref), custom_call_target="tpu_custom_call" | custom-call | flops 4000000000 | bytes 1048576 | tf_op jit(solution)/shard_map/pallas_call | solution.py:218
  33.3 1.7 %collective-permute-start.5 = (bf16[16,4096]{1,0:T(8,128)(2,1)S(1)}, bf16[16,4096]{1,0:T(8,128)(2,1)S(1)}, u32[]{:S(2)}, u32[]{:S(2)}) collective-permute-start(bf16[16,4096]{1,0:T(8,128)(2,1)S(1)} %shard_map.75.refs_1_), channel_id=1, source_target_pairs={{0,4},{1,3},{4,8},{5,1},{8,12},{9,5},{12,14},{13,9},{14,10},{15,13... | collective-permute-start | bytes 393224 | tf_op jit(solution)/shard_map/ppermute | solution.py:333
  35.0 0.4 collective-permute-start.2
  35.4 2.9 %collective-permute-done.5.refs_4_ = bf16[16,4096]{1,0:T(8,128)(2,1)S(1)} collective-permute-done((bf16[16,4096]{1,0:T(8,128)(2,1)S(1)}, bf16[16,4096]{1,0:T(8,128)(2,1)S(1)}, u32[]{:S(2)}, u32[]{:S(2)}) %collective-permute-start.5) | collective-permute-done | bytes 131104 | tf_op jit(solution)/shard_map/ppermute | solution.py:333
  38.3 1.7 %collective-permute-start.7 = (bf16[32,4096]{1,0:T(8,128)(2,1)S(1)}, bf16[32,4096]{1,0:T(8,128)(2,1)S(1)}, u32[]{:S(2)}, u32[]{:S(2)}) collective-permute-start(bf16[32,4096]{1,0:T(8,128)(2,1)S(1)} %pad_maximum_fusion.1), channel_id=1, source_target_pairs={{0,4},{1,3},{4,8},{5,1},{8,12},{9,5},{12,14},{13,9},{14,10},{15,13... | collective-permute-start | bytes 786440 | tf_op jit(solution)/shard_map/ppermute | solution.py:333
  40.0 1.4 %collective-permute-done.2.refs_3_ = bf16[32,4096]{1,0:T(8,128)(2,1)S(1)} collective-permute-done((bf16[32,4096]{1,0:T(8,128)(2,1)S(1)}, bf16[32,4096]{1,0:T(8,128)(2,1)S(1)}, u32[]{:S(2)}, u32[]{:S(2)}) %collective-permute-start.2) | collective-permute-done | bytes 262176 | tf_op jit(solution)/shard_map/ppermute | solution.py:333
  41.4 1.3 %collective-permute-start.3 = (bf16[32,4096]{1,0:T(8,128)(2,1)S(1)}, bf16[32,4096]{1,0:T(8,128)(2,1)S(1)}, u32[]{:S(2)}, u32[]{:S(2)}) collective-permute-start(bf16[32,4096]{1,0:T(8,128)(2,1)S(1)} %collective-permute-done.2.refs_3_), channel_id=1, source_target_pairs={{0,4},{1,3},{4,8},{5,1},{8,12},{9,5},{12,14},{13,9},{14,10},{15,13... | collective-permute-start | bytes 786440 | tf_op jit(solution)/shard_map/ppermute | solution.py:333
  42.8 1.9 %collective-permute-done.7.refs_6_ = bf16[32,4096]{1,0:T(8,128)(2,1)S(1)} collective-permute-done((bf16[32,4096]{1,0:T(8,128)(2,1)S(1)}, bf16[32,4096]{1,0:T(8,128)(2,1)S(1)}, u32[]{:S(2)}, u32[]{:S(2)}) %collective-permute-start.7) | collective-permute-done | bytes 262176 | tf_op jit(solution)/shard_map/ppermute | solution.py:333
  44.7 1.7 %collective-permute-start.8 = (bf16[32,4096]{1,0:T(8,128)(2,1)S(1)}, bf16[32,4096]{1,0:T(8,128)(2,1)S(1)}, u32[]{:S(2)}, u32[]{:S(2)}) collective-permute-start(bf16[32,4096]{1,0:T(8,128)(2,1)S(1)} %collective-permute-done.7.refs_6_), channel_id=1, source_target_pairs={{0,4},{1,3},{4,8},{5,1},{8,12},{9,5},{12,14},{13,9},{14,10},{15,13... | collective-permute-start | bytes 786440 | tf_op jit(solution)/shard_map/ppermute | solution.py:333
  46.4 1.4 %collective-permute-done.3.refs_5_ = bf16[32,4096]{1,0:T(8,128)(2,1)S(1)} collective-permute-done((bf16[32,4096]{1,0:T(8,128)(2,1)S(1)}, bf16[32,4096]{1,0:T(8,128)(2,1)S(1)}, u32[]{:S(2)}, u32[]{:S(2)}) %collective-permute-start.3) | collective-permute-done | bytes 262176 | tf_op jit(solution)/shard_map/ppermute | solution.py:333
  47.8 1.4 %collective-permute-start.4 = (bf16[32,4096]{1,0:T(8,128)(2,1)S(1)}, bf16[32,4096]{1,0:T(8,128)(2,1)S(1)}, u32[]{:S(2)}, u32[]{:S(2)}) collective-permute-start(bf16[32,4096]{1,0:T(8,128)(2,1)S(1)} %collective-permute-done.3.refs_5_), channel_id=1, source_target_pairs={{0,4},{1,3},{4,8},{5,1},{8,12},{9,5},{12,14},{13,9},{14,10},{15,13... | collective-permute-start | bytes 786440 | tf_op jit(solution)/shard_map/ppermute | solution.py:333
  49.2 1.9 %collective-permute-done.8.refs_1_ = bf16[32,4096]{1,0:T(8,128)(2,1)S(1)} collective-permute-done((bf16[32,4096]{1,0:T(8,128)(2,1)S(1)}, bf16[32,4096]{1,0:T(8,128)(2,1)S(1)}, u32[]{:S(2)}, u32[]{:S(2)}) %collective-permute-start.8) | collective-permute-done | bytes 262176 | tf_op jit(solution)/shard_map/ppermute | solution.py:333
  51.1 1.7 %collective-permute-start.9 = (bf16[32,4096]{1,0:T(8,128)(2,1)S(1)}, bf16[32,4096]{1,0:T(8,128)(2,1)S(1)}, u32[]{:S(2)}, u32[]{:S(2)}) collective-permute-start(bf16[32,4096]{1,0:T(8,128)(2,1)S(1)} %collective-permute-done.8.refs_1_), channel_id=1, source_target_pairs={{0,4},{1,3},{4,8},{5,1},{8,12},{9,5},{12,14},{13,9},{14,10},{15,13... | collective-permute-start | bytes 786440 | tf_op jit(solution)/shard_map/ppermute | solution.py:333
  52.8 1.5 %shard_map.76 = (bf16[160,256]{1,0:T(8,128)(2,1)S(1)}, bf16[160,256]{1,0:T(8,128)(2,1)S(1)}) custom-call(bf16[16,4096]{1,0:T(8,128)(2,1)S(1)} %shard_map.74.refs_0_, bf16[16,4096]{1,0:T(8,128)(2,1)S(1)} %shard_map.75.refs_1_, bf16[16,4096]{1,0:T(8,128)(2,1)S(1)} %collective-permute-done.refs_2_, bf16[32,4096]{1,0:T(8,128)(2,1)S(1)} %collective-permute-done.2.refs_3_, ...), custom_call_target="tpu_custom_call" | custom-call | flops 6000000000 | bytes 1048576 | tf_op jit(solution)/shard_map/pallas_call | solution.py:244
  54.4 1.3 %collective-permute-done.11.refs_1_ = bf16[160,256]{1,0:T(8,128)(2,1)S(1)} collective-permute-done((bf16[160,256]{1,0:T(8,128)(2,1)S(1)}, bf16[160,256]{1,0:T(8,128)(2,1)S(1)}, u32[]{:S(2)}, u32[]{:S(2)}) %collective-permute-start.11) | collective-permute-done | bytes 81952 | tf_op jit(solution)/shard_map/ppermute | solution.py:359
  55.7 0.8 %shard_map.77.args_2_ = bf16[12,32,256]{2,1,0:T(8,128)(2,1)} custom-call(bf16[160,256]{1,0:T(8,128)(2,1)S(1)} %get-tuple-element.21.refs_0_, bf16[160,256]{1,0:T(8,128)(2,1)S(1)} %collective-permute-done.11.refs_1_), custom_call_target="tpu_custom_call" | custom-call | flops 1 | bytes 1 | tf_op jit(solution)/shard_map/pallas_call | solution.py:296
  56.5 1.0 %collective-permute-done.9.refs_2_ = bf16[32,4096]{1,0:T(8,128)(2,1)S(1)} collective-permute-done((bf16[32,4096]{1,0:T(8,128)(2,1)S(1)}, bf16[32,4096]{1,0:T(8,128)(2,1)S(1)}, u32[]{:S(2)}, u32[]{:S(2)}) %collective-permute-start.9) | collective-permute-done | bytes 262176 | tf_op jit(solution)/shard_map/ppermute | solution.py:333
  57.5 0.8 %shard_map.79 = bf16[96,256]{1,0:T(8,128)(2,1)S(1)} custom-call(bf16[32,4096]{1,0:T(8,128)(2,1)S(1)} %collective-permute-done.4.refs_0_, bf16[32,4096]{1,0:T(8,128)(2,1)S(1)} %collective-permute-done.8.refs_1_, bf16[32,4096]{1,0:T(8,128)(2,1)S(1)} %collective-permute-done.9.refs_2_, bf16[256,4096]{1,0:T(8,128)(2,1)S(1)} %collective-permute-done.10.refs_8_.refs_3_), custom_call_target="tpu_custom_call" | custom-call | flops 6000000000 | bytes 1048576 | tf_op jit(solution)/shard_map/pallas_call | solution.py:244
  58.3 0.8 %shard_map.78.args_0_ = bf16[96,256]{1,0:T(8,128)(2,1)S(1)} custom-call(bf16[32,4096]{1,0:T(8,128)(2,1)S(1)} %collective-permute-done.4.refs_0_, bf16[32,4096]{1,0:T(8,128)(2,1)S(1)} %collective-permute-done.8.refs_1_, bf16[32,4096]{1,0:T(8,128)(2,1)S(1)} %collective-permute-done.9.refs_2_, bf16[256,4096]{1,0:T(8,128)(2,1)S(1)} %copy-done), custom_call_target="tpu_custom_call" | custom-call | flops 6000000000 | bytes 1048576 | tf_op jit(solution)/shard_map/pallas_call | solution.py:244
  59.1 0.4 collective-permute-done.12.args_1_
  59.5 0.7 %shard_map.80 = bf16[12,32,256]{2,1,0:T(8,128)(2,1)} custom-call(bf16[96,256]{1,0:T(8,128)(2,1)S(1)} %shard_map.78.args_0_, bf16[96,256]{1,0:T(8,128)(2,1)S(1)} %collective-permute-done.12.args_1_, bf16[12,32,256]{2,1,0:T(8,128)(2,1)} %shard_map.77.args_2_), custom_call_target="tpu_custom_call", output_to_operand_aliasing={{}: (2, {})} | custom-call | flops 1 | bytes 1 | tf_op jit(solution)/shard_map/pallas_call | solution.py:296
  (15 shorter events, 1.1 us)
Async XLA Ops:
  27.6 5.4 %copy-start = (bf16[256,4096]{1,0:T(8,128)(2,1)S(1)}, bf16[256,4096]{1,0:T(8,128)(2,1)}, u32[]{:S(2)}) copy-start(bf16[256,4096]{1,0:T(8,128)(2,1)} %refs_3_.1) | copy-start | bytes 6291460
  27.6 5.4 %collective-permute-start = (bf16[16,4096]{1,0:T(8,128)(2,1)S(1)}, bf16[16,4096]{1,0:T(8,128)(2,1)S(1)}, u32[]{:S(2)}, u32[]{:S(2)}) collective-permute-start(bf16[16,4096]{1,0:T(8,128)(2,1)S(1)} %shard_map.74.refs_0_), channel_id=1, source_target_pairs={{0,4},{1,3},{4,8},{5,1},{8,12},{9,5},{12,14},{13,9},{14,10},{15,13... | collective-permute-start | bytes 393224 | tf_op jit(solution)/shard_map/ppermute | solution.py:333
  27.9 5.0 %collective-permute-start.1 = (bf16[16,4096]{1,0:T(8,128)(2,1)S(1)}, bf16[16,4096]{1,0:T(8,128)(2,1)S(1)}, u32[]{:S(2)}, u32[]{:S(2)}) collective-permute-start(bf16[16,4096]{1,0:T(8,128)(2,1)S(1)} %shard_map.74.refs_0_), channel_id=1, source_target_pairs={{0,1},{1,0},{2,3},{3,2},{4,5},{5,4},{6,7},{7,6},{8,9},{9,8},{10,11... | collective-permute-start | bytes 393224 | tf_op jit(solution)/shard_map/ppermute | solution.py:337
  32.9 19.8 %collective-permute-start.10 = (bf16[256,4096]{1,0:T(8,128)(2,1)S(1)}, bf16[256,4096]{1,0:T(8,128)(2,1)S(1)}, u32[]{:S(2)}, u32[]{:S(2)}) collective-permute-start(bf16[256,4096]{1,0:T(8,128)(2,1)S(1)} %copy-done), channel_id=1, source_target_pairs={{0,1},{1,0},{2,3},{3,2},{4,5},{5,4},{6,7},{7,6},{8,9},{9,8},{10,11... | collective-permute-start | bytes 6291464 | tf_op jit(solution)/shard_map/ppermute | solution.py:345
  33.3 5.0 %collective-permute-start.5 = (bf16[16,4096]{1,0:T(8,128)(2,1)S(1)}, bf16[16,4096]{1,0:T(8,128)(2,1)S(1)}, u32[]{:S(2)}, u32[]{:S(2)}) collective-permute-start(bf16[16,4096]{1,0:T(8,128)(2,1)S(1)} %shard_map.75.refs_1_), channel_id=1, source_target_pairs={{0,4},{1,3},{4,8},{5,1},{8,12},{9,5},{12,14},{13,9},{14,10},{15,13... | collective-permute-start | bytes 393224 | tf_op jit(solution)/shard_map/ppermute | solution.py:333
  35.0 3.3 %collective-permute-start.6 = (bf16[16,4096]{1,0:T(8,128)(2,1)S(1)}, bf16[16,4096]{1,0:T(8,128)(2,1)S(1)}, u32[]{:S(2)}, u32[]{:S(2)}) collective-permute-start(bf16[16,4096]{1,0:T(8,128)(2,1)S(1)} %shard_map.75.refs_1_), channel_id=1, source_target_pairs={{0,1},{1,0},{2,3},{3,2},{4,5},{5,4},{6,7},{7,6},{8,9},{9,8},{10,11... | collective-permute-start | bytes 393224 | tf_op jit(solution)/shard_map/ppermute | solution.py:344
  35.0 6.4 %collective-permute-start.2 = (bf16[32,4096]{1,0:T(8,128)(2,1)S(1)}, bf16[32,4096]{1,0:T(8,128)(2,1)S(1)}, u32[]{:S(2)}, u32[]{:S(2)}) collective-permute-start(bf16[32,4096]{1,0:T(8,128)(2,1)S(1)} %pad_maximum_fusion), channel_id=1, source_target_pairs={{0,4},{1,3},{4,8},{5,1},{8,12},{9,5},{12,14},{13,9},{14,10},{15,13... | collective-permute-start | bytes 786440 | tf_op jit(solution)/shard_map/ppermute | solution.py:333
  38.3 6.4 %collective-permute-start.7 = (bf16[32,4096]{1,0:T(8,128)(2,1)S(1)}, bf16[32,4096]{1,0:T(8,128)(2,1)S(1)}, u32[]{:S(2)}, u32[]{:S(2)}) collective-permute-start(bf16[32,4096]{1,0:T(8,128)(2,1)S(1)} %pad_maximum_fusion.1), channel_id=1, source_target_pairs={{0,4},{1,3},{4,8},{5,1},{8,12},{9,5},{12,14},{13,9},{14,10},{15,13... | collective-permute-start | bytes 786440 | tf_op jit(solution)/shard_map/ppermute | solution.py:333
  41.4 6.4 %collective-permute-start.3 = (bf16[32,4096]{1,0:T(8,128)(2,1)S(1)}, bf16[32,4096]{1,0:T(8,128)(2,1)S(1)}, u32[]{:S(2)}, u32[]{:S(2)}) collective-permute-start(bf16[32,4096]{1,0:T(8,128)(2,1)S(1)} %collective-permute-done.2.refs_3_), channel_id=1, source_target_pairs={{0,4},{1,3},{4,8},{5,1},{8,12},{9,5},{12,14},{13,9},{14,10},{15,13... | collective-permute-start | bytes 786440 | tf_op jit(solution)/shard_map/ppermute | solution.py:333
  44.7 6.4 %collective-permute-start.8 = (bf16[32,4096]{1,0:T(8,128)(2,1)S(1)}, bf16[32,4096]{1,0:T(8,128)(2,1)S(1)}, u32[]{:S(2)}, u32[]{:S(2)}) collective-permute-start(bf16[32,4096]{1,0:T(8,128)(2,1)S(1)} %collective-permute-done.7.refs_6_), channel_id=1, source_target_pairs={{0,4},{1,3},{4,8},{5,1},{8,12},{9,5},{12,14},{13,9},{14,10},{15,13... | collective-permute-start | bytes 786440 | tf_op jit(solution)/shard_map/ppermute | solution.py:333
  47.8 9.6 %collective-permute-start.4 = (bf16[32,4096]{1,0:T(8,128)(2,1)S(1)}, bf16[32,4096]{1,0:T(8,128)(2,1)S(1)}, u32[]{:S(2)}, u32[]{:S(2)}) collective-permute-start(bf16[32,4096]{1,0:T(8,128)(2,1)S(1)} %collective-permute-done.3.refs_5_), channel_id=1, source_target_pairs={{0,4},{1,3},{4,8},{5,1},{8,12},{9,5},{12,14},{13,9},{14,10},{15,13... | collective-permute-start | bytes 786440 | tf_op jit(solution)/shard_map/ppermute | solution.py:333
  51.1 6.4 %collective-permute-start.9 = (bf16[32,4096]{1,0:T(8,128)(2,1)S(1)}, bf16[32,4096]{1,0:T(8,128)(2,1)S(1)}, u32[]{:S(2)}, u32[]{:S(2)}) collective-permute-start(bf16[32,4096]{1,0:T(8,128)(2,1)S(1)} %collective-permute-done.8.refs_1_), channel_id=1, source_target_pairs={{0,4},{1,3},{4,8},{5,1},{8,12},{9,5},{12,14},{13,9},{14,10},{15,13... | collective-permute-start | bytes 786440 | tf_op jit(solution)/shard_map/ppermute | solution.py:333
  54.3 1.3 %collective-permute-start.11 = (bf16[160,256]{1,0:T(8,128)(2,1)S(1)}, bf16[160,256]{1,0:T(8,128)(2,1)S(1)}, u32[]{:S(2)}, u32[]{:S(2)}) collective-permute-start(bf16[160,256]{1,0:T(8,128)(2,1)S(1)} %get-tuple-element.22), channel_id=1, source_target_pairs={{0,1},{1,0},{2,3},{3,2},{4,5},{5,4},{6,7},{7,6},{8,9},{9,8},{10,11... | collective-permute-start | bytes 245768 | tf_op jit(solution)/shard_map/ppermute | solution.py:359
  58.2 1.3 %collective-permute-start.12 = (bf16[96,256]{1,0:T(8,128)(2,1)S(1)}, bf16[96,256]{1,0:T(8,128)(2,1)S(1)}, u32[]{:S(2)}, u32[]{:S(2)}) collective-permute-start(bf16[96,256]{1,0:T(8,128)(2,1)S(1)} %shard_map.79), channel_id=1, source_target_pairs={{0,1},{1,0},{2,3},{3,2},{4,5},{5,4},{6,7},{7,6},{8,9},{9,8},{10,11... | collective-permute-start | bytes 147464 | tf_op jit(solution)/shard_map/ppermute | solution.py:363
